TPU v7x, 32 devices: a whole 2x2x4 slice. The times are simulated.
32 devices in a mesh: videos: 2 (over x), rows: 16 (over z, y, core).
Axes of the slice: x: 2, y: 2, z: 4, core: 2. Of those that a mesh axis runs over, the one named last changes fastest.
Arguments:
- latents: bfloat16 [4, 32, 64, 384], P('videos', 'rows'), parts along dimension 0, may hold values from -6 to 6
- conv_cache: bfloat16 [4, 32, 64, 384], P('videos', 'rows'), parts along dimension 0, may hold values from -4 to 4
- norm_gain: float32 [384], replicated, may hold values from 0.1 to 1.9
- conv_weight: bfloat16 [3, 3, 3, 384, 384], replicated, may hold values from -0.0625 to 0.0625
- attn_gain: float32 [384], replicated, may hold values from 0.1 to 1.9
- query_weight: bfloat16 [384, 384], replicated, may hold values from -3 to 3
- key_weight: bfloat16 [384, 384], replicated, may hold values from -3 to 3
- value_weight: bfloat16 [384, 384], replicated, may hold values from -0.3125 to 0.3125
- out_weight: bfloat16 [384, 384], replicated, may hold values from -0.3125 to 0.3125
- up_weight: bfloat16 [3, 3, 384, 192], replicated, may hold values from -0.109375 to 0.109375
Outputs:
- decoded: bfloat16 [4, 64, 128, 192], P('videos', 'rows'), parts along dimension 0
- next_cache: bfloat16 [4, 32, 64, 384], P('videos', 'rows'), parts along dimension 0
There are 2 independent parts, one for each index of `videos`. A program takes and returns all parts, laid end to end along the dimension named above; an argument that names none is the same for every part. Nothing has to cross between parts.
All inputs are finite; a program needn't handle non-finite values.
Results may differ from a plain program's by a relative error of at most 0.0058.
Values may be sent and summed in bfloat16 or wider, within the bound.
No kernel may reach another device: no remote copies, remote signals or barrier semaphores. Data moves between devices by JAX's collectives and lax.ppermute only.
A program may use at most 128 MiB of HBM per device.

v0:
```python
import functools

import jax
import jax.numpy as jnp
from jax import lax
from jax.experimental import pallas as pl
from jax.experimental.pallas import tpu as pltpu
from jax.sharding import PartitionSpec as P

BF16 = jnp.bfloat16
F32 = jnp.float32
EPS = 1e-06
MIB = 1024 * 1024
EXTRA = 16


def normalize(values, gain):
    return values * lax.rsqrt(jnp.mean(values * values, axis=-1, keepdims=True) + EPS) * gain


def activate(values, gain):
    normed = normalize(values.astype(F32), gain)
    return (normed / (1.0 + jnp.exp(-normed))).astype(BF16)


def vmem():
    return pl.BlockSpec(memory_space=pltpu.VMEM)


def params(mib):
    return pltpu.CompilerParams(vmem_limit_bytes=mib * MIB)


def cost(flops, size, exps=0):
    return pl.CostEstimate(flops=flops, bytes_accessed=size, transcendentals=exps)


def edges_kernel(latents_ref, cache_ref, edge_ref, both_ref, sems):
    core = lax.axis_index("rows") % 2
    row = core * (latents_ref.shape[1] - 1)
    copies = [
        pltpu.make_async_copy(cache_ref.at[:, row], edge_ref.at[pl.ds(0, 2)], sems.at[0]),
        pltpu.make_async_copy(latents_ref.at[:, row], edge_ref.at[pl.ds(2, 2)], sems.at[1]),
        pltpu.make_async_copy(cache_ref.at[1], both_ref.at[core], sems.at[2]),
        pltpu.make_async_copy(latents_ref.at[0], both_ref.at[1 + core], sems.at[3]),
    ]
    for copy in copies:
        copy.start()

    @pl.when(core == 0)
    def _():
        last = pltpu.make_async_copy(latents_ref.at[1], both_ref.at[2], sems.at[4])
        last.start()
        last.wait()

    @pl.when(core == 1)
    def _():
        last = pltpu.make_async_copy(cache_ref.at[0], both_ref.at[0], sems.at[4])
        last.start()
        last.wait()

    for copy in copies:
        copy.wait()


def start_all(pairs, sems, first=0):
    copies = [
        pltpu.make_async_copy(source, target, sems.at[first + i])
        for i, (source, target) in enumerate(pairs)
    ]
    for copy in copies:
        copy.start()
    return copies


def wait_all(copies):
    for copy in copies:
        copy.wait()


def prepare_kernel(
    latents_ref,
    cache_ref,
    weight_ref,
    gain_ref,
    act_ref,
    own_ref,
    staged_ref,
    latents,
    cache,
    gain,
    act,
    sems,
):
    channels = latents_ref.shape[-1]
    core = lax.axis_index("rows") % 2
    loads = start_all([(latents_ref, latents), (cache_ref, cache), (gain_ref, gain)], sems)
    stages = start_all(
        [
            (
                weight_ref.at[time, :, col],
                staged_ref.at[time, :, :, pl.ds(col * channels, channels)],
            )
            for time in range(3)
            for col in range(3)
        ],
        sems,
        4,
    )
    wait_all(loads)
    act[...] = activate(latents[...], gain[...].reshape(1, channels))
    store = start_all([(act, act_ref)], sems, 3)
    own_ref[0] = cache[core]
    own_ref[1] = jnp.where(core == 0, cache[1], latents[0])
    own_ref[2] = latents[core]
    wait_all(store + stages)


def conv_kernel(
    width,
    own_ref,
    swap_ref,
    edge_ref,
    far_ref,
    norm_gain_ref,
    attn_gain_ref,
    weights,
    sent_ref,
    front_ref,
    back_ref,
    resid_ref,
    raw,
    second,
    third,
    total,
):
    channels = own_ref.shape[-1]
    core = lax.axis_index("rows") % 2
    own = 2 * width
    span = 4 * width
    gain = norm_gain_ref[...].reshape(1, channels)

    def put(index, values):
        rows = pl.ds(pl.multiple_of(index * width, width), values.shape[1])
        raw[:, rows, :] = values

    put(1 + 2 * core, own_ref[...])
    put(3 - 2 * core, swap_ref[...])
    put(5 * core, edge_ref[pl.ds(core, 3)])
    put(5 * (1 - core), far_ref[pl.ds(core, 3)])

    def taps(ref, time):
        lhs = jnp.concatenate([ref[row * width : row * width + span] for row in range(3)], axis=1)
        rhs = weights[time].reshape(3 * channels, 3 * channels)
        return jnp.dot(lhs, rhs, preferred_element_type=F32)

    total[...] = taps(raw.at[0], 0)
    second[...] = jnp.where(core == 1, activate(raw[1], gain), raw[1])
    third[...] = activate(raw[2], gain)
    total[...] += taps(second, 1)
    total[...] += taps(third, 2)

    column = lax.broadcasted_iota(jnp.int32, (span, 1), 0) % width
    left = pltpu.roll(total[:, :channels], 1, axis=0)
    right = pltpu.roll(total[:, 2 * channels :], span - 1, axis=0)
    conv_out = total[:, channels : 2 * channels]
    conv_out = conv_out + jnp.where(column == 0, 0.0, left)
    conv_out = conv_out + jnp.where(column == width - 1, 0.0, right)
    resid = raw[2, width : width + span].astype(F32) + conv_out
    resid_ref[...] = resid
    size = jnp.mean(resid * resid, axis=-1, keepdims=True) + EPS
    normed = resid * lax.rsqrt(size) * attn_gain_ref[...].reshape(1, channels)
    edges = jnp.sqrt(jnp.concatenate([size[:width], size[span - width :]], axis=0))
    across = jnp.transpose(jnp.broadcast_to(edges, (2 * width, 128)))[:EXTRA]
    high = across.astype(BF16).astype(F32)
    line = lax.broadcasted_iota(jnp.int32, (EXTRA, 1), 0)
    extra = jnp.where(line == 0, high, jnp.where(line == 1, across - high, 0.0)).astype(BF16)
    half = span // 2
    for ref, low, count in ((sent_ref, 0, span), (front_ref, 0, half), (back_ref, half, half)):
        ref[:count] = normed[low : low + count].astype(BF16)
        ref[count:] = jnp.zeros((EXTRA, channels), BF16)
        ref[count:, : 2 * width] = extra


def nt_dot(a, b):
    return lax.dot_general(a, b, (((1,), (1,)), ((), ())), preferred_element_type=F32)


def whole(parts):
    rows = [part[: part.shape[0] - EXTRA] for part in parts]
    return rows[0] if len(rows) == 1 else jnp.concatenate(rows, axis=0)


def grouped(refs, counts):
    blocks, first = [], 0
    for count in counts:
        blocks.append(refs[first : first + count])
        first += count
    return blocks


def fold(values, combine, total):
    for lane in range(0, values.shape[1], 128):
        piece = values[:, lane : lane + 128]
        total = piece if total is None else combine(total, piece)
    return total


def attend(queries, keys, scores, start, peak, sums, added):
    height = queries.shape[0]
    top = None
    for i, key in enumerate(keys):
        part = nt_dot(queries, key)
        scores[i, start : start + height] = part
        top = fold(part, jnp.maximum, top)
    top = jnp.max(top, axis=-1, keepdims=True)
    if peak is not None:
        top = jnp.maximum(top, peak)
        shrink = jnp.exp2(peak - top)
        sums = sums * shrink
        added = added * shrink
    for i, key in enumerate(keys):
        weights = jnp.exp2(scores[i, start : start + height] - top)
        sums = fold(weights, jnp.add, sums)
        part = jnp.dot(weights.astype(BF16), key, preferred_element_type=F32)
        added = part if added is None else added + part
    return top, sums, added


def fuse_kernel(scale, query_ref, key_ref, value_ref, out_ref, score_ref, mix_ref):
    score_ref[...] = (nt_dot(query_ref[...], key_ref[...]) * scale).astype(BF16)
    mix_ref[...] = jnp.dot(
        value_ref[...], out_ref[...], preferred_element_type=F32
    ).astype(BF16)


def lead(rows, score_weight):
    return jnp.dot(rows, score_weight[...], preferred_element_type=F32).astype(BF16)


def early_kernel(counts, score_ref, *refs):
    blocks = grouped(refs, counts)
    own_query_ref, peak_ref, sums_ref, added_ref, scores = refs[-5:]
    keys = [whole(parts) for parts in blocks]
    queries = lead(keys[0], score_ref)
    own_query_ref[...] = queries
    peak, sums, added = attend(queries, keys, scores, 0, None, None, None)
    peak_ref[...] = jnp.broadcast_to(peak, peak_ref.shape)
    sums_ref[...] = sums
    added_ref[...] = added


def late_kernel(
    width,
    sources,
    counts,
    early,
    own_query_ref,
    peak_ref,
    sums_ref,
    added_ref,
    resid_ref,
    gain_ref,
    score_ref,
    mix_weight_ref,
    *refs,
):
    blocks = grouped(refs, counts)
    mid_ref, swap_ref, scores, mid, halo, sizes = refs[sum(counts) :]
    place = lax.axis_index("rows")
    core = place % 2
    chip = place // 2
    own, channels = own_query_ref.shape
    devices = len(sources[0])

    for block, origin in zip(blocks, sources):
        for step, part, low in ((-1, block[-1], 0), (1, block[0], width)):
            rows = part.shape[0] - EXTRA
            first = rows - width if step < 0 else 0
            takers = [d for d in range(devices) if origin[d] == d // 2 + step]
            if not takers:
                continue
            wanted = place == takers[0]
            for d in takers[1:]:
                wanted = jnp.logical_or(wanted, place == d)

            @pl.when(wanted)
            def _(part=part, rows=rows, first=first, low=low):
                halo[low : low + width] = part[first : first + width, :]
                sizes[low // width] = part[rows : rows + EXTRA, : 2 * width]

    no_above = chip == 0
    no_below = chip == devices // 2 - 1

    @pl.when(no_above)
    def _():
        halo[:width] = jnp.zeros((width, channels), BF16)
        sizes[0] = jnp.zeros((EXTRA, 2 * width), BF16)

    @pl.when(no_below)
    def _():
        halo[width:] = jnp.zeros((width, channels), BF16)
        sizes[1] = jnp.zeros((EXTRA, 2 * width), BF16)

    def column(index):
        parts = sizes[index].astype(F32)
        line = parts[0:1] + parts[1:2]
        return jnp.transpose(jnp.broadcast_to(line, (128, 2 * width)))[:, :1]

    edge_rows = halo[...]
    edge_size = jnp.concatenate([column(0)[width:], column(1)[:width]], axis=0)
    edge_resid = edge_rows.astype(F32) * edge_size / gain_ref[...].reshape(1, channels)
    edge_query = lead(edge_rows, score_ref)
    keys = [whole(parts) for parts in blocks]
    _, edge_sums, edge_added = attend(edge_query, keys, scores, own, None, None, None)
    _, own_sums, own_added = attend(
        own_query_ref[...],
        keys[early:],
        scores,
        0,
        peak_ref[:, :1],
        sums_ref[...],
        added_ref[...],
    )

    def finish(added, sums):
        return (added / jnp.sum(sums, axis=-1, keepdims=True)).astype(BF16)

    mixed = jnp.concatenate([finish(own_added, own_sums), finish(edge_added, edge_sums)], axis=0)
    projected = jnp.dot(mixed, mix_weight_ref[...], preferred_element_type=F32)
    inner = own + width
    mid[width:inner] = (resid_ref[...] + projected[:own]).astype(BF16)
    edges = edge_resid + projected[own:]
    mid[:width] = jnp.where(no_above, 0.0, edges[:width]).astype(BF16)
    mid[inner:] = jnp.where(no_below, 0.0, edges[width:]).astype(BF16)
    mid_ref[...] = mid[pl.ds(pl.multiple_of(2 * core * width, width), 4 * width), :]
    swap_ref[...] = mid[pl.ds(pl.multiple_of(2 * (1 - core) * width, width), 4 * width), :]


def up_kernel(width, mid_ref, swap_ref, weight_ref, out_ref, fine, total, results, sems):
    core = lax.axis_index("rows") % 2
    channels = mid_ref.shape[1]
    outputs = weight_ref.shape[2]
    wide = 2 * width
    lane = lax.broadcasted_iota(jnp.int32, (1, wide), 1)
    lhs = weight_ref[...].reshape(9 * outputs, channels)
    stores = []
    for slot, ref, frame in ((0, mid_ref, core), (1, swap_ref, 1 - core)):
        values = ref[...].astype(F32)
        pieces = []
        for i in range(channels // 128):
            piece = values[:, 128 * i : 128 * (i + 1)]
            fine[slot, i, pl.ds(0, 4 * width, stride=2), :] = piece
            fine[slot, i, pl.ds(1, 4 * width, stride=2), :] = piece
            pieces.append(fine[slot, i].astype(BF16))
        total[slot] = nt_dot(lhs, jnp.concatenate(pieces, axis=1))
        for row in range(4):
            low = row // 2 + 1
            picks = (low - 1, low, low) if row % 2 == 0 else (low, low, low + 1)
            taps = []
            for col in range(3):
                tap = None
                for j, pick in enumerate(picks):
                    piece = total[
                        slot,
                        (3 * j + col) * outputs : (3 * j + col + 1) * outputs,
                        pick * wide : (pick + 1) * wide,
                    ]
                    tap = piece if tap is None else tap + piece
                taps.append(tap)
            result = taps[1]
            result = result + jnp.where(lane == 0, 0.0, pltpu.roll(taps[0], 1, axis=1))
            result = result + jnp.where(
                lane == wide - 1, 0.0, pltpu.roll(taps[2], wide - 1, axis=1)
            )
            results[slot, row] = result.astype(BF16)
        stores = stores + start_all([(results.at[slot], out_ref.at[frame])], sems, slot)
    wait_all(stores)


def gather_blocks(block, halves, count):
    chips = count // 2
    depth = 2 if chips % 2 == 0 else 1
    length = chips // depth

    ring = [0] + list(range(1, length, 2)) + list(range(2, length, 2))[::-1]
    follow = {a: ring[(i + 1) % length] for i, a in enumerate(ring)}
    forth = {a * depth + b: follow[a] * depth + b for a in range(length) for b in range(depth)}
    return_ = {target: source for source, target in forth.items()}
    onward = (forth, return_)
    backward = (return_, forth)
    across = ({k: k ^ 1 for k in range(chips)},) * 2

    def send(parts, targets):
        pairs = [(2 * k + c, 2 * targets[c][k] + c) for k in range(chips) for c in range(2)]
        return [lax.ppermute(part, "rows", pairs) for part in parts]

    def moved(origin, targets):
        return tuple({targets[c][k]: origin[c][k] for k in range(chips)} for c in range(2))

    def tie(*places):
        fixed = lax.optimization_barrier(tuple(where[i] for where, i in places))
        for (where, i), value in zip(places, fixed):
            where[i] = value

    here = ({k: k for k in range(chips)},) * 2
    early, late = [([block], here)], []
    own_again = [block]
    crossed = last = None
    if depth == 2:
        crossed = send([block], across)
    steps = length - 2
    parts, origin = list(halves), here
    for step in range(1, steps + 1):
        parts, origin = send(parts, onward), moved(origin, onward)
        for h in range(2):
            places = [(parts, h)]
            if last:
                places.append((last, h))
            if (step, h) == (1, 1) and depth == 2:
                places.append((crossed, 0))
            tie(*places)
        early.append((parts, origin))
        if depth == 2:
            last = send(parts, across)
            (late if step == steps else early).append((last, moved(origin, across)))
    if length > 1:
        if steps > 0:
            tie((own_again, 0), (parts, 0))
        late.append((send(own_again, backward), moved(here, backward)))
    if depth == 2:
        (early if length > 1 else late).append((crossed, moved(here, across)))
        if length > 1:
            again = list(crossed)
            if steps > 0:
                tie((again, 0), (parts, 0))
            late.append((send(again, backward), moved(moved(here, across), backward)))
    return early, late


def shards(
    latents,
    conv_cache,
    norm_gain,
    conv_weight,
    attn_gain,
    query_weight,
    key_weight,
    value_weight,
    out_weight,
    up_weight,
):
    frames, rows_here, width, channels = latents.shape
    outputs = up_weight.shape[3]
    count = lax.axis_size("rows")
    span = 2 * rows_here * width
    own = rows_here * width
    edge = jax.ShapeDtypeStruct((width, channels), BF16)
    anywhere = pl.BlockSpec(memory_space=pl.ANY)
    hbm = pl.BlockSpec(memory_space=pltpu.HBM)

    chips = count // 2
    swap = [(2 * k + c, 2 * k + 1 - c) for k in range(chips) for c in range(2)]
    neighbour = [(2 * k + 1, 2 * k + 2) for k in range(chips - 1)]
    neighbour = neighbour + [(target, source) for source, target in neighbour]

    latents_in = pltpu.with_memory_space_constraint(latents, pltpu.HBM)
    cache_in = pltpu.with_memory_space_constraint(conv_cache, pltpu.HBM)
    edge_rows, both = pl.pallas_call(
        edges_kernel,
        out_shape=(
            jax.ShapeDtypeStruct((2 * frames, width, channels), BF16),
            jax.ShapeDtypeStruct((3, rows_here, width, channels), BF16),
        ),
        in_specs=[hbm] * 2,
        out_specs=(anywhere,) * 2,
        scratch_shapes=[pltpu.SemaphoreType.DMA((5,))],
        cost_estimate=cost(0, 20 * width * channels),
        compiler_params=params(4),
    )(latents_in, cache_in)
    edge_rows = lax.ppermute(edge_rows, "rows", neighbour)
    both = lax.ppermute(both, "rows", swap)
    act, own_rows, staged = pl.pallas_call(
        prepare_kernel,
        out_shape=(
            jax.ShapeDtypeStruct((frames, own, channels), BF16),
            jax.ShapeDtypeStruct((3, own, channels), BF16),
            jax.ShapeDtypeStruct((3, 3, channels, 3 * channels), BF16),
        ),
        in_specs=[hbm] * 4,
        out_specs=(anywhere, vmem(), anywhere),
        scratch_shapes=[
            pltpu.VMEM((frames, own, channels), BF16),
            pltpu.VMEM((frames, own, channels), BF16),
            pltpu.VMEM((channels,), F32),
            pltpu.VMEM((frames, own, channels), BF16),
            pltpu.SemaphoreType.DMA((13,)),
        ],
        cost_estimate=cost(10 * frames * own * channels, 2 * 27 * channels * channels),
        compiler_params=params(8),
    )(
        pltpu.with_memory_space_constraint(latents.reshape(frames, own, channels), pltpu.HBM),
        pltpu.with_memory_space_constraint(conv_cache.reshape(frames, own, channels), pltpu.HBM),
        pltpu.with_memory_space_constraint(conv_weight, pltpu.HBM),
        pltpu.with_memory_space_constraint(norm_gain, pltpu.HBM),
    )

    edge_rows, own_rows = lax.optimization_barrier((edge_rows, own_rows))
    far_rows = lax.ppermute(edge_rows, "rows", swap)
    block = jax.ShapeDtypeStruct((span + EXTRA, channels), BF16)
    half = jax.ShapeDtypeStruct((span // 2 + EXTRA, channels), BF16)
    sent, front, back, resid = pl.pallas_call(
        functools.partial(conv_kernel, width),
        out_shape=(block, half, half, jax.ShapeDtypeStruct((span, channels), F32)),
        in_specs=[vmem()] * 7,
        out_specs=(vmem(),) * 4,
        scratch_shapes=[
            pltpu.VMEM((3, 6 * width, channels), BF16),
            pltpu.VMEM((6 * width, channels), BF16),
            pltpu.VMEM((6 * width, channels), BF16),
            pltpu.VMEM((span, 3 * channels), F32),
        ],
        cost_estimate=cost(2 * 27 * span * channels * channels, 2 * 27 * channels * channels),
        compiler_params=params(20),
    )(
        own_rows,
        both.reshape(3, own, channels),
        edge_rows,
        far_rows,
        norm_gain,
        attn_gain,
        staged,
    )

    early, late = gather_blocks(sent, (front, back), count)
    blocks = early + late
    sources = [[origin[d % 2][d // 2] for d in range(count)] for _, origin in blocks]
    counts = [len(parts) for parts, _ in blocks]
    early_parts = [part for parts, _ in early for part in parts]
    all_parts = [part for parts, _ in blocks for part in parts]

    scale = channels ** (-0.5) * 1.4426950408889634
    square = jax.ShapeDtypeStruct((channels, channels), BF16)
    score_weight, mix_weight = pl.pallas_call(
        functools.partial(fuse_kernel, scale),
        out_shape=(square, square),
        in_specs=[vmem()] * 4,
        out_specs=(vmem(),) * 2,
        cost_estimate=cost(4 * channels**3, 12 * channels * channels),
        compiler_params=params(8),
    )(query_weight, key_weight, value_weight, out_weight)

    wide = span + 2 * width
    lanes = jax.ShapeDtypeStruct((span, 128), F32)
    own_query, peak, sums, added = pl.pallas_call(
        functools.partial(early_kernel, counts[: len(early)]),
        out_shape=(
            jax.ShapeDtypeStruct((span, channels), BF16),
            lanes,
            lanes,
            jax.ShapeDtypeStruct((span, channels), F32),
        ),
        in_specs=[vmem()] * (1 + len(early_parts)),
        out_specs=(vmem(),) * 4,
        scratch_shapes=[pltpu.VMEM((len(early), span, span), F32)],
        cost_estimate=cost(
            4 * span * span * len(early) * channels,
            2 * span * channels * len(early),
            span * span * len(early),
        ),
        compiler_params=params(24),
    )(score_weight, *early_parts)

    mid, swap_rows = pl.pallas_call(
        functools.partial(late_kernel, width, sources, counts, len(early)),
        out_shape=(jax.ShapeDtypeStruct((4 * width, channels), BF16),) * 2,
        in_specs=[vmem()] * (8 + len(all_parts)),
        out_specs=(vmem(),) * 2,
        scratch_shapes=[
            pltpu.VMEM((len(blocks), wide, span), F32),
            pltpu.VMEM((wide, channels), BF16),
            pltpu.VMEM((2 * width, channels), BF16),
            pltpu.VMEM((2, EXTRA, 2 * width), BF16),
        ],
        cost_estimate=cost(
            2 * wide * span * len(blocks) * channels,
            2 * span * channels * len(blocks),
            wide * span * len(blocks) // 2,
        ),
        compiler_params=params(28),
    )(
        own_query,
        peak,
        sums,
        added,
        resid,
        attn_gain,
        score_weight,
        mix_weight,
        *all_parts,
    )

    swap_rows = lax.ppermute(swap_rows, "rows", swap)

    fine_shape = (2 * rows_here, outputs, 2 * width)
    decoded = pl.pallas_call(
        functools.partial(up_kernel, width),
        out_shape=jax.ShapeDtypeStruct((frames, *fine_shape), BF16),
        in_specs=[vmem()] * 3,
        out_specs=anywhere,
        scratch_shapes=[
            pltpu.VMEM((2, channels // 128, 8 * width, 128), F32),
            pltpu.VMEM((2, 9 * outputs, 8 * width), F32),
            pltpu.VMEM((2, *fine_shape), BF16),
            pltpu.SemaphoreType.DMA((2,)),
        ],
        cost_estimate=cost(
            2 * 9 * outputs * channels * 16 * width, 2 * 9 * outputs * channels
        ),
        compiler_params=params(24),
    )(mid, swap_rows, jnp.transpose(up_weight, (0, 1, 3, 2)))
    decoded = jnp.transpose(decoded, (0, 1, 3, 2))
    return (decoded, act.reshape(frames, rows_here, width, channels))


def solution(mesh):
    return jax.shard_map(
        shards,
        mesh=mesh,
        in_specs=(
            P("videos", "rows", None, None),
            P("videos", "rows", None, None),
            P(),
            P(),
            P(),
            P(),
            P(),
            P(),
            P(),
            P(),
        ),
        out_specs=(P("videos", "rows", None, None), P("videos", "rows", None, None)),
        check_vma=False,
    )
```

profile of v0, /device:TPU:1, one launch (start us, length us, event | category | flops | bytes accessed | tf_op | source)
XLA Modules:
  0.0 48.2 jit_solution(6150962640944924924)
XLA Ops:
  0.7 1.1 %shard_map.114 = (bf16[4,64,384]{2,1,0:T(8,128)(2,1)S(1)}, bf16[3,2,64,384]{3,2,1,0:T(8,128)(2,1)S(1)}) custom-call(bf16[2,2,64,384]{3,2,1,0:T(8,128)(2,1)} %latents_ref.1, bf16[2,2,64,384]{3,2,1,0:T(8,128)(2,1)} %cache_ref.1), custom_call_target="tpu_custom_call" | custom-call | bytes 491520 | tf_op jit(solution)/shard_map/pallas_call | solution.py:469
  1.8 4.5 %collective-permute-start = (bf16[4,64,384]{2,1,0:T(8,128)(2,1)S(1)}, bf16[4,64,384]{2,1,0:T(8,128)(2,1)S(1)}, u32[]{:S(2)}, u32[]{:S(2)}) collective-permute-start(bf16[4,64,384]{2,1,0:T(8,128)(2,1)S(1)} %get-tuple-element.32), channel_id=1, source_target_pairs={{1,2},{3,4},{5,6},{7,8},{9,10},{11,12},{13,14},{2,1},{4,3},{6,5},{... | collective-permute-start | bytes 589832 | tf_op jit(solution)/shard_map/ppermute | solution.py:481
  6.5 3.8 %shard_map.115 = (bf16[2,128,384]{2,1,0:T(8,128)(2,1)}, bf16[3,128,384]{2,1,0:T(8,128)(2,1)S(1)}, bf16[3,3,384,1152]{3,2,1,0:T(8,128)(2,1)S(1)}) custom-call(bf16[2,128,384]{2,1,0:T(8,128)(2,1)} %bitcast.8, bf16[2,128,384]{2,1,0:T(8,128)(2,1)} %bitcast.9, bf16[3,3,3,384,384]{4,3,2,1,0:T(8,128)(2,1)} %weight_ref.1, f32[384]{0:T(512)} %norm_gain_ref.1), custom_call_target="tpu_custom_call" | custom-call | flops 983040 | bytes 7962624 | tf_op jit(solution)/shard_map/pallas_call | solution.py:483
  10.3 0.8 %collective-permute-done.edge_ref = bf16[4,64,384]{2,1,0:T(8,128)(2,1)S(1)} collective-permute-done((bf16[4,64,384]{2,1,0:T(8,128)(2,1)S(1)}, bf16[4,64,384]{2,1,0:T(8,128)(2,1)S(1)}, u32[]{:S(2)}, u32[]{:S(2)}) %collective-permute-start) | collective-permute-done | bytes 196640 | tf_op jit(solution)/shard_map/ppermute | solution.py:481
  11.1 1.4 %collective-permute-done.2.far_ref = bf16[4,64,384]{2,1,0:T(8,128)(2,1)S(1)} collective-permute-done((bf16[4,64,384]{2,1,0:T(8,128)(2,1)S(1)}, bf16[4,64,384]{2,1,0:T(8,128)(2,1)S(1)}, u32[]{:S(2)}, u32[]{:S(2)}) %collective-permute-start.2) | collective-permute-done | bytes 196640 | tf_op jit(solution)/shard_map/ppermute | solution.py:509
  12.5 3.1 %shard_map.116 = (bf16[272,384]{1,0:T(8,128)(2,1)S(1)}, bf16[144,384]{1,0:T(8,128)(2,1)S(1)}, bf16[144,384]{1,0:T(8,128)(2,1)S(1)}, f32[256,384]{1,0:T(8,128)S(1)}) custom-call(bf16[3,128,384]{2,1,0:T(8,128)(2,1)S(1)} %get-tuple-element.34.own_ref, bf16[3,128,384]{2,1,0:T(8,128)(2,1)S(1)} %bitcast.6, bf16[4,64,384]{2,1,0:T(8,128)(2,1)S(1)} %collective-permute-done.edge_ref, ...), custom_call_target="tpu_custom_call" | custom-call | flops 2038431744 | bytes 7962624 | tf_op jit(solution)/shard_map/pallas_call | solution.py:512
  15.6 3.1 %collective-permute-start.3 = (bf16[144,384]{1,0:T(8,128)(2,1)S(1)}, bf16[144,384]{1,0:T(8,128)(2,1)S(1)}, u32[]{:S(2)}, u32[]{:S(2)}) collective-permute-start(bf16[144,384]{1,0:T(8,128)(2,1)S(1)} %get-tuple-element.39), channel_id=1, source_target_pairs={{0,4},{1,9},{2,6},{3,11},{4,12},{5,1},{6,14},{7,3},{8,0},{9,13},{1... | collective-permute-start | bytes 331784 | tf_op jit(solution)/shard_map/ppermute | solution.py:396
  18.7 1.5 %collective-permute-start.5 = (bf16[272,384]{1,0:T(8,128)(2,1)S(1)}, bf16[272,384]{1,0:T(8,128)(2,1)S(1)}, u32[]{:S(2)}, u32[]{:S(2)}) collective-permute-start(bf16[272,384]{1,0:T(8,128)(2,1)S(1)} %get-tuple-element.55.refs_0_), channel_id=1, source_target_pairs={{0,2},{1,3},{2,0},{3,1},{4,6},{5,7},{6,4},{7,5},{8,10},{9,11},{10,... | collective-permute-start | bytes 626696 | tf_op jit(solution)/shard_map/ppermute | solution.py:396
  20.2 0.9 %collective-permute-done.3.refs_1_ = bf16[144,384]{1,0:T(8,128)(2,1)S(1)} collective-permute-done((bf16[144,384]{1,0:T(8,128)(2,1)S(1)}, bf16[144,384]{1,0:T(8,128)(2,1)S(1)}, u32[]{:S(2)}, u32[]{:S(2)}) %collective-permute-start.3) | collective-permute-done | bytes 110624 | tf_op jit(solution)/shard_map/ppermute | solution.py:396
  21.2 2.9 %collective-permute-start.6 = (bf16[144,384]{1,0:T(8,128)(2,1)S(1)}, bf16[144,384]{1,0:T(8,128)(2,1)S(1)}, u32[]{:S(2)}, u32[]{:S(2)}) collective-permute-start(bf16[144,384]{1,0:T(8,128)(2,1)S(1)} %collective-permute-done.3.refs_1_), channel_id=1, source_target_pairs={{0,4},{1,9},{2,6},{3,11},{4,12},{5,1},{6,14},{7,3},{8,0},{9,13},{1... | collective-permute-start | bytes 331784 | tf_op jit(solution)/shard_map/ppermute | solution.py:396
  24.1 1.7 %collective-permute-start.7 = (bf16[144,384]{1,0:T(8,128)(2,1)S(1)}, bf16[144,384]{1,0:T(8,128)(2,1)S(1)}, u32[]{:S(2)}, u32[]{:S(2)}) collective-permute-start(bf16[144,384]{1,0:T(8,128)(2,1)S(1)} %collective-permute-done.3.refs_1_), channel_id=1, source_target_pairs={{0,2},{1,3},{2,0},{3,1},{4,6},{5,7},{6,4},{7,5},{8,10},{9,11},{10,... | collective-permute-start | bytes 331784 | tf_op jit(solution)/shard_map/ppermute | solution.py:396
  25.8 0.7 %collective-permute-start.8 = (bf16[144,384]{1,0:T(8,128)(2,1)S(1)}, bf16[144,384]{1,0:T(8,128)(2,1)S(1)}, u32[]{:S(2)}, u32[]{:S(2)}) collective-permute-start(bf16[144,384]{1,0:T(8,128)(2,1)S(1)} %collective-permute-done.4.refs_2_), channel_id=1, source_target_pairs={{0,4},{1,9},{2,6},{3,11},{4,12},{5,1},{6,14},{7,3},{8,0},{9,13},{1... | collective-permute-start | bytes 331784 | tf_op jit(solution)/shard_map/ppermute | solution.py:396
  26.5 1.2 %collective-permute-start.9 = (bf16[144,384]{1,0:T(8,128)(2,1)S(1)}, bf16[144,384]{1,0:T(8,128)(2,1)S(1)}, u32[]{:S(2)}, u32[]{:S(2)}) collective-permute-start(bf16[144,384]{1,0:T(8,128)(2,1)S(1)} %collective-permute-done.4.refs_2_), channel_id=1, source_target_pairs={{0,2},{1,3},{2,0},{3,1},{4,6},{5,7},{6,4},{7,5},{8,10},{9,11},{10,... | collective-permute-start | bytes 331784 | tf_op jit(solution)/shard_map/ppermute | solution.py:396
  27.7 0.8 %collective-permute-done.7.refs_3_ = bf16[144,384]{1,0:T(8,128)(2,1)S(1)} collective-permute-done((bf16[144,384]{1,0:T(8,128)(2,1)S(1)}, bf16[144,384]{1,0:T(8,128)(2,1)S(1)}, u32[]{:S(2)}, u32[]{:S(2)}) %collective-permute-start.7) | collective-permute-done | bytes 110624 | tf_op jit(solution)/shard_map/ppermute | solution.py:396
  28.7 0.4 collective-permute-start.12
  29.1 1.7 %collective-permute-start.10 = (bf16[144,384]{1,0:T(8,128)(2,1)S(1)}, bf16[144,384]{1,0:T(8,128)(2,1)S(1)}, u32[]{:S(2)}, u32[]{:S(2)}) collective-permute-start(bf16[144,384]{1,0:T(8,128)(2,1)S(1)} %collective-permute-done.6.refs_5_), channel_id=1, source_target_pairs={{0,2},{1,3},{2,0},{3,1},{4,6},{5,7},{6,4},{7,5},{8,10},{9,11},{10,... | collective-permute-start | bytes 331784 | tf_op jit(solution)/shard_map/ppermute | solution.py:396
  30.8 2.6 %collective-permute-start.11 = (bf16[144,384]{1,0:T(8,128)(2,1)S(1)}, bf16[144,384]{1,0:T(8,128)(2,1)S(1)}, u32[]{:S(2)}, u32[]{:S(2)}) collective-permute-start(bf16[144,384]{1,0:T(8,128)(2,1)S(1)} %collective-permute-done.8.refs_6_), channel_id=1, source_target_pairs={{0,2},{1,3},{2,0},{3,1},{4,6},{5,7},{6,4},{7,5},{8,10},{9,11},{10,... | collective-permute-start | bytes 331784 | tf_op jit(solution)/shard_map/ppermute | solution.py:396
  33.5 0.5 %shard_map.113 = (bf16[384,384]{1,0:T(8,128)(2,1)S(1)}, bf16[384,384]{1,0:T(8,128)(2,1)S(1)}) custom-call(bf16[384,384]{1,0:T(8,128)(2,1)S(1)} %copy-done, bf16[384,384]{1,0:T(8,128)(2,1)S(1)} %copy-done.1, bf16[384,384]{1,0:T(8,128)(2,1)S(1)} %copy-done.2, bf16[384,384]{1,0:T(8,128)(2,1)S(1)} %copy-done.3), custom_call_target="tpu_custom_call" | custom-call | flops 226492416 | bytes 1769472 | tf_op jit(solution)/shard_map/pallas_call | solution.py:544
  34.0 1.4 %shard_map.117 = (bf16[256,384]{1,0:T(8,128)(2,1)S(1)}, f32[256,128]{1,0:T(8,128)S(1)}, f32[256,128]{1,0:T(8,128)S(1)}, f32[256,384]{1,0:T(8,128)S(1)}) custom-call(bf16[384,384]{1,0:T(8,128)(2,1)S(1)} %get-tuple-element.31.score_ref, bf16[272,384]{1,0:T(8,128)(2,1)S(1)} %get-tuple-element.55.refs_0_, bf16[144,384]{1,0:T(8,128)(2,1)S(1)} %collective-permute-done.3.refs_1_, ...), custom_call_target="tpu_custom_call" | custom-call | flops 503316480 | bytes 983040 | tf_op jit(solution)/shard_map/pallas_call | solution.py:555
  35.5 1.0 %collective-permute-done.12.refs_10_ = bf16[272,384]{1,0:T(8,128)(2,1)S(1)} collective-permute-done((bf16[272,384]{1,0:T(8,128)(2,1)S(1)}, bf16[272,384]{1,0:T(8,128)(2,1)S(1)}, u32[]{:S(2)}, u32[]{:S(2)}) %collective-permute-start.12) | collective-permute-done | bytes 208928 | tf_op jit(solution)/shard_map/ppermute | solution.py:396
  36.5 2.6 %shard_map.118 = (bf16[256,384]{1,0:T(8,128)(2,1)S(1)}, bf16[256,384]{1,0:T(8,128)(2,1)S(1)}) custom-call(bf16[256,384]{1,0:T(8,128)(2,1)S(1)} %get-tuple-element.49.own_query_ref, f32[256,128]{1,0:T(8,128)S(1)} %get-tuple-element.50.peak_ref, f32[256,128]{1,0:T(8,128)S(1)} %get-tuple-element.51.sums_ref, f32[256,384]{1,0:T(8,128)S(1)} %get-tuple-element.52.added_ref, ...), custom_call_target="tpu_custom_call" | custom-call | flops 603979776 | bytes 1572864 | tf_op jit(solution)/shard_map/pallas_call | solution.py:574
  39.0 5.1 %collective-permute-start.14 = (bf16[256,384]{1,0:T(8,128)(2,1)S(1)}, bf16[256,384]{1,0:T(8,128)(2,1)S(1)}, u32[]{:S(2)}, u32[]{:S(2)}) collective-permute-start(bf16[256,384]{1,0:T(8,128)(2,1)S(1)} %get-tuple-element.58), channel_id=1, source_target_pairs={{0,1},{1,0},{2,3},{3,2},{4,5},{5,4},{6,7},{7,6},{8,9},{9,8},{10,11... | collective-permute-start | bytes 589832 | tf_op jit(solution)/shard_map/ppermute | solution.py:603
  44.1 1.1 %collective-permute-done.14.swap_ref = bf16[256,384]{1,0:T(8,128)(2,1)S(1)} collective-permute-done((bf16[256,384]{1,0:T(8,128)(2,1)S(1)}, bf16[256,384]{1,0:T(8,128)(2,1)S(1)}, u32[]{:S(2)}, u32[]{:S(2)}) %collective-permute-start.14) | collective-permute-done | bytes 196640 | tf_op jit(solution)/shard_map/ppermute | solution.py:603
  45.2 3.0 %shard_map.119 = bf16[2,4,192,128]{3,2,1,0:T(8,128)(2,1)} custom-call(bf16[256,384]{1,0:T(8,128)(2,1)S(1)} %get-tuple-element.57.mid_ref, bf16[256,384]{1,0:T(8,128)(2,1)S(1)} %collective-permute-done.14.swap_ref, bf16[3,3,192,384]{3,2,1,0:T(8,128)(2,1)S(1)} %bitcast.7), custom_call_target="tpu_custom_call" | custom-call | flops 1358954496 | bytes 1327104 | tf_op jit(solution)/shard_map/pallas_call | solution.py:606
  (27 shorter events, 0.4 us)
Async XLA Ops:
  0.6 11.9 %copy-start.4 = (f32[384]{0:T(512)S(1)}, f32[384]{0:T(512)}, u32[]{:S(2)}) copy-start(f32[384]{0:T(512)} %norm_gain_ref.1) | copy-start | bytes 4612
  0.6 11.9 %copy-start.5 = (f32[384]{0:T(512)S(1)}, f32[384]{0:T(512)}, u32[]{:S(2)}) copy-start(f32[384]{0:T(512)} %gain_ref.3) | copy-start | bytes 4612
  1.8 9.2 %collective-permute-start = (bf16[4,64,384]{2,1,0:T(8,128)(2,1)S(1)}, bf16[4,64,384]{2,1,0:T(8,128)(2,1)S(1)}, u32[]{:S(2)}, u32[]{:S(2)}) collective-permute-start(bf16[4,64,384]{2,1,0:T(8,128)(2,1)S(1)} %get-tuple-element.32), channel_id=1, source_target_pairs={{1,2},{3,4},{5,6},{7,8},{9,10},{11,12},{13,14},{2,1},{4,3},{6,5},{... | collective-permute-start | bytes 589832 | tf_op jit(solution)/shard_map/ppermute | solution.py:481
  6.3 4.7 %collective-permute-start.1 = (bf16[3,2,64,384]{3,2,1,0:T(8,128)(2,1)S(1)}, bf16[3,2,64,384]{3,2,1,0:T(8,128)(2,1)S(1)}, u32[]{:S(2)}, u32[]{:S(2)}) collective-permute-start(bf16[3,2,64,384]{3,2,1,0:T(8,128)(2,1)S(1)} %get-tuple-element.35), channel_id=1, source_target_pairs={{0,1},{1,0},{2,3},{3,2},{4,5},{5,4},{6,7},{7,6},{8,9},{9,8},{10,11... | collective-permute-start | bytes 884744 | tf_op jit(solution)/shard_map/ppermute | solution.py:482
  6.4 27.0 %copy-start = (bf16[384,384]{1,0:T(8,128)(2,1)S(1)}, bf16[384,384]{1,0:T(8,128)(2,1)}, u32[]{:S(2)}) copy-start(bf16[384,384]{1,0:T(8,128)(2,1)} %query_ref.1) | copy-start | bytes 884740
  6.4 27.0 %copy-start.1 = (bf16[384,384]{1,0:T(8,128)(2,1)S(1)}, bf16[384,384]{1,0:T(8,128)(2,1)}, u32[]{:S(2)}) copy-start(bf16[384,384]{1,0:T(8,128)(2,1)} %key_ref.1) | copy-start | bytes 884740
  6.5 27.0 %copy-start.2 = (bf16[384,384]{1,0:T(8,128)(2,1)S(1)}, bf16[384,384]{1,0:T(8,128)(2,1)}, u32[]{:S(2)}) copy-start(bf16[384,384]{1,0:T(8,128)(2,1)} %value_ref.1) | copy-start | bytes 884740
  6.5 27.0 %copy-start.3 = (bf16[384,384]{1,0:T(8,128)(2,1)S(1)}, bf16[384,384]{1,0:T(8,128)(2,1)}, u32[]{:S(2)}) copy-start(bf16[384,384]{1,0:T(8,128)(2,1)} %out_ref.1) | copy-start | bytes 884740
  10.2 35.0 %copy-start.6 = (bf16[3,3,384,192]{2,3,1,0:T(8,128)(2,1)S(1)}, bf16[3,3,384,192]{2,3,1,0:T(8,128)(2,1)}, u32[]{:S(2)}) copy-start(bf16[3,3,384,192]{2,3,1,0:T(8,128)(2,1)} %param.19) | copy-start | bytes 3981316
  11.0 1.4 %collective-permute-start.2 = (bf16[4,64,384]{2,1,0:T(8,128)(2,1)S(1)}, bf16[4,64,384]{2,1,0:T(8,128)(2,1)S(1)}, u32[]{:S(2)}, u32[]{:S(2)}) collective-permute-start(bf16[4,64,384]{2,1,0:T(8,128)(2,1)S(1)} %collective-permute-done.edge_ref), channel_id=1, source_target_pairs={{0,1},{1,0},{2,3},{3,2},{4,5},{5,4},{6,7},{7,6},{8,9},{9,8},{10,11... | collective-permute-start | bytes 589832 | tf_op jit(solution)/shard_map/ppermute | solution.py:509
  15.6 5.6 %collective-permute-start.3 = (bf16[144,384]{1,0:T(8,128)(2,1)S(1)}, bf16[144,384]{1,0:T(8,128)(2,1)S(1)}, u32[]{:S(2)}, u32[]{:S(2)}) collective-permute-start(bf16[144,384]{1,0:T(8,128)(2,1)S(1)} %get-tuple-element.39), channel_id=1, source_target_pairs={{0,4},{1,9},{2,6},{3,11},{4,12},{5,1},{6,14},{7,3},{8,0},{9,13},{1... | collective-permute-start | bytes 331784 | tf_op jit(solution)/shard_map/ppermute | solution.py:396
  18.7 7.1 %collective-permute-start.5 = (bf16[272,384]{1,0:T(8,128)(2,1)S(1)}, bf16[272,384]{1,0:T(8,128)(2,1)S(1)}, u32[]{:S(2)}, u32[]{:S(2)}) collective-permute-start(bf16[272,384]{1,0:T(8,128)(2,1)S(1)} %get-tuple-element.55.refs_0_), channel_id=1, source_target_pairs={{0,2},{1,3},{2,0},{3,1},{4,6},{5,7},{6,4},{7,5},{8,10},{9,11},{10,... | collective-permute-start | bytes 626696 | tf_op jit(solution)/shard_map/ppermute | solution.py:396
  20.2 5.6 %collective-permute-start.4 = (bf16[144,384]{1,0:T(8,128)(2,1)S(1)}, bf16[144,384]{1,0:T(8,128)(2,1)S(1)}, u32[]{:S(2)}, u32[]{:S(2)}) collective-permute-start(bf16[144,384]{1,0:T(8,128)(2,1)S(1)} %get-tuple-element.40), channel_id=1, source_target_pairs={{0,4},{1,9},{2,6},{3,11},{4,12},{5,1},{6,14},{7,3},{8,0},{9,13},{1... | collective-permute-start | bytes 331784 | tf_op jit(solution)/shard_map/ppermute | solution.py:396
  21.2 6.6 %collective-permute-start.6 = (bf16[144,384]{1,0:T(8,128)(2,1)S(1)}, bf16[144,384]{1,0:T(8,128)(2,1)S(1)}, u32[]{:S(2)}, u32[]{:S(2)}) collective-permute-start(bf16[144,384]{1,0:T(8,128)(2,1)S(1)} %collective-permute-done.3.refs_1_), channel_id=1, source_target_pairs={{0,4},{1,9},{2,6},{3,11},{4,12},{5,1},{6,14},{7,3},{8,0},{9,13},{1... | collective-permute-start | bytes 331784 | tf_op jit(solution)/shard_map/ppermute | solution.py:396
  24.1 4.5 %collective-permute-start.7 = (bf16[144,384]{1,0:T(8,128)(2,1)S(1)}, bf16[144,384]{1,0:T(8,128)(2,1)S(1)}, u32[]{:S(2)}, u32[]{:S(2)}) collective-permute-start(bf16[144,384]{1,0:T(8,128)(2,1)S(1)} %collective-permute-done.3.refs_1_), channel_id=1, source_target_pairs={{0,2},{1,3},{2,0},{3,1},{4,6},{5,7},{6,4},{7,5},{8,10},{9,11},{10,... | collective-permute-start | bytes 331784 | tf_op jit(solution)/shard_map/ppermute | solution.py:396
  25.8 5.1 %collective-permute-start.8 = (bf16[144,384]{1,0:T(8,128)(2,1)S(1)}, bf16[144,384]{1,0:T(8,128)(2,1)S(1)}, u32[]{:S(2)}, u32[]{:S(2)}) collective-permute-start(bf16[144,384]{1,0:T(8,128)(2,1)S(1)} %collective-permute-done.4.refs_2_), channel_id=1, source_target_pairs={{0,4},{1,9},{2,6},{3,11},{4,12},{5,1},{6,14},{7,3},{8,0},{9,13},{1... | collective-permute-start | bytes 331784 | tf_op jit(solution)/shard_map/ppermute | solution.py:396
  26.5 4.4 %collective-permute-start.9 = (bf16[144,384]{1,0:T(8,128)(2,1)S(1)}, bf16[144,384]{1,0:T(8,128)(2,1)S(1)}, u32[]{:S(2)}, u32[]{:S(2)}) collective-permute-start(bf16[144,384]{1,0:T(8,128)(2,1)S(1)} %collective-permute-done.4.refs_2_), channel_id=1, source_target_pairs={{0,2},{1,3},{2,0},{3,1},{4,6},{5,7},{6,4},{7,5},{8,10},{9,11},{10,... | collective-permute-start | bytes 331784 | tf_op jit(solution)/shard_map/ppermute | solution.py:396
  28.5 6.9 %collective-permute-start.13 = (bf16[272,384]{1,0:T(8,128)(2,1)S(1)}, bf16[272,384]{1,0:T(8,128)(2,1)S(1)}, u32[]{:S(2)}, u32[]{:S(2)}) collective-permute-start(bf16[272,384]{1,0:T(8,128)(2,1)S(1)} %collective-permute-done.5.refs_7_), channel_id=1, source_target_pairs={{0,8},{1,5},{2,10},{3,7},{4,0},{5,13},{6,2},{7,15},{8,12},{9,1},{1... | collective-permute-start | bytes 626696 | tf_op jit(solution)/shard_map/ppermute | solution.py:396
  28.7 7.7 %collective-permute-start.12 = (bf16[272,384]{1,0:T(8,128)(2,1)S(1)}, bf16[272,384]{1,0:T(8,128)(2,1)S(1)}, u32[]{:S(2)}, u32[]{:S(2)}) collective-permute-start(bf16[272,384]{1,0:T(8,128)(2,1)S(1)} %get-tuple-element.55.refs_0_), channel_id=1, source_target_pairs={{0,8},{1,5},{2,10},{3,7},{4,0},{5,13},{6,2},{7,15},{8,12},{9,1},{1... | collective-permute-start | bytes 626696 | tf_op jit(solution)/shard_map/ppermute | solution.py:396
  29.1 6.4 %collective-permute-start.10 = (bf16[144,384]{1,0:T(8,128)(2,1)S(1)}, bf16[144,384]{1,0:T(8,128)(2,1)S(1)}, u32[]{:S(2)}, u32[]{:S(2)}) collective-permute-start(bf16[144,384]{1,0:T(8,128)(2,1)S(1)} %collective-permute-done.6.refs_5_), channel_id=1, source_target_pairs={{0,2},{1,3},{2,0},{3,1},{4,6},{5,7},{6,4},{7,5},{8,10},{9,11},{10,... | collective-permute-start | bytes 331784 | tf_op jit(solution)/shard_map/ppermute | solution.py:396
  30.8 5.6 %collective-permute-start.11 = (bf16[144,384]{1,0:T(8,128)(2,1)S(1)}, bf16[144,384]{1,0:T(8,128)(2,1)S(1)}, u32[]{:S(2)}, u32[]{:S(2)}) collective-permute-start(bf16[144,384]{1,0:T(8,128)(2,1)S(1)} %collective-permute-done.8.refs_6_), channel_id=1, source_target_pairs={{0,2},{1,3},{2,0},{3,1},{4,6},{5,7},{6,4},{7,5},{8,10},{9,11},{10,... | collective-permute-start | bytes 331784 | tf_op jit(solution)/shard_map/ppermute | solution.py:396
  39.0 6.2 %collective-permute-start.14 = (bf16[256,384]{1,0:T(8,128)(2,1)S(1)}, bf16[256,384]{1,0:T(8,128)(2,1)S(1)}, u32[]{:S(2)}, u32[]{:S(2)}) collective-permute-start(bf16[256,384]{1,0:T(8,128)(2,1)S(1)} %get-tuple-element.58), channel_id=1, source_target_pairs={{0,1},{1,0},{2,3},{3,2},{4,5},{5,4},{6,7},{7,6},{8,9},{9,8},{10,11... | collective-permute-start | bytes 589832 | tf_op jit(solution)/shard_map/ppermute | solution.py:603
where the time goes:
time: 48.7 us; the launch traced here: 48.2 us
  starting transfers between devices  25.9 us (53%)
  Pallas kernels  15.5 us (32%)
  waiting for transfers between devices  6 us (12%)
  between operations  0.77 us (2%)
    ppermute x11, starting transfers between devices, send(): return [lax.ppermute(part, 'rows', pairs) for part in parts]  16.1 us
    ppermute x1, starting transfers between devices, shards(): swap_rows = lax.ppermute(swap_rows, 'rows', swap)  5.1 us
    ppermute x1, starting transfers between devices, shards(): edge_rows = lax.ppermute(edge_rows, 'rows', neighbour)  4.54 us
    pallas_call x1, Pallas kernels, shards(): pl.pallas_call(prepare_kernel, out_shape=(jax.ShapeDtypeStruct((frames, o...  3.76 us
    pallas_call x1, Pallas kernels, shards(): pl.pallas_call(functools.partial(conv_kernel, width), out_shape=(block, h...  3.08 us
    pallas_call x1, Pallas kernels, shards(): pl.pallas_call(functools.partial(up_kernel, width), out_shape=jax.ShapeDt...  2.98 us
    ppermute x11, waiting for transfers between devices, send(): return [lax.ppermute(part, 'rows', pairs) for part in parts]  2.7 us
    pallas_call x1, Pallas kernels, shards(): pl.pallas_call(functools.partial(late_kernel, width, sources, counts, len...  2.59 us
  transfers between devices with their start and end apart: 15, of which 6 were waited for; matrix products, arithmetic and copies ran while one was open for 0% of the time, Pallas kernels for 12%

commit v1 on v0

--- a/solution.py
+++ b/solution.py
@@ -337,43 +337,44 @@
     swap_ref[...] = mid[pl.ds(pl.multiple_of(2 * (1 - core) * width, width), 4 * width), :]
 
 
-def up_kernel(width, mid_ref, swap_ref, weight_ref, out_ref, fine, total, results, sems):
+def up_kernel(width, mid_ref, swap_ref, weight_ref, out_ref, results, sems):
     core = lax.axis_index("rows") % 2
     channels = mid_ref.shape[1]
     outputs = weight_ref.shape[2]
     wide = 2 * width
     lane = lax.broadcasted_iota(jnp.int32, (1, wide), 1)
-    lhs = weight_ref[...].reshape(9 * outputs, channels)
+    low = lax.broadcasted_iota(jnp.int32, (width, wide), 0)
+    spread = (lax.broadcasted_iota(jnp.int32, (width, wide), 1) // 2 == low).astype(BF16)
+    lhs = jnp.concatenate(
+        [weight_ref[j].reshape(3 * outputs, channels) for j in range(3)], axis=1
+    )
     stores = []
     for slot, ref, frame in ((0, mid_ref, core), (1, swap_ref, 1 - core)):
-        values = ref[...].astype(F32)
-        pieces = []
-        for i in range(channels // 128):
-            piece = values[:, 128 * i : 128 * (i + 1)]
-            fine[slot, i, pl.ds(0, 4 * width, stride=2), :] = piece
-            fine[slot, i, pl.ds(1, 4 * width, stride=2), :] = piece
-            pieces.append(fine[slot, i].astype(BF16))
-        total[slot] = nt_dot(lhs, jnp.concatenate(pieces, axis=1))
-        for row in range(4):
-            low = row // 2 + 1
-            picks = (low - 1, low, low) if row % 2 == 0 else (low, low, low + 1)
-            taps = []
-            for col in range(3):
-                tap = None
-                for j, pick in enumerate(picks):
-                    piece = total[
-                        slot,
-                        (3 * j + col) * outputs : (3 * j + col + 1) * outputs,
-                        pick * wide : (pick + 1) * wide,
-                    ]
-                    tap = piece if tap is None else tap + piece
-                taps.append(tap)
-            result = taps[1]
-            result = result + jnp.where(lane == 0, 0.0, pltpu.roll(taps[0], 1, axis=1))
-            result = result + jnp.where(
-                lane == wide - 1, 0.0, pltpu.roll(taps[2], wide - 1, axis=1)
+        rows = [
+            lax.dot_general(
+                ref[row * width : (row + 1) * width],
+                spread,
+                (((0,), (0,)), ((), ())),
+                preferred_element_type=F32,
+            ).astype(BF16)
+            for row in range(4)
+        ]
+        for phase in range(2):
+            pairs = [(0, 1, 1), (1, 2, 2)] if phase == 0 else [(1, 1, 2), (2, 2, 3)]
+            rhs = jnp.concatenate(
+                [jnp.concatenate([rows[p] for p in picks], axis=0) for picks in pairs], axis=1
             )
-            results[slot, row] = result.astype(BF16)
+            taps = jnp.dot(lhs, rhs, preferred_element_type=F32)
+            for i in range(2):
+                left, middle, right = (
+                    taps[col * outputs : (col + 1) * outputs, i * wide : (i + 1) * wide]
+                    for col in range(3)
+                )
+                result = middle + jnp.where(lane == 0, 0.0, pltpu.roll(left, 1, axis=1))
+                result = result + jnp.where(
+                    lane == wide - 1, 0.0, pltpu.roll(right, wide - 1, axis=1)
+                )
+                results[slot, 2 * i + phase] = result.astype(BF16)
         stores = stores + start_all([(results.at[slot], out_ref.at[frame])], sems, slot)
     wait_all(stores)
 
@@ -417,24 +418,24 @@
             places = [(parts, h)]
             if last:
                 places.append((last, h))
-            if (step, h) == (1, 1) and depth == 2:
-                places.append((crossed, 0))
+            if step == 1 and h == 1:
+                places.append((own_again, 0))
+                if depth == 2:
+                    places.append((crossed, 0))
             tie(*places)
         early.append((parts, origin))
         if depth == 2:
             last = send(parts, across)
             (late if step == steps else early).append((last, moved(origin, across)))
     if length > 1:
-        if steps > 0:
-            tie((own_again, 0), (parts, 0))
         late.append((send(own_again, backward), moved(here, backward)))
     if depth == 2:
         (early if length > 1 else late).append((crossed, moved(here, across)))
         if length > 1:
-            again = list(crossed)
             if steps > 0:
-                tie((again, 0), (parts, 0))
-            late.append((send(again, backward), moved(moved(here, across), backward)))
+                crossed = list(crossed)
+                tie((crossed, 0), (parts, 0))
+            late.append((send(crossed, backward), moved(moved(here, across), backward)))
     return early, late
 
 
@@ -609,8 +610,6 @@
         in_specs=[vmem()] * 3,
         out_specs=anywhere,
         scratch_shapes=[
-            pltpu.VMEM((2, channels // 128, 8 * width, 128), F32),
-            pltpu.VMEM((2, 9 * outputs, 8 * width), F32),
             pltpu.VMEM((2, *fine_shape), BF16),
             pltpu.SemaphoreType.DMA((2,)),
         ],

time: 48.7 us -> 48 us (0.986)
  waiting for transfers between devices: 6 us -> 5.35 us
    ppermute x11, starting transfers between devices: 16.1 us -> 18.6 us  [send(): return [lax.ppermute(part, 'rows', pairs) for part in parts]]
    ppermute x1, starting transfers between devices: 5.1 us -> 2.72 us  [shards(): swap_rows = lax.ppermute(swap_rows, 'rows', swap)]
    ppermute x11, waiting for transfers between devices: 2.7 us -> 2.04 us  [send(): return [lax.ppermute(part, 'rows', pairs) for part in parts]]
  transfers between devices with their start and end apart: 15 -> 15, of which waited for: 6 -> 7; matrix products, arithmetic and copies ran while one was open for 0% -> 0% of each run, Pallas kernels for 12% -> 12%
where the time goes in v1:
time: 48 us; the launch traced here: 47.5 us
  starting transfers between devices  25.9 us (54%)
  Pallas kernels  15.5 us (32%)
  waiting for transfers between devices  5.35 us (11%)
  between operations  0.77 us (2%)
    ppermute x11, starting transfers between devices, send(): return [lax.ppermute(part, 'rows', pairs) for part in parts]  18.6 us
    ppermute x1, starting transfers between devices, shards(): edge_rows = lax.ppermute(edge_rows, 'rows', neighbour)  4.54 us
    pallas_call x1, Pallas kernels, shards(): pl.pallas_call(prepare_kernel, out_shape=(jax.ShapeDtypeStruct((frames, o...  3.76 us
    pallas_call x1, Pallas kernels, shards(): pl.pallas_call(functools.partial(conv_kernel, width), out_shape=(block, h...  3.08 us
    pallas_call x1, Pallas kernels, shards(): pl.pallas_call(functools.partial(up_kernel, width), out_shape=jax.ShapeDt...  2.93 us
    ppermute x1, starting transfers between devices, shards(): swap_rows = lax.ppermute(swap_rows, 'rows', swap)  2.72 us
    pallas_call x1, Pallas kernels, shards(): pl.pallas_call(functools.partial(late_kernel, width, sources, counts, len...  2.57 us
    ppermute x11, waiting for transfers between devices, send(): return [lax.ppermute(part, 'rows', pairs) for part in parts]  2.04 us
  transfers between devices with their start and end apart: 15, of which 7 were waited for; matrix products, arithmetic and copies ran while one was open for 0% of the time, Pallas kernels for 12%

profile of v1, /device:TPU:1, one launch (start us, length us, event | category | flops | bytes accessed | tf_op | source)
XLA Modules:
  0.0 47.5 jit_solution(10508469265836815497)
XLA Ops:
  0.7 1.1 %shard_map.114 = (bf16[4,64,384]{2,1,0:T(8,128)(2,1)S(1)}, bf16[3,2,64,384]{3,2,1,0:T(8,128)(2,1)S(1)}) custom-call(bf16[2,2,64,384]{3,2,1,0:T(8,128)(2,1)} %latents_ref.1, bf16[2,2,64,384]{3,2,1,0:T(8,128)(2,1)} %cache_ref.1), custom_call_target="tpu_custom_call" | custom-call | bytes 491520 | tf_op jit(solution)/shard_map/pallas_call | solution.py:470
  1.8 4.5 %collective-permute-start = (bf16[4,64,384]{2,1,0:T(8,128)(2,1)S(1)}, bf16[4,64,384]{2,1,0:T(8,128)(2,1)S(1)}, u32[]{:S(2)}, u32[]{:S(2)}) collective-permute-start(bf16[4,64,384]{2,1,0:T(8,128)(2,1)S(1)} %get-tuple-element.31), channel_id=1, source_target_pairs={{1,2},{3,4},{5,6},{7,8},{9,10},{11,12},{13,14},{2,1},{4,3},{6,5},{... | collective-permute-start | bytes 589832 | tf_op jit(solution)/shard_map/ppermute | solution.py:482
  6.5 3.8 %shard_map.115 = (bf16[2,128,384]{2,1,0:T(8,128)(2,1)}, bf16[3,128,384]{2,1,0:T(8,128)(2,1)S(1)}, bf16[3,3,384,1152]{3,2,1,0:T(8,128)(2,1)S(1)}) custom-call(bf16[2,128,384]{2,1,0:T(8,128)(2,1)} %bitcast.8, bf16[2,128,384]{2,1,0:T(8,128)(2,1)} %bitcast.9, bf16[3,3,3,384,384]{4,3,2,1,0:T(8,128)(2,1)} %weight_ref.1, f32[384]{0:T(512)} %norm_gain_ref.1), custom_call_target="tpu_custom_call" | custom-call | flops 983040 | bytes 7962624 | tf_op jit(solution)/shard_map/pallas_call | solution.py:484
  10.3 0.8 %collective-permute-done.edge_ref = bf16[4,64,384]{2,1,0:T(8,128)(2,1)S(1)} collective-permute-done((bf16[4,64,384]{2,1,0:T(8,128)(2,1)S(1)}, bf16[4,64,384]{2,1,0:T(8,128)(2,1)S(1)}, u32[]{:S(2)}, u32[]{:S(2)}) %collective-permute-start) | collective-permute-done | bytes 196640 | tf_op jit(solution)/shard_map/ppermute | solution.py:482
  11.1 1.4 %collective-permute-done.2.far_ref = bf16[4,64,384]{2,1,0:T(8,128)(2,1)S(1)} collective-permute-done((bf16[4,64,384]{2,1,0:T(8,128)(2,1)S(1)}, bf16[4,64,384]{2,1,0:T(8,128)(2,1)S(1)}, u32[]{:S(2)}, u32[]{:S(2)}) %collective-permute-start.2) | collective-permute-done | bytes 196640 | tf_op jit(solution)/shard_map/ppermute | solution.py:510
  12.5 3.1 %shard_map.116 = (bf16[272,384]{1,0:T(8,128)(2,1)S(1)}, bf16[144,384]{1,0:T(8,128)(2,1)S(1)}, bf16[144,384]{1,0:T(8,128)(2,1)S(1)}, f32[256,384]{1,0:T(8,128)S(1)}) custom-call(bf16[3,128,384]{2,1,0:T(8,128)(2,1)S(1)} %get-tuple-element.33.own_ref, bf16[3,128,384]{2,1,0:T(8,128)(2,1)S(1)} %bitcast.6, bf16[4,64,384]{2,1,0:T(8,128)(2,1)S(1)} %collective-permute-done.edge_ref, ...), custom_call_target="tpu_custom_call" | custom-call | flops 2038431744 | bytes 7962624 | tf_op jit(solution)/shard_map/pallas_call | solution.py:513
  15.6 3.1 %collective-permute-start.3 = (bf16[144,384]{1,0:T(8,128)(2,1)S(1)}, bf16[144,384]{1,0:T(8,128)(2,1)S(1)}, u32[]{:S(2)}, u32[]{:S(2)}) collective-permute-start(bf16[144,384]{1,0:T(8,128)(2,1)S(1)} %get-tuple-element.38), channel_id=1, source_target_pairs={{0,4},{1,9},{2,6},{3,11},{4,12},{5,1},{6,14},{7,3},{8,0},{9,13},{1... | collective-permute-start | bytes 331784 | tf_op jit(solution)/shard_map/ppermute | solution.py:397
  18.7 1.5 %collective-permute-start.5 = (bf16[272,384]{1,0:T(8,128)(2,1)S(1)}, bf16[272,384]{1,0:T(8,128)(2,1)S(1)}, u32[]{:S(2)}, u32[]{:S(2)}) collective-permute-start(bf16[272,384]{1,0:T(8,128)(2,1)S(1)} %get-tuple-element.53.refs_0_), channel_id=1, source_target_pairs={{0,2},{1,3},{2,0},{3,1},{4,6},{5,7},{6,4},{7,5},{8,10},{9,11},{10,... | collective-permute-start | bytes 626696 | tf_op jit(solution)/shard_map/ppermute | solution.py:397
  20.2 0.9 %collective-permute-done.3.refs_1_ = bf16[144,384]{1,0:T(8,128)(2,1)S(1)} collective-permute-done((bf16[144,384]{1,0:T(8,128)(2,1)S(1)}, bf16[144,384]{1,0:T(8,128)(2,1)S(1)}, u32[]{:S(2)}, u32[]{:S(2)}) %collective-permute-start.3) | collective-permute-done | bytes 110624 | tf_op jit(solution)/shard_map/ppermute | solution.py:397
  21.2 2.9 %collective-permute-start.6 = (bf16[144,384]{1,0:T(8,128)(2,1)S(1)}, bf16[144,384]{1,0:T(8,128)(2,1)S(1)}, u32[]{:S(2)}, u32[]{:S(2)}) collective-permute-start(bf16[144,384]{1,0:T(8,128)(2,1)S(1)} %collective-permute-done.3.refs_1_), channel_id=1, source_target_pairs={{0,4},{1,9},{2,6},{3,11},{4,12},{5,1},{6,14},{7,3},{8,0},{9,13},{1... | collective-permute-start | bytes 331784 | tf_op jit(solution)/shard_map/ppermute | solution.py:397
  24.1 1.7 %collective-permute-start.7 = (bf16[144,384]{1,0:T(8,128)(2,1)S(1)}, bf16[144,384]{1,0:T(8,128)(2,1)S(1)}, u32[]{:S(2)}, u32[]{:S(2)}) collective-permute-start(bf16[144,384]{1,0:T(8,128)(2,1)S(1)} %collective-permute-done.3.refs_1_), channel_id=1, source_target_pairs={{0,2},{1,3},{2,0},{3,1},{4,6},{5,7},{6,4},{7,5},{8,10},{9,11},{10,... | collective-permute-start | bytes 331784 | tf_op jit(solution)/shard_map/ppermute | solution.py:397
  25.8 0.7 %collective-permute-start.8 = (bf16[144,384]{1,0:T(8,128)(2,1)S(1)}, bf16[144,384]{1,0:T(8,128)(2,1)S(1)}, u32[]{:S(2)}, u32[]{:S(2)}) collective-permute-start(bf16[144,384]{1,0:T(8,128)(2,1)S(1)} %collective-permute-done.4.refs_2_), channel_id=1, source_target_pairs={{0,4},{1,9},{2,6},{3,11},{4,12},{5,1},{6,14},{7,3},{8,0},{9,13},{1... | collective-permute-start | bytes 331784 | tf_op jit(solution)/shard_map/ppermute | solution.py:397
  26.5 1.2 %collective-permute-start.9 = (bf16[144,384]{1,0:T(8,128)(2,1)S(1)}, bf16[144,384]{1,0:T(8,128)(2,1)S(1)}, u32[]{:S(2)}, u32[]{:S(2)}) collective-permute-start(bf16[144,384]{1,0:T(8,128)(2,1)S(1)} %collective-permute-done.4.refs_2_), channel_id=1, source_target_pairs={{0,2},{1,3},{2,0},{3,1},{4,6},{5,7},{6,4},{7,5},{8,10},{9,11},{10,... | collective-permute-start | bytes 331784 | tf_op jit(solution)/shard_map/ppermute | solution.py:397
  27.7 1.0 %collective-permute-start.12 = (bf16[272,384]{1,0:T(8,128)(2,1)S(1)}, bf16[272,384]{1,0:T(8,128)(2,1)S(1)}, u32[]{:S(2)}, u32[]{:S(2)}) collective-permute-start(bf16[272,384]{1,0:T(8,128)(2,1)S(1)} %get-tuple-element.53.refs_0_), channel_id=1, source_target_pairs={{0,8},{1,5},{2,10},{3,7},{4,0},{5,13},{6,2},{7,15},{8,12},{9,1},{1... | collective-permute-start | bytes 626696 | tf_op jit(solution)/shard_map/ppermute | solution.py:397
  28.8 1.6 %collective-permute-start.10 = (bf16[144,384]{1,0:T(8,128)(2,1)S(1)}, bf16[144,384]{1,0:T(8,128)(2,1)S(1)}, u32[]{:S(2)}, u32[]{:S(2)}) collective-permute-start(bf16[144,384]{1,0:T(8,128)(2,1)S(1)} %collective-permute-done.6.refs_5_), channel_id=1, source_target_pairs={{0,2},{1,3},{2,0},{3,1},{4,6},{5,7},{6,4},{7,5},{8,10},{9,11},{10,... | collective-permute-start | bytes 331784 | tf_op jit(solution)/shard_map/ppermute | solution.py:397
  30.6 4.7 %collective-permute-start.11 = (bf16[144,384]{1,0:T(8,128)(2,1)S(1)}, bf16[144,384]{1,0:T(8,128)(2,1)S(1)}, u32[]{:S(2)}, u32[]{:S(2)}) collective-permute-start(bf16[144,384]{1,0:T(8,128)(2,1)S(1)} %collective-permute-done.8.refs_6_), channel_id=1, source_target_pairs={{0,2},{1,3},{2,0},{3,1},{4,6},{5,7},{6,4},{7,5},{8,10},{9,11},{10,... | collective-permute-start | bytes 331784 | tf_op jit(solution)/shard_map/ppermute | solution.py:397
  35.3 0.5 %shard_map.113 = (bf16[384,384]{1,0:T(8,128)(2,1)S(1)}, bf16[384,384]{1,0:T(8,128)(2,1)S(1)}) custom-call(bf16[384,384]{1,0:T(8,128)(2,1)S(1)} %copy-done, bf16[384,384]{1,0:T(8,128)(2,1)S(1)} %copy-done.1, bf16[384,384]{1,0:T(8,128)(2,1)S(1)} %copy-done.2, bf16[384,384]{1,0:T(8,128)(2,1)S(1)} %copy-done.3), custom_call_target="tpu_custom_call" | custom-call | flops 226492416 | bytes 1769472 | tf_op jit(solution)/shard_map/pallas_call | solution.py:545
  35.8 1.4 %shard_map.117 = (bf16[256,384]{1,0:T(8,128)(2,1)S(1)}, f32[256,128]{1,0:T(8,128)S(1)}, f32[256,128]{1,0:T(8,128)S(1)}, f32[256,384]{1,0:T(8,128)S(1)}) custom-call(bf16[384,384]{1,0:T(8,128)(2,1)S(1)} %get-tuple-element.30.score_ref, bf16[272,384]{1,0:T(8,128)(2,1)S(1)} %get-tuple-element.53.refs_0_, bf16[144,384]{1,0:T(8,128)(2,1)S(1)} %collective-permute-done.3.refs_1_, ...), custom_call_target="tpu_custom_call" | custom-call | flops 503316480 | bytes 983040 | tf_op jit(solution)/shard_map/pallas_call | solution.py:556
  37.3 0.3 collective-permute-done.13.refs_11_
  37.6 0.7 %collective-permute-done.11.refs_9_ = bf16[144,384]{1,0:T(8,128)(2,1)S(1)} collective-permute-done((bf16[144,384]{1,0:T(8,128)(2,1)S(1)}, bf16[144,384]{1,0:T(8,128)(2,1)S(1)}, u32[]{:S(2)}, u32[]{:S(2)}) %collective-permute-start.11) | collective-permute-done | bytes 110624 | tf_op jit(solution)/shard_map/ppermute | solution.py:397
  38.2 2.6 %shard_map.118 = (bf16[256,384]{1,0:T(8,128)(2,1)S(1)}, bf16[256,384]{1,0:T(8,128)(2,1)S(1)}) custom-call(bf16[256,384]{1,0:T(8,128)(2,1)S(1)} %get-tuple-element.47.own_query_ref, f32[256,128]{1,0:T(8,128)S(1)} %get-tuple-element.48.peak_ref, f32[256,128]{1,0:T(8,128)S(1)} %get-tuple-element.49.sums_ref, f32[256,384]{1,0:T(8,128)S(1)} %get-tuple-element.50.added_ref, ...), custom_call_target="tpu_custom_call" | custom-call | flops 603979776 | bytes 1572864 | tf_op jit(solution)/shard_map/pallas_call | solution.py:575
  40.8 2.7 %collective-permute-start.14 = (bf16[256,384]{1,0:T(8,128)(2,1)S(1)}, bf16[256,384]{1,0:T(8,128)(2,1)S(1)}, u32[]{:S(2)}, u32[]{:S(2)}) collective-permute-start(bf16[256,384]{1,0:T(8,128)(2,1)S(1)} %get-tuple-element.56), channel_id=1, source_target_pairs={{0,1},{1,0},{2,3},{3,2},{4,5},{5,4},{6,7},{7,6},{8,9},{9,8},{10,11... | collective-permute-start | bytes 589832 | tf_op jit(solution)/shard_map/ppermute | solution.py:604
  43.5 1.1 %collective-permute-done.14.swap_ref = bf16[256,384]{1,0:T(8,128)(2,1)S(1)} collective-permute-done((bf16[256,384]{1,0:T(8,128)(2,1)S(1)}, bf16[256,384]{1,0:T(8,128)(2,1)S(1)}, u32[]{:S(2)}, u32[]{:S(2)}) %collective-permute-start.14) | collective-permute-done | bytes 196640 | tf_op jit(solution)/shard_map/ppermute | solution.py:604
  44.6 2.9 %shard_map.119 = bf16[2,4,192,128]{3,2,1,0:T(8,128)(2,1)} custom-call(bf16[256,384]{1,0:T(8,128)(2,1)S(1)} %get-tuple-element.55.mid_ref, bf16[256,384]{1,0:T(8,128)(2,1)S(1)} %collective-permute-done.14.swap_ref, bf16[3,3,192,384]{3,2,1,0:T(8,128)(2,1)S(1)} %bitcast.7), custom_call_target="tpu_custom_call" | custom-call | flops 1358954496 | bytes 1327104 | tf_op jit(solution)/shard_map/pallas_call | solution.py:607
  (27 shorter events, 0.4 us)
Async XLA Ops:
  0.6 11.9 %copy-start.4 = (f32[384]{0:T(512)S(1)}, f32[384]{0:T(512)}, u32[]{:S(2)}) copy-start(f32[384]{0:T(512)} %norm_gain_ref.1) | copy-start | bytes 4612
  0.6 11.9 %copy-start.5 = (f32[384]{0:T(512)S(1)}, f32[384]{0:T(512)}, u32[]{:S(2)}) copy-start(f32[384]{0:T(512)} %gain_ref.3) | copy-start | bytes 4612
  1.8 9.2 %collective-permute-start = (bf16[4,64,384]{2,1,0:T(8,128)(2,1)S(1)}, bf16[4,64,384]{2,1,0:T(8,128)(2,1)S(1)}, u32[]{:S(2)}, u32[]{:S(2)}) collective-permute-start(bf16[4,64,384]{2,1,0:T(8,128)(2,1)S(1)} %get-tuple-element.31), channel_id=1, source_target_pairs={{1,2},{3,4},{5,6},{7,8},{9,10},{11,12},{13,14},{2,1},{4,3},{6,5},{... | collective-permute-start | bytes 589832 | tf_op jit(solution)/shard_map/ppermute | solution.py:482
  6.3 4.7 %collective-permute-start.1 = (bf16[3,2,64,384]{3,2,1,0:T(8,128)(2,1)S(1)}, bf16[3,2,64,384]{3,2,1,0:T(8,128)(2,1)S(1)}, u32[]{:S(2)}, u32[]{:S(2)}) collective-permute-start(bf16[3,2,64,384]{3,2,1,0:T(8,128)(2,1)S(1)} %get-tuple-element.34), channel_id=1, source_target_pairs={{0,1},{1,0},{2,3},{3,2},{4,5},{5,4},{6,7},{7,6},{8,9},{9,8},{10,11... | collective-permute-start | bytes 884744 | tf_op jit(solution)/shard_map/ppermute | solution.py:483
  6.4 28.8 %copy-start = (bf16[384,384]{1,0:T(8,128)(2,1)S(1)}, bf16[384,384]{1,0:T(8,128)(2,1)}, u32[]{:S(2)}) copy-start(bf16[384,384]{1,0:T(8,128)(2,1)} %query_ref.1) | copy-start | bytes 884740
  6.4 28.8 %copy-start.1 = (bf16[384,384]{1,0:T(8,128)(2,1)S(1)}, bf16[384,384]{1,0:T(8,128)(2,1)}, u32[]{:S(2)}) copy-start(bf16[384,384]{1,0:T(8,128)(2,1)} %key_ref.1) | copy-start | bytes 884740
  6.5 28.8 %copy-start.2 = (bf16[384,384]{1,0:T(8,128)(2,1)S(1)}, bf16[384,384]{1,0:T(8,128)(2,1)}, u32[]{:S(2)}) copy-start(bf16[384,384]{1,0:T(8,128)(2,1)} %value_ref.1) | copy-start | bytes 884740
  6.5 28.8 %copy-start.3 = (bf16[384,384]{1,0:T(8,128)(2,1)S(1)}, bf16[384,384]{1,0:T(8,128)(2,1)}, u32[]{:S(2)}) copy-start(bf16[384,384]{1,0:T(8,128)(2,1)} %out_ref.1) | copy-start | bytes 884740
  10.2 34.4 %copy-start.6 = (bf16[3,3,384,192]{2,3,1,0:T(8,128)(2,1)S(1)}, bf16[3,3,384,192]{2,3,1,0:T(8,128)(2,1)}, u32[]{:S(2)}) copy-start(bf16[3,3,384,192]{2,3,1,0:T(8,128)(2,1)} %param.19) | copy-start | bytes 3981316
  11.0 1.4 %collective-permute-start.2 = (bf16[4,64,384]{2,1,0:T(8,128)(2,1)S(1)}, bf16[4,64,384]{2,1,0:T(8,128)(2,1)S(1)}, u32[]{:S(2)}, u32[]{:S(2)}) collective-permute-start(bf16[4,64,384]{2,1,0:T(8,128)(2,1)S(1)} %collective-permute-done.edge_ref), channel_id=1, source_target_pairs={{0,1},{1,0},{2,3},{3,2},{4,5},{5,4},{6,7},{7,6},{8,9},{9,8},{10,11... | collective-permute-start | bytes 589832 | tf_op jit(solution)/shard_map/ppermute | solution.py:510
  15.6 5.6 %collective-permute-start.3 = (bf16[144,384]{1,0:T(8,128)(2,1)S(1)}, bf16[144,384]{1,0:T(8,128)(2,1)S(1)}, u32[]{:S(2)}, u32[]{:S(2)}) collective-permute-start(bf16[144,384]{1,0:T(8,128)(2,1)S(1)} %get-tuple-element.38), channel_id=1, source_target_pairs={{0,4},{1,9},{2,6},{3,11},{4,12},{5,1},{6,14},{7,3},{8,0},{9,13},{1... | collective-permute-start | bytes 331784 | tf_op jit(solution)/shard_map/ppermute | solution.py:397
  18.7 7.1 %collective-permute-start.5 = (bf16[272,384]{1,0:T(8,128)(2,1)S(1)}, bf16[272,384]{1,0:T(8,128)(2,1)S(1)}, u32[]{:S(2)}, u32[]{:S(2)}) collective-permute-start(bf16[272,384]{1,0:T(8,128)(2,1)S(1)} %get-tuple-element.53.refs_0_), channel_id=1, source_target_pairs={{0,2},{1,3},{2,0},{3,1},{4,6},{5,7},{6,4},{7,5},{8,10},{9,11},{10,... | collective-permute-start | bytes 626696 | tf_op jit(solution)/shard_map/ppermute | solution.py:397
  20.2 5.6 %collective-permute-start.4 = (bf16[144,384]{1,0:T(8,128)(2,1)S(1)}, bf16[144,384]{1,0:T(8,128)(2,1)S(1)}, u32[]{:S(2)}, u32[]{:S(2)}) collective-permute-start(bf16[144,384]{1,0:T(8,128)(2,1)S(1)} %get-tuple-element.39), channel_id=1, source_target_pairs={{0,4},{1,9},{2,6},{3,11},{4,12},{5,1},{6,14},{7,3},{8,0},{9,13},{1... | collective-permute-start | bytes 331784 | tf_op jit(solution)/shard_map/ppermute | solution.py:397
  21.2 7.6 %collective-permute-start.6 = (bf16[144,384]{1,0:T(8,128)(2,1)S(1)}, bf16[144,384]{1,0:T(8,128)(2,1)S(1)}, u32[]{:S(2)}, u32[]{:S(2)}) collective-permute-start(bf16[144,384]{1,0:T(8,128)(2,1)S(1)} %collective-permute-done.3.refs_1_), channel_id=1, source_target_pairs={{0,4},{1,9},{2,6},{3,11},{4,12},{5,1},{6,14},{7,3},{8,0},{9,13},{1... | collective-permute-start | bytes 331784 | tf_op jit(solution)/shard_map/ppermute | solution.py:397
  24.1 4.7 %collective-permute-start.7 = (bf16[144,384]{1,0:T(8,128)(2,1)S(1)}, bf16[144,384]{1,0:T(8,128)(2,1)S(1)}, u32[]{:S(2)}, u32[]{:S(2)}) collective-permute-start(bf16[144,384]{1,0:T(8,128)(2,1)S(1)} %collective-permute-done.3.refs_1_), channel_id=1, source_target_pairs={{0,2},{1,3},{2,0},{3,1},{4,6},{5,7},{6,4},{7,5},{8,10},{9,11},{10,... | collective-permute-start | bytes 331784 | tf_op jit(solution)/shard_map/ppermute | solution.py:397
  25.8 4.7 %collective-permute-start.8 = (bf16[144,384]{1,0:T(8,128)(2,1)S(1)}, bf16[144,384]{1,0:T(8,128)(2,1)S(1)}, u32[]{:S(2)}, u32[]{:S(2)}) collective-permute-start(bf16[144,384]{1,0:T(8,128)(2,1)S(1)} %collective-permute-done.4.refs_2_), channel_id=1, source_target_pairs={{0,4},{1,9},{2,6},{3,11},{4,12},{5,1},{6,14},{7,3},{8,0},{9,13},{1... | collective-permute-start | bytes 331784 | tf_op jit(solution)/shard_map/ppermute | solution.py:397
  26.5 4.1 %collective-permute-start.9 = (bf16[144,384]{1,0:T(8,128)(2,1)S(1)}, bf16[144,384]{1,0:T(8,128)(2,1)S(1)}, u32[]{:S(2)}, u32[]{:S(2)}) collective-permute-start(bf16[144,384]{1,0:T(8,128)(2,1)S(1)} %collective-permute-done.4.refs_2_), channel_id=1, source_target_pairs={{0,2},{1,3},{2,0},{3,1},{4,6},{5,7},{6,4},{7,5},{8,10},{9,11},{10,... | collective-permute-start | bytes 331784 | tf_op jit(solution)/shard_map/ppermute | solution.py:397
  27.7 9.5 %collective-permute-start.12 = (bf16[272,384]{1,0:T(8,128)(2,1)S(1)}, bf16[272,384]{1,0:T(8,128)(2,1)S(1)}, u32[]{:S(2)}, u32[]{:S(2)}) collective-permute-start(bf16[272,384]{1,0:T(8,128)(2,1)S(1)} %get-tuple-element.53.refs_0_), channel_id=1, source_target_pairs={{0,8},{1,5},{2,10},{3,7},{4,0},{5,13},{6,2},{7,15},{8,12},{9,1},{1... | collective-permute-start | bytes 626696 | tf_op jit(solution)/shard_map/ppermute | solution.py:397
  28.7 8.9 %collective-permute-start.13 = (bf16[272,384]{1,0:T(8,128)(2,1)S(1)}, bf16[272,384]{1,0:T(8,128)(2,1)S(1)}, u32[]{:S(2)}, u32[]{:S(2)}) collective-permute-start(bf16[272,384]{1,0:T(8,128)(2,1)S(1)} %collective-permute-done.5.refs_7_), channel_id=1, source_target_pairs={{0,8},{1,5},{2,10},{3,7},{4,0},{5,13},{6,2},{7,15},{8,12},{9,1},{1... | collective-permute-start | bytes 626696 | tf_op jit(solution)/shard_map/ppermute | solution.py:397
  28.8 8.5 %collective-permute-start.10 = (bf16[144,384]{1,0:T(8,128)(2,1)S(1)}, bf16[144,384]{1,0:T(8,128)(2,1)S(1)}, u32[]{:S(2)}, u32[]{:S(2)}) collective-permute-start(bf16[144,384]{1,0:T(8,128)(2,1)S(1)} %collective-permute-done.6.refs_5_), channel_id=1, source_target_pairs={{0,2},{1,3},{2,0},{3,1},{4,6},{5,7},{6,4},{7,5},{8,10},{9,11},{10,... | collective-permute-start | bytes 331784 | tf_op jit(solution)/shard_map/ppermute | solution.py:397
  30.6 7.7 %collective-permute-start.11 = (bf16[144,384]{1,0:T(8,128)(2,1)S(1)}, bf16[144,384]{1,0:T(8,128)(2,1)S(1)}, u32[]{:S(2)}, u32[]{:S(2)}) collective-permute-start(bf16[144,384]{1,0:T(8,128)(2,1)S(1)} %collective-permute-done.8.refs_6_), channel_id=1, source_target_pairs={{0,2},{1,3},{2,0},{3,1},{4,6},{5,7},{6,4},{7,5},{8,10},{9,11},{10,... | collective-permute-start | bytes 331784 | tf_op jit(solution)/shard_map/ppermute | solution.py:397
  40.8 3.8 %collective-permute-start.14 = (bf16[256,384]{1,0:T(8,128)(2,1)S(1)}, bf16[256,384]{1,0:T(8,128)(2,1)S(1)}, u32[]{:S(2)}, u32[]{:S(2)}) collective-permute-start(bf16[256,384]{1,0:T(8,128)(2,1)S(1)} %get-tuple-element.56), channel_id=1, source_target_pairs={{0,1},{1,0},{2,3},{3,2},{4,5},{5,4},{6,7},{7,6},{8,9},{9,8},{10,11... | collective-permute-start | bytes 589832 | tf_op jit(solution)/shard_map/ppermute | solution.py:604

commit v2 on v1

--- a/solution.py
+++ b/solution.py
@@ -337,45 +337,48 @@
     swap_ref[...] = mid[pl.ds(pl.multiple_of(2 * (1 - core) * width, width), 4 * width), :]
 
 
-def up_kernel(width, mid_ref, swap_ref, weight_ref, out_ref, results, sems):
-    core = lax.axis_index("rows") % 2
-    channels = mid_ref.shape[1]
+def up_rows(width, ref, weight_ref, out):
+    channels = ref.shape[1]
     outputs = weight_ref.shape[2]
+    span = 4 * width
     wide = 2 * width
-    lane = lax.broadcasted_iota(jnp.int32, (1, wide), 1)
-    low = lax.broadcasted_iota(jnp.int32, (width, wide), 0)
-    spread = (lax.broadcasted_iota(jnp.int32, (width, wide), 1) // 2 == low).astype(BF16)
+    column = lax.broadcasted_iota(jnp.int32, (1, span), 1) % width
+    line = lax.broadcasted_iota(jnp.int32, (2 * wide, 2 * wide), 0)
+    lane = lax.broadcasted_iota(jnp.int32, (2 * wide, 2 * wide), 1)
+    target = 2 * (line % wide) + line // wide
+    weave = (target == lane).astype(BF16)
     lhs = jnp.concatenate(
         [weight_ref[j].reshape(3 * outputs, channels) for j in range(3)], axis=1
     )
-    stores = []
-    for slot, ref, frame in ((0, mid_ref, core), (1, swap_ref, 1 - core)):
-        rows = [
-            lax.dot_general(
-                ref[row * width : (row + 1) * width],
-                spread,
-                (((0,), (0,)), ((), ())),
-                preferred_element_type=F32,
-            ).astype(BF16)
-            for row in range(4)
-        ]
-        for phase in range(2):
-            pairs = [(0, 1, 1), (1, 2, 2)] if phase == 0 else [(1, 1, 2), (2, 2, 3)]
-            rhs = jnp.concatenate(
-                [jnp.concatenate([rows[p] for p in picks], axis=0) for picks in pairs], axis=1
-            )
-            taps = jnp.dot(lhs, rhs, preferred_element_type=F32)
-            for i in range(2):
-                left, middle, right = (
-                    taps[col * outputs : (col + 1) * outputs, i * wide : (i + 1) * wide]
-                    for col in range(3)
-                )
-                result = middle + jnp.where(lane == 0, 0.0, pltpu.roll(left, 1, axis=1))
-                result = result + jnp.where(
-                    lane == wide - 1, 0.0, pltpu.roll(right, wide - 1, axis=1)
-                )
-                results[slot, 2 * i + phase] = result.astype(BF16)
-        stores = stores + start_all([(results.at[slot], out_ref.at[frame])], sems, slot)
+    turned = jnp.transpose(ref[...].astype(F32)).astype(BF16)
+    rows = [turned[:, row * width : (row + 1) * width] for row in range(4)]
+    picks = ((0, 1, 1), (1, 1, 2), (1, 2, 2), (2, 2, 3))
+    rhs = jnp.concatenate(
+        [jnp.concatenate([rows[pick[j]] for pick in picks], axis=1) for j in range(3)], axis=0
+    )
+    taps = jnp.dot(lhs, rhs, preferred_element_type=F32)
+    left, middle, right = (taps[col * outputs : (col + 1) * outputs] for col in range(3))
+    even = middle + right + jnp.where(column == 0, 0.0, pltpu.roll(left, 1, axis=1))
+    odd = left + middle
+    odd = odd + jnp.where(column == width - 1, 0.0, pltpu.roll(right, span - 1, axis=1))
+    even, odd = even.astype(BF16), odd.astype(BF16)
+    for pair in range(2):
+        both = slice(pair * wide, (pair + 1) * wide)
+        mixed = jnp.concatenate([even[:, both], odd[:, both]], axis=1)
+        woven = jnp.dot(mixed, weave, preferred_element_type=F32).astype(BF16)
+        for i in range(2):
+            out[2 * pair + i] = woven[:, i * wide : (i + 1) * wide]
+
+
+def up_own_kernel(width, rows_ref, weight_ref, out_ref):
+    up_rows(width, rows_ref, weight_ref, out_ref)
+
+
+def up_kernel(width, rows_ref, weight_ref, own_ref, out_ref, result, sems):
+    core = lax.axis_index("rows") % 2
+    stores = start_all([(own_ref, out_ref.at[core])], sems)
+    up_rows(width, rows_ref, weight_ref, result)
+    stores = stores + start_all([(result, out_ref.at[1 - core])], sems, 1)
     wait_all(stores)
 
 
@@ -604,20 +607,28 @@
     swap_rows = lax.ppermute(swap_rows, "rows", swap)
 
     fine_shape = (2 * rows_here, outputs, 2 * width)
+    taps = jnp.transpose(up_weight, (0, 1, 3, 2))
+    up_cost = cost(2 * 9 * outputs * channels * 4 * width, 2 * 9 * outputs * channels)
+    own_fine = pl.pallas_call(
+        functools.partial(up_own_kernel, width),
+        out_shape=jax.ShapeDtypeStruct(fine_shape, BF16),
+        in_specs=[vmem()] * 2,
+        out_specs=vmem(),
+        cost_estimate=up_cost,
+        compiler_params=params(16),
+    )(mid, taps)
     decoded = pl.pallas_call(
         functools.partial(up_kernel, width),
         out_shape=jax.ShapeDtypeStruct((frames, *fine_shape), BF16),
         in_specs=[vmem()] * 3,
         out_specs=anywhere,
         scratch_shapes=[
-            pltpu.VMEM((2, *fine_shape), BF16),
+            pltpu.VMEM(fine_shape, BF16),
             pltpu.SemaphoreType.DMA((2,)),
         ],
-        cost_estimate=cost(
-            2 * 9 * outputs * channels * 16 * width, 2 * 9 * outputs * channels
-        ),
-        compiler_params=params(24),
-    )(mid, swap_rows, jnp.transpose(up_weight, (0, 1, 3, 2)))
+        cost_estimate=up_cost,
+        compiler_params=params(16),
+    )(swap_rows, taps, own_fine)
     decoded = jnp.transpose(decoded, (0, 1, 3, 2))
     return (decoded, act.reshape(frames, rows_here, width, channels))
 

time: 48 us -> 46.8 us (0.975)
  waiting for transfers between devices: 5.35 us -> 4.32 us
    pallas_call x1, Pallas kernels: 2.93 us -> 1.72 us  [shards(): pl.pallas_call(functools.partial(up_kernel, width), out_shape=jax.ShapeDt...]
    ppermute x1, waiting for transfers between devices: 1.07 us -> 0.04 us  [shards(): swap_rows = lax.ppermute(swap_rows, 'rows', swap)]
    pallas_call x0 -> x1, Pallas kernels: none -> 1.02 us  [shards(): pl.pallas_call(functools.partial(up_own_kernel, width), out_shape=jax.Sha...]
  transfers between devices with their start and end apart: 15 -> 15, of which waited for: 7 -> 6; matrix products, arithmetic and copies ran while one was open for 0% -> 0% of each run, Pallas kernels for 12% -> 15%
where the time goes in v2:
time: 46.8 us; the launch traced here: 46.3 us
  starting transfers between devices  25.9 us (55%)
  Pallas kernels  15.3 us (33%)
  waiting for transfers between devices  4.32 us (9%)
  between operations  0.78 us (2%)
    ppermute x11, starting transfers between devices, send(): return [lax.ppermute(part, 'rows', pairs) for part in parts]  18.6 us
    ppermute x1, starting transfers between devices, shards(): edge_rows = lax.ppermute(edge_rows, 'rows', neighbour)  4.54 us
    pallas_call x1, Pallas kernels, shards(): pl.pallas_call(prepare_kernel, out_shape=(jax.ShapeDtypeStruct((frames, o...  3.76 us
    pallas_call x1, Pallas kernels, shards(): pl.pallas_call(functools.partial(conv_kernel, width), out_shape=(block, h...  3.08 us
    ppermute x1, starting transfers between devices, shards(): swap_rows = lax.ppermute(swap_rows, 'rows', swap)  2.72 us
    pallas_call x1, Pallas kernels, shards(): pl.pallas_call(functools.partial(late_kernel, width, sources, counts, len...  2.57 us
    ppermute x11, waiting for transfers between devices, send(): return [lax.ppermute(part, 'rows', pairs) for part in parts]  2.04 us
    pallas_call x1, Pallas kernels, shards(): pl.pallas_call(functools.partial(up_kernel, width), out_shape=jax.ShapeDt...  1.72 us
  transfers between devices with their start and end apart: 15, of which 6 were waited for; matrix products, arithmetic and copies ran while one was open for 0% of the time, Pallas kernels for 15%

profile of v2, /device:TPU:1, one launch (start us, length us, event | category | flops | bytes accessed | tf_op | source)
XLA Modules:
  0.0 46.3 jit_solution(15086252512069722789)
XLA Ops:
  0.7 1.1 %shard_map.114 = (bf16[4,64,384]{2,1,0:T(8,128)(2,1)S(1)}, bf16[3,2,64,384]{3,2,1,0:T(8,128)(2,1)S(1)}) custom-call(bf16[2,2,64,384]{3,2,1,0:T(8,128)(2,1)} %latents_ref.1, bf16[2,2,64,384]{3,2,1,0:T(8,128)(2,1)} %cache_ref.1), custom_call_target="tpu_custom_call" | custom-call | bytes 491520 | tf_op jit(solution)/shard_map/pallas_call | solution.py:473
  1.8 4.5 %collective-permute-start = (bf16[4,64,384]{2,1,0:T(8,128)(2,1)S(1)}, bf16[4,64,384]{2,1,0:T(8,128)(2,1)S(1)}, u32[]{:S(2)}, u32[]{:S(2)}) collective-permute-start(bf16[4,64,384]{2,1,0:T(8,128)(2,1)S(1)} %get-tuple-element.31), channel_id=1, source_target_pairs={{1,2},{3,4},{5,6},{7,8},{9,10},{11,12},{13,14},{2,1},{4,3},{6,5},{... | collective-permute-start | bytes 589832 | tf_op jit(solution)/shard_map/ppermute | solution.py:485
  6.5 3.8 %shard_map.115 = (bf16[2,128,384]{2,1,0:T(8,128)(2,1)}, bf16[3,128,384]{2,1,0:T(8,128)(2,1)S(1)}, bf16[3,3,384,1152]{3,2,1,0:T(8,128)(2,1)S(1)}) custom-call(bf16[2,128,384]{2,1,0:T(8,128)(2,1)} %bitcast.9, bf16[2,128,384]{2,1,0:T(8,128)(2,1)} %bitcast.10, bf16[3,3,3,384,384]{4,3,2,1,0:T(8,128)(2,1)} %weight_ref.1, f32[384]{0:T(512)} %norm_gain_ref.1), custom_call_target="tpu_custom_call" | custom-call | flops 983040 | bytes 7962624 | tf_op jit(solution)/shard_map/pallas_call | solution.py:487
  10.3 0.8 %collective-permute-done.edge_ref = bf16[4,64,384]{2,1,0:T(8,128)(2,1)S(1)} collective-permute-done((bf16[4,64,384]{2,1,0:T(8,128)(2,1)S(1)}, bf16[4,64,384]{2,1,0:T(8,128)(2,1)S(1)}, u32[]{:S(2)}, u32[]{:S(2)}) %collective-permute-start) | collective-permute-done | bytes 196640 | tf_op jit(solution)/shard_map/ppermute | solution.py:485
  11.1 1.4 %collective-permute-done.2.far_ref = bf16[4,64,384]{2,1,0:T(8,128)(2,1)S(1)} collective-permute-done((bf16[4,64,384]{2,1,0:T(8,128)(2,1)S(1)}, bf16[4,64,384]{2,1,0:T(8,128)(2,1)S(1)}, u32[]{:S(2)}, u32[]{:S(2)}) %collective-permute-start.2) | collective-permute-done | bytes 196640 | tf_op jit(solution)/shard_map/ppermute | solution.py:513
  12.5 3.1 %shard_map.116 = (bf16[272,384]{1,0:T(8,128)(2,1)S(1)}, bf16[144,384]{1,0:T(8,128)(2,1)S(1)}, bf16[144,384]{1,0:T(8,128)(2,1)S(1)}, f32[256,384]{1,0:T(8,128)S(1)}) custom-call(bf16[3,128,384]{2,1,0:T(8,128)(2,1)S(1)} %get-tuple-element.33.own_ref, bf16[3,128,384]{2,1,0:T(8,128)(2,1)S(1)} %bitcast.8, bf16[4,64,384]{2,1,0:T(8,128)(2,1)S(1)} %collective-permute-done.edge_ref, ...), custom_call_target="tpu_custom_call" | custom-call | flops 2038431744 | bytes 7962624 | tf_op jit(solution)/shard_map/pallas_call | solution.py:516
  15.6 3.1 %collective-permute-start.3 = (bf16[144,384]{1,0:T(8,128)(2,1)S(1)}, bf16[144,384]{1,0:T(8,128)(2,1)S(1)}, u32[]{:S(2)}, u32[]{:S(2)}) collective-permute-start(bf16[144,384]{1,0:T(8,128)(2,1)S(1)} %get-tuple-element.38), channel_id=1, source_target_pairs={{0,4},{1,9},{2,6},{3,11},{4,12},{5,1},{6,14},{7,3},{8,0},{9,13},{1... | collective-permute-start | bytes 331784 | tf_op jit(solution)/shard_map/ppermute | solution.py:400
  18.7 1.5 %collective-permute-start.5 = (bf16[272,384]{1,0:T(8,128)(2,1)S(1)}, bf16[272,384]{1,0:T(8,128)(2,1)S(1)}, u32[]{:S(2)}, u32[]{:S(2)}) collective-permute-start(bf16[272,384]{1,0:T(8,128)(2,1)S(1)} %get-tuple-element.53.refs_0_), channel_id=1, source_target_pairs={{0,2},{1,3},{2,0},{3,1},{4,6},{5,7},{6,4},{7,5},{8,10},{9,11},{10,... | collective-permute-start | bytes 626696 | tf_op jit(solution)/shard_map/ppermute | solution.py:400
  20.2 0.9 %collective-permute-done.3.refs_1_ = bf16[144,384]{1,0:T(8,128)(2,1)S(1)} collective-permute-done((bf16[144,384]{1,0:T(8,128)(2,1)S(1)}, bf16[144,384]{1,0:T(8,128)(2,1)S(1)}, u32[]{:S(2)}, u32[]{:S(2)}) %collective-permute-start.3) | collective-permute-done | bytes 110624 | tf_op jit(solution)/shard_map/ppermute | solution.py:400
  21.2 2.9 %collective-permute-start.6 = (bf16[144,384]{1,0:T(8,128)(2,1)S(1)}, bf16[144,384]{1,0:T(8,128)(2,1)S(1)}, u32[]{:S(2)}, u32[]{:S(2)}) collective-permute-start(bf16[144,384]{1,0:T(8,128)(2,1)S(1)} %collective-permute-done.3.refs_1_), channel_id=1, source_target_pairs={{0,4},{1,9},{2,6},{3,11},{4,12},{5,1},{6,14},{7,3},{8,0},{9,13},{1... | collective-permute-start | bytes 331784 | tf_op jit(solution)/shard_map/ppermute | solution.py:400
  24.1 1.7 %collective-permute-start.7 = (bf16[144,384]{1,0:T(8,128)(2,1)S(1)}, bf16[144,384]{1,0:T(8,128)(2,1)S(1)}, u32[]{:S(2)}, u32[]{:S(2)}) collective-permute-start(bf16[144,384]{1,0:T(8,128)(2,1)S(1)} %collective-permute-done.3.refs_1_), channel_id=1, source_target_pairs={{0,2},{1,3},{2,0},{3,1},{4,6},{5,7},{6,4},{7,5},{8,10},{9,11},{10,... | collective-permute-start | bytes 331784 | tf_op jit(solution)/shard_map/ppermute | solution.py:400
  25.8 0.7 %collective-permute-start.8 = (bf16[144,384]{1,0:T(8,128)(2,1)S(1)}, bf16[144,384]{1,0:T(8,128)(2,1)S(1)}, u32[]{:S(2)}, u32[]{:S(2)}) collective-permute-start(bf16[144,384]{1,0:T(8,128)(2,1)S(1)} %collective-permute-done.4.refs_2_), channel_id=1, source_target_pairs={{0,4},{1,9},{2,6},{3,11},{4,12},{5,1},{6,14},{7,3},{8,0},{9,13},{1... | collective-permute-start | bytes 331784 | tf_op jit(solution)/shard_map/ppermute | solution.py:400
  26.5 1.2 %collective-permute-start.9 = (bf16[144,384]{1,0:T(8,128)(2,1)S(1)}, bf16[144,384]{1,0:T(8,128)(2,1)S(1)}, u32[]{:S(2)}, u32[]{:S(2)}) collective-permute-start(bf16[144,384]{1,0:T(8,128)(2,1)S(1)} %collective-permute-done.4.refs_2_), channel_id=1, source_target_pairs={{0,2},{1,3},{2,0},{3,1},{4,6},{5,7},{6,4},{7,5},{8,10},{9,11},{10,... | collective-permute-start | bytes 331784 | tf_op jit(solution)/shard_map/ppermute | solution.py:400
  27.7 1.0 %collective-permute-start.12 = (bf16[272,384]{1,0:T(8,128)(2,1)S(1)}, bf16[272,384]{1,0:T(8,128)(2,1)S(1)}, u32[]{:S(2)}, u32[]{:S(2)}) collective-permute-start(bf16[272,384]{1,0:T(8,128)(2,1)S(1)} %get-tuple-element.53.refs_0_), channel_id=1, source_target_pairs={{0,8},{1,5},{2,10},{3,7},{4,0},{5,13},{6,2},{7,15},{8,12},{9,1},{1... | collective-permute-start | bytes 626696 | tf_op jit(solution)/shard_map/ppermute | solution.py:400
  28.8 1.6 %collective-permute-start.10 = (bf16[144,384]{1,0:T(8,128)(2,1)S(1)}, bf16[144,384]{1,0:T(8,128)(2,1)S(1)}, u32[]{:S(2)}, u32[]{:S(2)}) collective-permute-start(bf16[144,384]{1,0:T(8,128)(2,1)S(1)} %collective-permute-done.6.refs_5_), channel_id=1, source_target_pairs={{0,2},{1,3},{2,0},{3,1},{4,6},{5,7},{6,4},{7,5},{8,10},{9,11},{10,... | collective-permute-start | bytes 331784 | tf_op jit(solution)/shard_map/ppermute | solution.py:400
  30.6 4.7 %collective-permute-start.11 = (bf16[144,384]{1,0:T(8,128)(2,1)S(1)}, bf16[144,384]{1,0:T(8,128)(2,1)S(1)}, u32[]{:S(2)}, u32[]{:S(2)}) collective-permute-start(bf16[144,384]{1,0:T(8,128)(2,1)S(1)} %collective-permute-done.8.refs_6_), channel_id=1, source_target_pairs={{0,2},{1,3},{2,0},{3,1},{4,6},{5,7},{6,4},{7,5},{8,10},{9,11},{10,... | collective-permute-start | bytes 331784 | tf_op jit(solution)/shard_map/ppermute | solution.py:400
  35.3 0.5 %shard_map.113 = (bf16[384,384]{1,0:T(8,128)(2,1)S(1)}, bf16[384,384]{1,0:T(8,128)(2,1)S(1)}) custom-call(bf16[384,384]{1,0:T(8,128)(2,1)S(1)} %copy-done.1, bf16[384,384]{1,0:T(8,128)(2,1)S(1)} %copy-done.2, bf16[384,384]{1,0:T(8,128)(2,1)S(1)} %copy-done.3, bf16[384,384]{1,0:T(8,128)(2,1)S(1)} %copy-done.4), custom_call_target="tpu_custom_call" | custom-call | flops 226492416 | bytes 1769472 | tf_op jit(solution)/shard_map/pallas_call | solution.py:548
  35.8 1.4 %shard_map.117 = (bf16[256,384]{1,0:T(8,128)(2,1)S(1)}, f32[256,128]{1,0:T(8,128)S(1)}, f32[256,128]{1,0:T(8,128)S(1)}, f32[256,384]{1,0:T(8,128)S(1)}) custom-call(bf16[384,384]{1,0:T(8,128)(2,1)S(1)} %get-tuple-element.30.score_ref, bf16[272,384]{1,0:T(8,128)(2,1)S(1)} %get-tuple-element.53.refs_0_, bf16[144,384]{1,0:T(8,128)(2,1)S(1)} %collective-permute-done.3.refs_1_, ...), custom_call_target="tpu_custom_call" | custom-call | flops 503316480 | bytes 983040 | tf_op jit(solution)/shard_map/pallas_call | solution.py:559
  37.3 0.3 collective-permute-done.13.refs_11_
  37.6 0.7 %collective-permute-done.11.refs_9_ = bf16[144,384]{1,0:T(8,128)(2,1)S(1)} collective-permute-done((bf16[144,384]{1,0:T(8,128)(2,1)S(1)}, bf16[144,384]{1,0:T(8,128)(2,1)S(1)}, u32[]{:S(2)}, u32[]{:S(2)}) %collective-permute-start.11) | collective-permute-done | bytes 110624 | tf_op jit(solution)/shard_map/ppermute | solution.py:400
  38.2 2.6 %shard_map.118 = (bf16[256,384]{1,0:T(8,128)(2,1)S(1)}, bf16[256,384]{1,0:T(8,128)(2,1)S(1)}) custom-call(bf16[256,384]{1,0:T(8,128)(2,1)S(1)} %get-tuple-element.47.own_query_ref, f32[256,128]{1,0:T(8,128)S(1)} %get-tuple-element.48.peak_ref, f32[256,128]{1,0:T(8,128)S(1)} %get-tuple-element.49.sums_ref, f32[256,384]{1,0:T(8,128)S(1)} %get-tuple-element.50.added_ref, ...), custom_call_target="tpu_custom_call" | custom-call | flops 603979776 | bytes 1572864 | tf_op jit(solution)/shard_map/pallas_call | solution.py:578
  40.8 2.7 %collective-permute-start.14 = (bf16[256,384]{1,0:T(8,128)(2,1)S(1)}, bf16[256,384]{1,0:T(8,128)(2,1)S(1)}, u32[]{:S(2)}, u32[]{:S(2)}) collective-permute-start(bf16[256,384]{1,0:T(8,128)(2,1)S(1)} %get-tuple-element.55), channel_id=1, source_target_pairs={{0,1},{1,0},{2,3},{3,2},{4,5},{5,4},{6,7},{7,6},{8,9},{9,8},{10,11... | collective-permute-start | bytes 589832 | tf_op jit(solution)/shard_map/ppermute | solution.py:607
  43.5 1.0 %shard_map.119.own_ref = bf16[4,192,128]{2,1,0:T(8,128)(2,1)S(1)} custom-call(bf16[256,384]{1,0:T(8,128)(2,1)S(1)} %get-tuple-element.56.rows_ref, bf16[3,3,192,384]{3,2,1,0:T(8,128)(2,1)S(1)} %bitcast.6), custom_call_target="tpu_custom_call" | custom-call | flops 339738624 | bytes 1327104 | tf_op jit(solution)/shard_map/pallas_call | solution.py:612
  44.6 1.7 %shard_map.120 = bf16[2,4,192,128]{3,2,1,0:T(8,128)(2,1)} custom-call(bf16[256,384]{1,0:T(8,128)(2,1)S(1)} %collective-permute-done.14.rows_ref, bf16[3,3,192,384]{3,2,1,0:T(8,128)(2,1)S(1)} %bitcast.7, bf16[4,192,128]{2,1,0:T(8,128)(2,1)S(1)} %shard_map.119.own_ref), custom_call_target="tpu_custom_call" | custom-call | flops 339738624 | bytes 1327104 | tf_op jit(solution)/shard_map/pallas_call | solution.py:620
  (28 shorter events, 0.4 us)
Async XLA Ops:
  0.6 11.9 %copy-start.5 = (f32[384]{0:T(512)S(1)}, f32[384]{0:T(512)}, u32[]{:S(2)}) copy-start(f32[384]{0:T(512)} %norm_gain_ref.1) | copy-start | bytes 4612
  0.6 11.9 %copy-start.6 = (f32[384]{0:T(512)S(1)}, f32[384]{0:T(512)}, u32[]{:S(2)}) copy-start(f32[384]{0:T(512)} %gain_ref.3) | copy-start | bytes 4612
  1.8 9.2 %collective-permute-start = (bf16[4,64,384]{2,1,0:T(8,128)(2,1)S(1)}, bf16[4,64,384]{2,1,0:T(8,128)(2,1)S(1)}, u32[]{:S(2)}, u32[]{:S(2)}) collective-permute-start(bf16[4,64,384]{2,1,0:T(8,128)(2,1)S(1)} %get-tuple-element.31), channel_id=1, source_target_pairs={{1,2},{3,4},{5,6},{7,8},{9,10},{11,12},{13,14},{2,1},{4,3},{6,5},{... | collective-permute-start | bytes 589832 | tf_op jit(solution)/shard_map/ppermute | solution.py:485
  6.3 4.7 %collective-permute-start.1 = (bf16[3,2,64,384]{3,2,1,0:T(8,128)(2,1)S(1)}, bf16[3,2,64,384]{3,2,1,0:T(8,128)(2,1)S(1)}, u32[]{:S(2)}, u32[]{:S(2)}) collective-permute-start(bf16[3,2,64,384]{3,2,1,0:T(8,128)(2,1)S(1)} %get-tuple-element.34), channel_id=1, source_target_pairs={{0,1},{1,0},{2,3},{3,2},{4,5},{5,4},{6,7},{7,6},{8,9},{9,8},{10,11... | collective-permute-start | bytes 884744 | tf_op jit(solution)/shard_map/ppermute | solution.py:486
  6.4 28.8 %copy-start.1 = (bf16[384,384]{1,0:T(8,128)(2,1)S(1)}, bf16[384,384]{1,0:T(8,128)(2,1)}, u32[]{:S(2)}) copy-start(bf16[384,384]{1,0:T(8,128)(2,1)} %query_ref.1) | copy-start | bytes 884740
  6.4 28.8 %copy-start.2 = (bf16[384,384]{1,0:T(8,128)(2,1)S(1)}, bf16[384,384]{1,0:T(8,128)(2,1)}, u32[]{:S(2)}) copy-start(bf16[384,384]{1,0:T(8,128)(2,1)} %key_ref.1) | copy-start | bytes 884740
  6.5 28.8 %copy-start.3 = (bf16[384,384]{1,0:T(8,128)(2,1)S(1)}, bf16[384,384]{1,0:T(8,128)(2,1)}, u32[]{:S(2)}) copy-start(bf16[384,384]{1,0:T(8,128)(2,1)} %value_ref.1) | copy-start | bytes 884740
  6.5 28.8 %copy-start.4 = (bf16[384,384]{1,0:T(8,128)(2,1)S(1)}, bf16[384,384]{1,0:T(8,128)(2,1)}, u32[]{:S(2)}) copy-start(bf16[384,384]{1,0:T(8,128)(2,1)} %out_ref.1) | copy-start | bytes 884740
  10.2 33.3 %copy-start = (bf16[3,3,384,192]{2,3,1,0:T(8,128)(2,1)S(1)}, bf16[3,3,384,192]{2,3,1,0:T(8,128)(2,1)}, u32[]{:S(2)}) copy-start(bf16[3,3,384,192]{2,3,1,0:T(8,128)(2,1)} %param.19) | copy-start | bytes 3981316
  11.0 1.4 %collective-permute-start.2 = (bf16[4,64,384]{2,1,0:T(8,128)(2,1)S(1)}, bf16[4,64,384]{2,1,0:T(8,128)(2,1)S(1)}, u32[]{:S(2)}, u32[]{:S(2)}) collective-permute-start(bf16[4,64,384]{2,1,0:T(8,128)(2,1)S(1)} %collective-permute-done.edge_ref), channel_id=1, source_target_pairs={{0,1},{1,0},{2,3},{3,2},{4,5},{5,4},{6,7},{7,6},{8,9},{9,8},{10,11... | collective-permute-start | bytes 589832 | tf_op jit(solution)/shard_map/ppermute | solution.py:513
  15.6 5.6 %collective-permute-start.3 = (bf16[144,384]{1,0:T(8,128)(2,1)S(1)}, bf16[144,384]{1,0:T(8,128)(2,1)S(1)}, u32[]{:S(2)}, u32[]{:S(2)}) collective-permute-start(bf16[144,384]{1,0:T(8,128)(2,1)S(1)} %get-tuple-element.38), channel_id=1, source_target_pairs={{0,4},{1,9},{2,6},{3,11},{4,12},{5,1},{6,14},{7,3},{8,0},{9,13},{1... | collective-permute-start | bytes 331784 | tf_op jit(solution)/shard_map/ppermute | solution.py:400
  18.7 7.1 %collective-permute-start.5 = (bf16[272,384]{1,0:T(8,128)(2,1)S(1)}, bf16[272,384]{1,0:T(8,128)(2,1)S(1)}, u32[]{:S(2)}, u32[]{:S(2)}) collective-permute-start(bf16[272,384]{1,0:T(8,128)(2,1)S(1)} %get-tuple-element.53.refs_0_), channel_id=1, source_target_pairs={{0,2},{1,3},{2,0},{3,1},{4,6},{5,7},{6,4},{7,5},{8,10},{9,11},{10,... | collective-permute-start | bytes 626696 | tf_op jit(solution)/shard_map/ppermute | solution.py:400
  20.2 5.6 %collective-permute-start.4 = (bf16[144,384]{1,0:T(8,128)(2,1)S(1)}, bf16[144,384]{1,0:T(8,128)(2,1)S(1)}, u32[]{:S(2)}, u32[]{:S(2)}) collective-permute-start(bf16[144,384]{1,0:T(8,128)(2,1)S(1)} %get-tuple-element.39), channel_id=1, source_target_pairs={{0,4},{1,9},{2,6},{3,11},{4,12},{5,1},{6,14},{7,3},{8,0},{9,13},{1... | collective-permute-start | bytes 331784 | tf_op jit(solution)/shard_map/ppermute | solution.py:400
  21.2 7.6 %collective-permute-start.6 = (bf16[144,384]{1,0:T(8,128)(2,1)S(1)}, bf16[144,384]{1,0:T(8,128)(2,1)S(1)}, u32[]{:S(2)}, u32[]{:S(2)}) collective-permute-start(bf16[144,384]{1,0:T(8,128)(2,1)S(1)} %collective-permute-done.3.refs_1_), channel_id=1, source_target_pairs={{0,4},{1,9},{2,6},{3,11},{4,12},{5,1},{6,14},{7,3},{8,0},{9,13},{1... | collective-permute-start | bytes 331784 | tf_op jit(solution)/shard_map/ppermute | solution.py:400
  24.1 4.7 %collective-permute-start.7 = (bf16[144,384]{1,0:T(8,128)(2,1)S(1)}, bf16[144,384]{1,0:T(8,128)(2,1)S(1)}, u32[]{:S(2)}, u32[]{:S(2)}) collective-permute-start(bf16[144,384]{1,0:T(8,128)(2,1)S(1)} %collective-permute-done.3.refs_1_), channel_id=1, source_target_pairs={{0,2},{1,3},{2,0},{3,1},{4,6},{5,7},{6,4},{7,5},{8,10},{9,11},{10,... | collective-permute-start | bytes 331784 | tf_op jit(solution)/shard_map/ppermute | solution.py:400
  25.8 4.7 %collective-permute-start.8 = (bf16[144,384]{1,0:T(8,128)(2,1)S(1)}, bf16[144,384]{1,0:T(8,128)(2,1)S(1)}, u32[]{:S(2)}, u32[]{:S(2)}) collective-permute-start(bf16[144,384]{1,0:T(8,128)(2,1)S(1)} %collective-permute-done.4.refs_2_), channel_id=1, source_target_pairs={{0,4},{1,9},{2,6},{3,11},{4,12},{5,1},{6,14},{7,3},{8,0},{9,13},{1... | collective-permute-start | bytes 331784 | tf_op jit(solution)/shard_map/ppermute | solution.py:400
  26.5 4.1 %collective-permute-start.9 = (bf16[144,384]{1,0:T(8,128)(2,1)S(1)}, bf16[144,384]{1,0:T(8,128)(2,1)S(1)}, u32[]{:S(2)}, u32[]{:S(2)}) collective-permute-start(bf16[144,384]{1,0:T(8,128)(2,1)S(1)} %collective-permute-done.4.refs_2_), channel_id=1, source_target_pairs={{0,2},{1,3},{2,0},{3,1},{4,6},{5,7},{6,4},{7,5},{8,10},{9,11},{10,... | collective-permute-start | bytes 331784 | tf_op jit(solution)/shard_map/ppermute | solution.py:400
  27.7 9.5 %collective-permute-start.12 = (bf16[272,384]{1,0:T(8,128)(2,1)S(1)}, bf16[272,384]{1,0:T(8,128)(2,1)S(1)}, u32[]{:S(2)}, u32[]{:S(2)}) collective-permute-start(bf16[272,384]{1,0:T(8,128)(2,1)S(1)} %get-tuple-element.53.refs_0_), channel_id=1, source_target_pairs={{0,8},{1,5},{2,10},{3,7},{4,0},{5,13},{6,2},{7,15},{8,12},{9,1},{1... | collective-permute-start | bytes 626696 | tf_op jit(solution)/shard_map/ppermute | solution.py:400
  28.7 8.9 %collective-permute-start.13 = (bf16[272,384]{1,0:T(8,128)(2,1)S(1)}, bf16[272,384]{1,0:T(8,128)(2,1)S(1)}, u32[]{:S(2)}, u32[]{:S(2)}) collective-permute-start(bf16[272,384]{1,0:T(8,128)(2,1)S(1)} %collective-permute-done.5.refs_7_), channel_id=1, source_target_pairs={{0,8},{1,5},{2,10},{3,7},{4,0},{5,13},{6,2},{7,15},{8,12},{9,1},{1... | collective-permute-start | bytes 626696 | tf_op jit(solution)/shard_map/ppermute | solution.py:400
  28.8 8.5 %collective-permute-start.10 = (bf16[144,384]{1,0:T(8,128)(2,1)S(1)}, bf16[144,384]{1,0:T(8,128)(2,1)S(1)}, u32[]{:S(2)}, u32[]{:S(2)}) collective-permute-start(bf16[144,384]{1,0:T(8,128)(2,1)S(1)} %collective-permute-done.6.refs_5_), channel_id=1, source_target_pairs={{0,2},{1,3},{2,0},{3,1},{4,6},{5,7},{6,4},{7,5},{8,10},{9,11},{10,... | collective-permute-start | bytes 331784 | tf_op jit(solution)/shard_map/ppermute | solution.py:400
  30.6 7.7 %collective-permute-start.11 = (bf16[144,384]{1,0:T(8,128)(2,1)S(1)}, bf16[144,384]{1,0:T(8,128)(2,1)S(1)}, u32[]{:S(2)}, u32[]{:S(2)}) collective-permute-start(bf16[144,384]{1,0:T(8,128)(2,1)S(1)} %collective-permute-done.8.refs_6_), channel_id=1, source_target_pairs={{0,2},{1,3},{2,0},{3,1},{4,6},{5,7},{6,4},{7,5},{8,10},{9,11},{10,... | collective-permute-start | bytes 331784 | tf_op jit(solution)/shard_map/ppermute | solution.py:400
  40.8 3.8 %collective-permute-start.14 = (bf16[256,384]{1,0:T(8,128)(2,1)S(1)}, bf16[256,384]{1,0:T(8,128)(2,1)S(1)}, u32[]{:S(2)}, u32[]{:S(2)}) collective-permute-start(bf16[256,384]{1,0:T(8,128)(2,1)S(1)} %get-tuple-element.55), channel_id=1, source_target_pairs={{0,1},{1,0},{2,3},{3,2},{4,5},{5,4},{6,7},{7,6},{8,9},{9,8},{10,11... | collective-permute-start | bytes 589832 | tf_op jit(solution)/shard_map/ppermute | solution.py:607

commit v3 on v2

--- a/solution.py
+++ b/solution.py
@@ -11,7 +11,6 @@
 F32 = jnp.float32
 EPS = 1e-06
 MIB = 1024 * 1024
-EXTRA = 16
 
 
 def normalize(values, gain):
@@ -123,7 +122,6 @@
     edge_ref,
     far_ref,
     norm_gain_ref,
-    attn_gain_ref,
     weights,
     sent_ref,
     front_ref,
@@ -168,27 +166,23 @@
     conv_out = conv_out + jnp.where(column == width - 1, 0.0, right)
     resid = raw[2, width : width + span].astype(F32) + conv_out
     resid_ref[...] = resid
-    size = jnp.mean(resid * resid, axis=-1, keepdims=True) + EPS
-    normed = resid * lax.rsqrt(size) * attn_gain_ref[...].reshape(1, channels)
-    edges = jnp.sqrt(jnp.concatenate([size[:width], size[span - width :]], axis=0))
-    across = jnp.transpose(jnp.broadcast_to(edges, (2 * width, 128)))[:EXTRA]
-    high = across.astype(BF16).astype(F32)
-    line = lax.broadcasted_iota(jnp.int32, (EXTRA, 1), 0)
-    extra = jnp.where(line == 0, high, jnp.where(line == 1, across - high, 0.0)).astype(BF16)
-    half = span // 2
-    for ref, low, count in ((sent_ref, 0, span), (front_ref, 0, half), (back_ref, half, half)):
-        ref[:count] = normed[low : low + count].astype(BF16)
-        ref[count:] = jnp.zeros((EXTRA, channels), BF16)
-        ref[count:, : 2 * width] = extra
+    rounded = resid.astype(BF16)
+    sent_ref[...] = rounded
+    front_ref[...] = rounded[: span // 2]
+    back_ref[...] = rounded[span // 2 :]
 
 
 def nt_dot(a, b):
     return lax.dot_general(a, b, (((1,), (1,)), ((), ())), preferred_element_type=F32)
 
 
-def whole(parts):
-    rows = [part[: part.shape[0] - EXTRA] for part in parts]
-    return rows[0] if len(rows) == 1 else jnp.concatenate(rows, axis=0)
+def normed(rows, gain):
+    return normalize(rows.astype(F32), gain).astype(BF16)
+
+
+def whole(parts, gain):
+    rows = [part[...] for part in parts]
+    return normed(rows[0] if len(rows) == 1 else jnp.concatenate(rows, axis=0), gain)
 
 
 def grouped(refs, counts):
@@ -238,10 +232,13 @@
     return jnp.dot(rows, score_weight[...], preferred_element_type=F32).astype(BF16)
 
 
-def early_kernel(counts, score_ref, *refs):
+def early_kernel(counts, score_ref, gain_ref, *refs):
     blocks = grouped(refs, counts)
-    own_query_ref, peak_ref, sums_ref, added_ref, scores = refs[-5:]
-    keys = [whole(parts) for parts in blocks]
+    own_query_ref, peak_ref, sums_ref, added_ref, keys_ref, scores = refs[-6:]
+    gain = gain_ref[...].reshape(1, score_ref.shape[0])
+    keys = [whole(parts, gain) for parts in blocks]
+    for i, key in enumerate(keys):
+        keys_ref[i] = key
     queries = lead(keys[0], score_ref)
     own_query_ref[...] = queries
     peak, sums, added = attend(queries, keys, scores, 0, None, None, None)
@@ -259,6 +256,7 @@
     peak_ref,
     sums_ref,
     added_ref,
+    keys_ref,
     resid_ref,
     gain_ref,
     score_ref,
@@ -266,7 +264,7 @@
     *refs,
 ):
     blocks = grouped(refs, counts)
-    mid_ref, swap_ref, scores, mid, halo, sizes = refs[sum(counts) :]
+    mid_ref, swap_ref, scores, mid, halo = refs[sum(counts) :]
     place = lax.axis_index("rows")
     core = place % 2
     chip = place // 2
@@ -275,8 +273,7 @@
 
     for block, origin in zip(blocks, sources):
         for step, part, low in ((-1, block[-1], 0), (1, block[0], width)):
-            rows = part.shape[0] - EXTRA
-            first = rows - width if step < 0 else 0
+            first = part.shape[0] - width if step < 0 else 0
             takers = [d for d in range(devices) if origin[d] == d // 2 + step]
             if not takers:
                 continue
@@ -285,9 +282,8 @@
                 wanted = jnp.logical_or(wanted, place == d)
 
             @pl.when(wanted)
-            def _(part=part, rows=rows, first=first, low=low):
+            def _(part=part, first=first, low=low):
                 halo[low : low + width] = part[first : first + width, :]
-                sizes[low // width] = part[rows : rows + EXTRA, : 2 * width]
 
     no_above = chip == 0
     no_below = chip == devices // 2 - 1
@@ -295,23 +291,16 @@
     @pl.when(no_above)
     def _():
         halo[:width] = jnp.zeros((width, channels), BF16)
-        sizes[0] = jnp.zeros((EXTRA, 2 * width), BF16)
 
     @pl.when(no_below)
     def _():
         halo[width:] = jnp.zeros((width, channels), BF16)
-        sizes[1] = jnp.zeros((EXTRA, 2 * width), BF16)
-
-    def column(index):
-        parts = sizes[index].astype(F32)
-        line = parts[0:1] + parts[1:2]
-        return jnp.transpose(jnp.broadcast_to(line, (128, 2 * width)))[:, :1]
-
-    edge_rows = halo[...]
-    edge_size = jnp.concatenate([column(0)[width:], column(1)[:width]], axis=0)
-    edge_resid = edge_rows.astype(F32) * edge_size / gain_ref[...].reshape(1, channels)
-    edge_query = lead(edge_rows, score_ref)
-    keys = [whole(parts) for parts in blocks]
+
+    gain = gain_ref[...].reshape(1, channels)
+    edge_resid = halo[...].astype(F32)
+    edge_query = lead(normed(edge_resid, gain), score_ref)
+    keys = [keys_ref[i] for i in range(early)]
+    keys = keys + [whole(parts, gain) for parts in blocks[early:]]
     _, edge_sums, edge_added = attend(edge_query, keys, scores, own, None, None, None)
     _, own_sums, own_added = attend(
         own_query_ref[...],
@@ -412,7 +401,7 @@
     own_again = [block]
     crossed = last = None
     if depth == 2:
-        crossed = send([block], across)
+        crossed = send(halves, across)
     steps = length - 2
     parts, origin = list(halves), here
     for step in range(1, steps + 1):
@@ -511,12 +500,12 @@
 
     edge_rows, own_rows = lax.optimization_barrier((edge_rows, own_rows))
     far_rows = lax.ppermute(edge_rows, "rows", swap)
-    block = jax.ShapeDtypeStruct((span + EXTRA, channels), BF16)
-    half = jax.ShapeDtypeStruct((span // 2 + EXTRA, channels), BF16)
+    block = jax.ShapeDtypeStruct((span, channels), BF16)
+    half = jax.ShapeDtypeStruct((span // 2, channels), BF16)
     sent, front, back, resid = pl.pallas_call(
         functools.partial(conv_kernel, width),
         out_shape=(block, half, half, jax.ShapeDtypeStruct((span, channels), F32)),
-        in_specs=[vmem()] * 7,
+        in_specs=[vmem()] * 6,
         out_specs=(vmem(),) * 4,
         scratch_shapes=[
             pltpu.VMEM((3, 6 * width, channels), BF16),
@@ -532,7 +521,6 @@
         edge_rows,
         far_rows,
         norm_gain,
-        attn_gain,
         staged,
     )
 
@@ -556,16 +544,17 @@
 
     wide = span + 2 * width
     lanes = jax.ShapeDtypeStruct((span, 128), F32)
-    own_query, peak, sums, added = pl.pallas_call(
+    own_query, peak, sums, added, early_keys = pl.pallas_call(
         functools.partial(early_kernel, counts[: len(early)]),
         out_shape=(
             jax.ShapeDtypeStruct((span, channels), BF16),
             lanes,
             lanes,
             jax.ShapeDtypeStruct((span, channels), F32),
+            jax.ShapeDtypeStruct((len(early), span, channels), BF16),
         ),
-        in_specs=[vmem()] * (1 + len(early_parts)),
-        out_specs=(vmem(),) * 4,
+        in_specs=[vmem()] * (2 + len(early_parts)),
+        out_specs=(vmem(),) * 5,
         scratch_shapes=[pltpu.VMEM((len(early), span, span), F32)],
         cost_estimate=cost(
             4 * span * span * len(early) * channels,
@@ -573,18 +562,17 @@
             span * span * len(early),
         ),
         compiler_params=params(24),
-    )(score_weight, *early_parts)
+    )(score_weight, attn_gain, *early_parts)
 
     mid, swap_rows = pl.pallas_call(
         functools.partial(late_kernel, width, sources, counts, len(early)),
         out_shape=(jax.ShapeDtypeStruct((4 * width, channels), BF16),) * 2,
-        in_specs=[vmem()] * (8 + len(all_parts)),
+        in_specs=[vmem()] * (9 + len(all_parts)),
         out_specs=(vmem(),) * 2,
         scratch_shapes=[
             pltpu.VMEM((len(blocks), wide, span), F32),
             pltpu.VMEM((wide, channels), BF16),
             pltpu.VMEM((2 * width, channels), BF16),
-            pltpu.VMEM((2, EXTRA, 2 * width), BF16),
         ],
         cost_estimate=cost(
             2 * wide * span * len(blocks) * channels,
@@ -597,6 +585,7 @@
         peak,
         sums,
         added,
+        early_keys,
         resid,
         attn_gain,
         score_weight,

time: 46.8 us -> 46.3 us (0.989)
  starting transfers between devices: 25.9 us -> 20.4 us
  waiting for transfers between devices: 4.32 us -> 9.35 us
    ppermute x11 -> x13, waiting for transfers between devices: 2.04 us -> 7.07 us  [send(): return [lax.ppermute(part, 'rows', pairs) for part in parts]]
    ppermute x11 -> x13, starting transfers between devices: 18.6 us -> 14.7 us  [send(): return [lax.ppermute(part, 'rows', pairs) for part in parts]]
    ppermute x1, starting transfers between devices: 2.72 us -> 1.04 us  [shards(): swap_rows = lax.ppermute(swap_rows, 'rows', swap)]
  transfers between devices with their start and end apart: 15 -> 17, of which waited for: 6 -> 7; matrix products, arithmetic and copies ran while one was open for 0% -> 0% of each run, Pallas kernels for 15% -> 15%
where the time goes in v3:
time: 46.3 us; the launch traced here: 45.8 us
  starting transfers between devices  20.4 us (44%)
  Pallas kernels  15.3 us (33%)
  waiting for transfers between devices  9.35 us (20%)
  between operations  0.78 us (2%)
    ppermute x13, starting transfers between devices, send(): return [lax.ppermute(part, 'rows', pairs) for part in parts]  14.7 us
    ppermute x13, waiting for transfers between devices, send(): return [lax.ppermute(part, 'rows', pairs) for part in parts]  7.07 us
    ppermute x1, starting transfers between devices, shards(): edge_rows = lax.ppermute(edge_rows, 'rows', neighbour)  4.54 us
    pallas_call x1, Pallas kernels, shards(): pl.pallas_call(prepare_kernel, out_shape=(jax.ShapeDtypeStruct((frames, o...  3.75 us
    pallas_call x1, Pallas kernels, shards(): pl.pallas_call(functools.partial(conv_kernel, width), out_shape=(block, h...  2.87 us
    pallas_call x1, Pallas kernels, shards(): pl.pallas_call(functools.partial(late_kernel, width, sources, counts, len...  2.7 us
    pallas_call x1, Pallas kernels, shards(): pl.pallas_call(functools.partial(up_kernel, width), out_shape=jax.ShapeDt...  1.72 us
    pallas_call x1, Pallas kernels, shards(): pl.pallas_call(functools.partial(early_kernel, counts[:len(early)]), out_...  1.52 us
  transfers between devices with their start and end apart: 17, of which 7 were waited for; matrix products, arithmetic and copies ran while one was open for 0% of the time, Pallas kernels for 15%

profile of v3, /device:TPU:1, one launch (start us, length us, event | category | flops | bytes accessed | tf_op | source)
XLA Modules:
  0.0 45.8 jit_solution(2894105107397355582)
XLA Ops:
  0.6 1.1 %shard_map.114 = (bf16[4,64,384]{2,1,0:T(8,128)(2,1)S(1)}, bf16[3,2,64,384]{3,2,1,0:T(8,128)(2,1)S(1)}) custom-call(bf16[2,2,64,384]{3,2,1,0:T(8,128)(2,1)} %latents_ref.1, bf16[2,2,64,384]{3,2,1,0:T(8,128)(2,1)} %cache_ref.1), custom_call_target="tpu_custom_call" | custom-call | bytes 491520 | tf_op jit(solution)/shard_map/pallas_call | solution.py:462
  1.8 4.5 %collective-permute-start = (bf16[4,64,384]{2,1,0:T(8,128)(2,1)S(1)}, bf16[4,64,384]{2,1,0:T(8,128)(2,1)S(1)}, u32[]{:S(2)}, u32[]{:S(2)}) collective-permute-start(bf16[4,64,384]{2,1,0:T(8,128)(2,1)S(1)} %get-tuple-element.32), channel_id=1, source_target_pairs={{1,2},{3,4},{5,6},{7,8},{9,10},{11,12},{13,14},{2,1},{4,3},{6,5},{... | collective-permute-start | bytes 589832 | tf_op jit(solution)/shard_map/ppermute | solution.py:474
  6.5 3.8 %shard_map.115 = (bf16[2,128,384]{2,1,0:T(8,128)(2,1)}, bf16[3,128,384]{2,1,0:T(8,128)(2,1)S(1)}, bf16[3,3,384,1152]{3,2,1,0:T(8,128)(2,1)S(1)}) custom-call(bf16[2,128,384]{2,1,0:T(8,128)(2,1)} %bitcast.9, bf16[2,128,384]{2,1,0:T(8,128)(2,1)} %bitcast.10, bf16[3,3,3,384,384]{4,3,2,1,0:T(8,128)(2,1)} %weight_ref.1, f32[384]{0:T(512)} %norm_gain_ref.1), custom_call_target="tpu_custom_call" | custom-call | flops 983040 | bytes 7962624 | tf_op jit(solution)/shard_map/pallas_call | solution.py:476
  10.2 0.8 %collective-permute-done.edge_ref = bf16[4,64,384]{2,1,0:T(8,128)(2,1)S(1)} collective-permute-done((bf16[4,64,384]{2,1,0:T(8,128)(2,1)S(1)}, bf16[4,64,384]{2,1,0:T(8,128)(2,1)S(1)}, u32[]{:S(2)}, u32[]{:S(2)}) %collective-permute-start) | collective-permute-done | bytes 196640 | tf_op jit(solution)/shard_map/ppermute | solution.py:474
  11.0 1.4 %collective-permute-done.2.far_ref = bf16[4,64,384]{2,1,0:T(8,128)(2,1)S(1)} collective-permute-done((bf16[4,64,384]{2,1,0:T(8,128)(2,1)S(1)}, bf16[4,64,384]{2,1,0:T(8,128)(2,1)S(1)}, u32[]{:S(2)}, u32[]{:S(2)}) %collective-permute-start.2) | collective-permute-done | bytes 196640 | tf_op jit(solution)/shard_map/ppermute | solution.py:502
  12.5 2.9 %shard_map.116 = (bf16[256,384]{1,0:T(8,128)(2,1)S(1)}, bf16[128,384]{1,0:T(8,128)(2,1)S(1)}, bf16[128,384]{1,0:T(8,128)(2,1)S(1)}, f32[256,384]{1,0:T(8,128)S(1)}) custom-call(bf16[3,128,384]{2,1,0:T(8,128)(2,1)S(1)} %get-tuple-element.34.own_ref, bf16[3,128,384]{2,1,0:T(8,128)(2,1)S(1)} %bitcast.8, bf16[4,64,384]{2,1,0:T(8,128)(2,1)S(1)} %collective-permute-done.edge_ref, ...), custom_call_target="tpu_custom_call" | custom-call | flops 2038431744 | bytes 7962624 | tf_op jit(solution)/shard_map/pallas_call | solution.py:505
  15.4 3.1 %collective-permute-start.3 = (bf16[128,384]{1,0:T(8,128)(2,1)S(1)}, bf16[128,384]{1,0:T(8,128)(2,1)S(1)}, u32[]{:S(2)}, u32[]{:S(2)}) collective-permute-start(bf16[128,384]{1,0:T(8,128)(2,1)S(1)} %get-tuple-element.39), channel_id=1, source_target_pairs={{0,4},{1,9},{2,6},{3,11},{4,12},{5,1},{6,14},{7,3},{8,0},{9,13},{1... | collective-permute-start | bytes 294920 | tf_op jit(solution)/shard_map/ppermute | solution.py:389
  18.5 1.3 %collective-permute-start.4 = (bf16[128,384]{1,0:T(8,128)(2,1)S(1)}, bf16[128,384]{1,0:T(8,128)(2,1)S(1)}, u32[]{:S(2)}, u32[]{:S(2)}) collective-permute-start(bf16[128,384]{1,0:T(8,128)(2,1)S(1)} %get-tuple-element.40), channel_id=1, source_target_pairs={{0,4},{1,9},{2,6},{3,11},{4,12},{5,1},{6,14},{7,3},{8,0},{9,13},{1... | collective-permute-start | bytes 294920 | tf_op jit(solution)/shard_map/ppermute | solution.py:389
  20.0 1.2 %collective-permute-start.10 = (bf16[128,384]{1,0:T(8,128)(2,1)S(1)}, bf16[128,384]{1,0:T(8,128)(2,1)S(1)}, u32[]{:S(2)}, u32[]{:S(2)}) collective-permute-start(bf16[128,384]{1,0:T(8,128)(2,1)S(1)} %get-tuple-element.40), channel_id=1, source_target_pairs={{0,2},{1,3},{2,0},{3,1},{4,6},{5,7},{6,4},{7,5},{8,10},{9,11},{10,... | collective-permute-start | bytes 294920 | tf_op jit(solution)/shard_map/ppermute | solution.py:389
  21.2 2.3 %collective-permute-start.6 = (bf16[128,384]{1,0:T(8,128)(2,1)S(1)}, bf16[128,384]{1,0:T(8,128)(2,1)S(1)}, u32[]{:S(2)}, u32[]{:S(2)}) collective-permute-start(bf16[128,384]{1,0:T(8,128)(2,1)S(1)} %collective-permute-done.3.refs_1_), channel_id=1, source_target_pairs={{0,4},{1,9},{2,6},{3,11},{4,12},{5,1},{6,14},{7,3},{8,0},{9,13},{1... | collective-permute-start | bytes 294920 | tf_op jit(solution)/shard_map/ppermute | solution.py:389
  23.6 1.8 %collective-permute-start.7 = (bf16[128,384]{1,0:T(8,128)(2,1)S(1)}, bf16[128,384]{1,0:T(8,128)(2,1)S(1)}, u32[]{:S(2)}, u32[]{:S(2)}) collective-permute-start(bf16[128,384]{1,0:T(8,128)(2,1)S(1)} %collective-permute-done.3.refs_1_), channel_id=1, source_target_pairs={{0,2},{1,3},{2,0},{3,1},{4,6},{5,7},{6,4},{7,5},{8,10},{9,11},{10,... | collective-permute-start | bytes 294920 | tf_op jit(solution)/shard_map/ppermute | solution.py:389
  25.4 1.9 %collective-permute-start.9 = (bf16[128,384]{1,0:T(8,128)(2,1)S(1)}, bf16[128,384]{1,0:T(8,128)(2,1)S(1)}, u32[]{:S(2)}, u32[]{:S(2)}) collective-permute-start(bf16[128,384]{1,0:T(8,128)(2,1)S(1)} %collective-permute-done.4.refs_2_), channel_id=1, source_target_pairs={{0,2},{1,3},{2,0},{3,1},{4,6},{5,7},{6,4},{7,5},{8,10},{9,11},{10,... | collective-permute-start | bytes 294920 | tf_op jit(solution)/shard_map/ppermute | solution.py:389
  27.3 0.6 %collective-permute-start.15 = (bf16[128,384]{1,0:T(8,128)(2,1)S(1)}, bf16[128,384]{1,0:T(8,128)(2,1)S(1)}, u32[]{:S(2)}, u32[]{:S(2)}) collective-permute-start(bf16[128,384]{1,0:T(8,128)(2,1)S(1)} %collective-permute-done.10.refs_8_), channel_id=1, source_target_pairs={{0,8},{1,5},{2,10},{3,7},{4,0},{5,13},{6,2},{7,15},{8,12},{9,1},{1... | collective-permute-start | bytes 294920 | tf_op jit(solution)/shard_map/ppermute | solution.py:389
  28.0 1.0 %collective-permute-done.8.refs_6_ = bf16[128,384]{1,0:T(8,128)(2,1)S(1)} collective-permute-done((bf16[128,384]{1,0:T(8,128)(2,1)S(1)}, bf16[128,384]{1,0:T(8,128)(2,1)S(1)}, u32[]{:S(2)}, u32[]{:S(2)}) %collective-permute-start.8) | collective-permute-done | bytes 98336 | tf_op jit(solution)/shard_map/ppermute | solution.py:389
  29.6 0.8 %collective-permute-start.14 = (bf16[128,384]{1,0:T(8,128)(2,1)S(1)}, bf16[128,384]{1,0:T(8,128)(2,1)S(1)}, u32[]{:S(2)}, u32[]{:S(2)}) collective-permute-start(bf16[128,384]{1,0:T(8,128)(2,1)S(1)} %collective-permute-done.5.refs_7_), channel_id=1, source_target_pairs={{0,8},{1,5},{2,10},{3,7},{4,0},{5,13},{6,2},{7,15},{8,12},{9,1},{1... | collective-permute-start | bytes 294920 | tf_op jit(solution)/shard_map/ppermute | solution.py:389
  30.3 0.9 %collective-permute-start.12 = (bf16[128,384]{1,0:T(8,128)(2,1)S(1)}, bf16[128,384]{1,0:T(8,128)(2,1)S(1)}, u32[]{:S(2)}, u32[]{:S(2)}) collective-permute-start(bf16[128,384]{1,0:T(8,128)(2,1)S(1)} %collective-permute-done.8.refs_6_), channel_id=1, source_target_pairs={{0,2},{1,3},{2,0},{3,1},{4,6},{5,7},{6,4},{7,5},{8,10},{9,11},{10,... | collective-permute-start | bytes 294920 | tf_op jit(solution)/shard_map/ppermute | solution.py:389
  31.2 0.5 %collective-permute-start.11 = (bf16[128,384]{1,0:T(8,128)(2,1)S(1)}, bf16[128,384]{1,0:T(8,128)(2,1)S(1)}, u32[]{:S(2)}, u32[]{:S(2)}) collective-permute-start(bf16[128,384]{1,0:T(8,128)(2,1)S(1)} %collective-permute-done.6.refs_5_), channel_id=1, source_target_pairs={{0,2},{1,3},{2,0},{3,1},{4,6},{5,7},{6,4},{7,5},{8,10},{9,11},{10,... | collective-permute-start | bytes 294920 | tf_op jit(solution)/shard_map/ppermute | solution.py:389
  32.3 1.5 %shard_map.117 = (bf16[256,384]{1,0:T(8,128)(2,1)S(1)}, f32[256,128]{1,0:T(8,128)S(1)}, f32[256,128]{1,0:T(8,128)S(1)}, f32[256,384]{1,0:T(8,128)S(1)}, bf16[5,256,384]{2,1,0:T(8,128)(2,1)S(1)}) custom-call(bf16[384,384]{1,0:T(8,128)(2,1)S(1)} %get-tuple-element.31.score_ref, f32[384]{0:T(512)S(1)} %copy-done.6, ...), custom_call_target="tpu_custom_call" | custom-call | flops 503316480 | bytes 983040 | tf_op jit(solution)/shard_map/pallas_call | solution.py:547
  33.9 1.0 %collective-permute-done.15.refs_13_ = bf16[128,384]{1,0:T(8,128)(2,1)S(1)} collective-permute-done((bf16[128,384]{1,0:T(8,128)(2,1)S(1)}, bf16[128,384]{1,0:T(8,128)(2,1)S(1)}, u32[]{:S(2)}, u32[]{:S(2)}) %collective-permute-start.15) | collective-permute-done | bytes 98336 | tf_op jit(solution)/shard_map/ppermute | solution.py:389
  34.9 4.4 %collective-permute-done.14.refs_12_ = bf16[128,384]{1,0:T(8,128)(2,1)S(1)} collective-permute-done((bf16[128,384]{1,0:T(8,128)(2,1)S(1)}, bf16[128,384]{1,0:T(8,128)(2,1)S(1)}, u32[]{:S(2)}, u32[]{:S(2)}) %collective-permute-start.14) | collective-permute-done | bytes 98336 | tf_op jit(solution)/shard_map/ppermute | solution.py:389
  39.3 2.7 %shard_map.118 = (bf16[256,384]{1,0:T(8,128)(2,1)S(1)}, bf16[256,384]{1,0:T(8,128)(2,1)S(1)}) custom-call(bf16[256,384]{1,0:T(8,128)(2,1)S(1)} %get-tuple-element.48.own_query_ref, f32[256,128]{1,0:T(8,128)S(1)} %get-tuple-element.49.peak_ref, f32[256,128]{1,0:T(8,128)S(1)} %get-tuple-element.50.sums_ref, f32[256,384]{1,0:T(8,128)S(1)} %get-tuple-element.51.added_ref, ...), custom_call_target="tpu_custom_call" | custom-call | flops 603979776 | bytes 1572864 | tf_op jit(solution)/shard_map/pallas_call | solution.py:567
  42.0 1.0 %collective-permute-start.16 = (bf16[256,384]{1,0:T(8,128)(2,1)S(1)}, bf16[256,384]{1,0:T(8,128)(2,1)S(1)}, u32[]{:S(2)}, u32[]{:S(2)}) collective-permute-start(bf16[256,384]{1,0:T(8,128)(2,1)S(1)} %get-tuple-element.57), channel_id=1, source_target_pairs={{0,1},{1,0},{2,3},{3,2},{4,5},{5,4},{6,7},{7,6},{8,9},{9,8},{10,11... | collective-permute-start | bytes 589832 | tf_op jit(solution)/shard_map/ppermute | solution.py:596
  43.0 1.0 %shard_map.119.own_ref = bf16[4,192,128]{2,1,0:T(8,128)(2,1)S(1)} custom-call(bf16[256,384]{1,0:T(8,128)(2,1)S(1)} %get-tuple-element.58.rows_ref, bf16[3,3,192,384]{3,2,1,0:T(8,128)(2,1)S(1)} %bitcast.6), custom_call_target="tpu_custom_call" | custom-call | flops 339738624 | bytes 1327104 | tf_op jit(solution)/shard_map/pallas_call | solution.py:601
  44.1 1.7 %shard_map.120 = bf16[2,4,192,128]{3,2,1,0:T(8,128)(2,1)} custom-call(bf16[256,384]{1,0:T(8,128)(2,1)S(1)} %collective-permute-done.16.rows_ref, bf16[3,3,192,384]{3,2,1,0:T(8,128)(2,1)S(1)} %bitcast.7, bf16[4,192,128]{2,1,0:T(8,128)(2,1)S(1)} %shard_map.119.own_ref), custom_call_target="tpu_custom_call" | custom-call | flops 339738624 | bytes 1327104 | tf_op jit(solution)/shard_map/pallas_call | solution.py:609
  (32 shorter events, 1.5 us)
Async XLA Ops:
  0.6 11.9 %copy-start.5 = (f32[384]{0:T(512)S(1)}, f32[384]{0:T(512)}, u32[]{:S(2)}) copy-start(f32[384]{0:T(512)} %norm_gain_ref.1) | copy-start | bytes 4612
  1.8 9.2 %collective-permute-start = (bf16[4,64,384]{2,1,0:T(8,128)(2,1)S(1)}, bf16[4,64,384]{2,1,0:T(8,128)(2,1)S(1)}, u32[]{:S(2)}, u32[]{:S(2)}) collective-permute-start(bf16[4,64,384]{2,1,0:T(8,128)(2,1)S(1)} %get-tuple-element.32), channel_id=1, source_target_pairs={{1,2},{3,4},{5,6},{7,8},{9,10},{11,12},{13,14},{2,1},{4,3},{6,5},{... | collective-permute-start | bytes 589832 | tf_op jit(solution)/shard_map/ppermute | solution.py:474
  6.3 4.7 %collective-permute-start.1 = (bf16[3,2,64,384]{3,2,1,0:T(8,128)(2,1)S(1)}, bf16[3,2,64,384]{3,2,1,0:T(8,128)(2,1)S(1)}, u32[]{:S(2)}, u32[]{:S(2)}) collective-permute-start(bf16[3,2,64,384]{3,2,1,0:T(8,128)(2,1)S(1)} %get-tuple-element.35), channel_id=1, source_target_pairs={{0,1},{1,0},{2,3},{3,2},{4,5},{5,4},{6,7},{7,6},{8,9},{9,8},{10,11... | collective-permute-start | bytes 884744 | tf_op jit(solution)/shard_map/ppermute | solution.py:475
  6.4 25.4 %copy-start.1 = (bf16[384,384]{1,0:T(8,128)(2,1)S(1)}, bf16[384,384]{1,0:T(8,128)(2,1)}, u32[]{:S(2)}) copy-start(bf16[384,384]{1,0:T(8,128)(2,1)} %query_ref.1) | copy-start | bytes 884740
  6.4 25.3 %copy-start.2 = (bf16[384,384]{1,0:T(8,128)(2,1)S(1)}, bf16[384,384]{1,0:T(8,128)(2,1)}, u32[]{:S(2)}) copy-start(bf16[384,384]{1,0:T(8,128)(2,1)} %key_ref.1) | copy-start | bytes 884740
  6.4 25.3 %copy-start.3 = (bf16[384,384]{1,0:T(8,128)(2,1)S(1)}, bf16[384,384]{1,0:T(8,128)(2,1)}, u32[]{:S(2)}) copy-start(bf16[384,384]{1,0:T(8,128)(2,1)} %value_ref.1) | copy-start | bytes 884740
  6.5 25.3 %copy-start.4 = (bf16[384,384]{1,0:T(8,128)(2,1)S(1)}, bf16[384,384]{1,0:T(8,128)(2,1)}, u32[]{:S(2)}) copy-start(bf16[384,384]{1,0:T(8,128)(2,1)} %out_ref.1) | copy-start | bytes 884740
  6.5 25.9 %copy-start.6 = (f32[384]{0:T(512)S(1)}, f32[384]{0:T(512)}, u32[]{:S(2)}) copy-start(f32[384]{0:T(512)} %gain_ref.5) | copy-start | bytes 4612
  11.0 1.4 %collective-permute-start.2 = (bf16[4,64,384]{2,1,0:T(8,128)(2,1)S(1)}, bf16[4,64,384]{2,1,0:T(8,128)(2,1)S(1)}, u32[]{:S(2)}, u32[]{:S(2)}) collective-permute-start(bf16[4,64,384]{2,1,0:T(8,128)(2,1)S(1)} %collective-permute-done.edge_ref), channel_id=1, source_target_pairs={{0,1},{1,0},{2,3},{3,2},{4,5},{5,4},{6,7},{7,6},{8,9},{9,8},{10,11... | collective-permute-start | bytes 589832 | tf_op jit(solution)/shard_map/ppermute | solution.py:502
  12.5 30.6 %copy-start = (bf16[3,3,384,192]{2,3,1,0:T(8,128)(2,1)S(1)}, bf16[3,3,384,192]{2,3,1,0:T(8,128)(2,1)}, u32[]{:S(2)}) copy-start(bf16[3,3,384,192]{2,3,1,0:T(8,128)(2,1)} %param.19) | copy-start | bytes 3981316
  15.4 5.9 %collective-permute-start.3 = (bf16[128,384]{1,0:T(8,128)(2,1)S(1)}, bf16[128,384]{1,0:T(8,128)(2,1)S(1)}, u32[]{:S(2)}, u32[]{:S(2)}) collective-permute-start(bf16[128,384]{1,0:T(8,128)(2,1)S(1)} %get-tuple-element.39), channel_id=1, source_target_pairs={{0,4},{1,9},{2,6},{3,11},{4,12},{5,1},{6,14},{7,3},{8,0},{9,13},{1... | collective-permute-start | bytes 294920 | tf_op jit(solution)/shard_map/ppermute | solution.py:389
  18.5 6.9 %collective-permute-start.4 = (bf16[128,384]{1,0:T(8,128)(2,1)S(1)}, bf16[128,384]{1,0:T(8,128)(2,1)S(1)}, u32[]{:S(2)}, u32[]{:S(2)}) collective-permute-start(bf16[128,384]{1,0:T(8,128)(2,1)S(1)} %get-tuple-element.40), channel_id=1, source_target_pairs={{0,4},{1,9},{2,6},{3,11},{4,12},{5,1},{6,14},{7,3},{8,0},{9,13},{1... | collective-permute-start | bytes 294920 | tf_op jit(solution)/shard_map/ppermute | solution.py:389
  19.8 5.6 %collective-permute-start.5 = (bf16[128,384]{1,0:T(8,128)(2,1)S(1)}, bf16[128,384]{1,0:T(8,128)(2,1)S(1)}, u32[]{:S(2)}, u32[]{:S(2)}) collective-permute-start(bf16[128,384]{1,0:T(8,128)(2,1)S(1)} %get-tuple-element.39), channel_id=1, source_target_pairs={{0,2},{1,3},{2,0},{3,1},{4,6},{5,7},{6,4},{7,5},{8,10},{9,11},{10,... | collective-permute-start | bytes 294920 | tf_op jit(solution)/shard_map/ppermute | solution.py:389
  20.0 7.3 %collective-permute-start.10 = (bf16[128,384]{1,0:T(8,128)(2,1)S(1)}, bf16[128,384]{1,0:T(8,128)(2,1)S(1)}, u32[]{:S(2)}, u32[]{:S(2)}) collective-permute-start(bf16[128,384]{1,0:T(8,128)(2,1)S(1)} %get-tuple-element.40), channel_id=1, source_target_pairs={{0,2},{1,3},{2,0},{3,1},{4,6},{5,7},{6,4},{7,5},{8,10},{9,11},{10,... | collective-permute-start | bytes 294920 | tf_op jit(solution)/shard_map/ppermute | solution.py:389
  21.2 6.1 %collective-permute-start.6 = (bf16[128,384]{1,0:T(8,128)(2,1)S(1)}, bf16[128,384]{1,0:T(8,128)(2,1)S(1)}, u32[]{:S(2)}, u32[]{:S(2)}) collective-permute-start(bf16[128,384]{1,0:T(8,128)(2,1)S(1)} %collective-permute-done.3.refs_1_), channel_id=1, source_target_pairs={{0,4},{1,9},{2,6},{3,11},{4,12},{5,1},{6,14},{7,3},{8,0},{9,13},{1... | collective-permute-start | bytes 294920 | tf_op jit(solution)/shard_map/ppermute | solution.py:389
  23.6 4.4 %collective-permute-start.7 = (bf16[128,384]{1,0:T(8,128)(2,1)S(1)}, bf16[128,384]{1,0:T(8,128)(2,1)S(1)}, u32[]{:S(2)}, u32[]{:S(2)}) collective-permute-start(bf16[128,384]{1,0:T(8,128)(2,1)S(1)} %collective-permute-done.3.refs_1_), channel_id=1, source_target_pairs={{0,2},{1,3},{2,0},{3,1},{4,6},{5,7},{6,4},{7,5},{8,10},{9,11},{10,... | collective-permute-start | bytes 294920 | tf_op jit(solution)/shard_map/ppermute | solution.py:389
  25.4 3.7 %collective-permute-start.8 = (bf16[128,384]{1,0:T(8,128)(2,1)S(1)}, bf16[128,384]{1,0:T(8,128)(2,1)S(1)}, u32[]{:S(2)}, u32[]{:S(2)}) collective-permute-start(bf16[128,384]{1,0:T(8,128)(2,1)S(1)} %collective-permute-done.4.refs_2_), channel_id=1, source_target_pairs={{0,4},{1,9},{2,6},{3,11},{4,12},{5,1},{6,14},{7,3},{8,0},{9,13},{1... | collective-permute-start | bytes 294920 | tf_op jit(solution)/shard_map/ppermute | solution.py:389
  25.4 4.2 %collective-permute-start.9 = (bf16[128,384]{1,0:T(8,128)(2,1)S(1)}, bf16[128,384]{1,0:T(8,128)(2,1)S(1)}, u32[]{:S(2)}, u32[]{:S(2)}) collective-permute-start(bf16[128,384]{1,0:T(8,128)(2,1)S(1)} %collective-permute-done.4.refs_2_), channel_id=1, source_target_pairs={{0,2},{1,3},{2,0},{3,1},{4,6},{5,7},{6,4},{7,5},{8,10},{9,11},{10,... | collective-permute-start | bytes 294920 | tf_op jit(solution)/shard_map/ppermute | solution.py:389
  27.3 12.0 %collective-permute-start.13 = (bf16[256,384]{1,0:T(8,128)(2,1)S(1)}, bf16[256,384]{1,0:T(8,128)(2,1)S(1)}, u32[]{:S(2)}, u32[]{:S(2)}) collective-permute-start(bf16[256,384]{1,0:T(8,128)(2,1)S(1)} %get-tuple-element.55.refs_0_), channel_id=1, source_target_pairs={{0,8},{1,5},{2,10},{3,7},{4,0},{5,13},{6,2},{7,15},{8,12},{9,1},{1... | collective-permute-start | bytes 589832 | tf_op jit(solution)/shard_map/ppermute | solution.py:389
  27.3 7.5 %collective-permute-start.15 = (bf16[128,384]{1,0:T(8,128)(2,1)S(1)}, bf16[128,384]{1,0:T(8,128)(2,1)S(1)}, u32[]{:S(2)}, u32[]{:S(2)}) collective-permute-start(bf16[128,384]{1,0:T(8,128)(2,1)S(1)} %collective-permute-done.10.refs_8_), channel_id=1, source_target_pairs={{0,8},{1,5},{2,10},{3,7},{4,0},{5,13},{6,2},{7,15},{8,12},{9,1},{1... | collective-permute-start | bytes 294920 | tf_op jit(solution)/shard_map/ppermute | solution.py:389
  29.6 9.7 %collective-permute-start.14 = (bf16[128,384]{1,0:T(8,128)(2,1)S(1)}, bf16[128,384]{1,0:T(8,128)(2,1)S(1)}, u32[]{:S(2)}, u32[]{:S(2)}) collective-permute-start(bf16[128,384]{1,0:T(8,128)(2,1)S(1)} %collective-permute-done.5.refs_7_), channel_id=1, source_target_pairs={{0,8},{1,5},{2,10},{3,7},{4,0},{5,13},{6,2},{7,15},{8,12},{9,1},{1... | collective-permute-start | bytes 294920 | tf_op jit(solution)/shard_map/ppermute | solution.py:389
  30.3 9.0 %collective-permute-start.12 = (bf16[128,384]{1,0:T(8,128)(2,1)S(1)}, bf16[128,384]{1,0:T(8,128)(2,1)S(1)}, u32[]{:S(2)}, u32[]{:S(2)}) collective-permute-start(bf16[128,384]{1,0:T(8,128)(2,1)S(1)} %collective-permute-done.8.refs_6_), channel_id=1, source_target_pairs={{0,2},{1,3},{2,0},{3,1},{4,6},{5,7},{6,4},{7,5},{8,10},{9,11},{10,... | collective-permute-start | bytes 294920 | tf_op jit(solution)/shard_map/ppermute | solution.py:389
  31.2 8.1 %collective-permute-start.11 = (bf16[128,384]{1,0:T(8,128)(2,1)S(1)}, bf16[128,384]{1,0:T(8,128)(2,1)S(1)}, u32[]{:S(2)}, u32[]{:S(2)}) collective-permute-start(bf16[128,384]{1,0:T(8,128)(2,1)S(1)} %collective-permute-done.6.refs_5_), channel_id=1, source_target_pairs={{0,2},{1,3},{2,0},{3,1},{4,6},{5,7},{6,4},{7,5},{8,10},{9,11},{10,... | collective-permute-start | bytes 294920 | tf_op jit(solution)/shard_map/ppermute | solution.py:389
  42.0 2.1 %collective-permute-start.16 = (bf16[256,384]{1,0:T(8,128)(2,1)S(1)}, bf16[256,384]{1,0:T(8,128)(2,1)S(1)}, u32[]{:S(2)}, u32[]{:S(2)}) collective-permute-start(bf16[256,384]{1,0:T(8,128)(2,1)S(1)} %get-tuple-element.57), channel_id=1, source_target_pairs={{0,1},{1,0},{2,3},{3,2},{4,5},{5,4},{6,7},{7,6},{8,9},{9,8},{10,11... | collective-permute-start | bytes 589832 | tf_op jit(solution)/shard_map/ppermute | solution.py:596

commit v4 on v3

--- a/solution.py
+++ b/solution.py
@@ -326,7 +326,7 @@
     swap_ref[...] = mid[pl.ds(pl.multiple_of(2 * (1 - core) * width, width), 4 * width), :]
 
 
-def up_rows(width, ref, weight_ref, out):
+def up_rows(width, ref, weight_ref, out, done=lambda pair: None):
     channels = ref.shape[1]
     outputs = weight_ref.shape[2]
     span = 4 * width
@@ -357,6 +357,7 @@
         woven = jnp.dot(mixed, weave, preferred_element_type=F32).astype(BF16)
         for i in range(2):
             out[2 * pair + i] = woven[:, i * wide : (i + 1) * wide]
+        done(pair)
 
 
 def up_own_kernel(width, rows_ref, weight_ref, out_ref):
@@ -366,8 +367,12 @@
 def up_kernel(width, rows_ref, weight_ref, own_ref, out_ref, result, sems):
     core = lax.axis_index("rows") % 2
     stores = start_all([(own_ref, out_ref.at[core])], sems)
-    up_rows(width, rows_ref, weight_ref, result)
-    stores = stores + start_all([(result, out_ref.at[1 - core])], sems, 1)
+
+    def store(pair):
+        rows = pl.ds(2 * pair, 2)
+        stores.extend(start_all([(result.at[rows], out_ref.at[1 - core, rows])], sems, 1 + pair))
+
+    up_rows(width, rows_ref, weight_ref, result, store)
     wait_all(stores)
 
 
@@ -380,8 +385,8 @@
     follow = {a: ring[(i + 1) % length] for i, a in enumerate(ring)}
     forth = {a * depth + b: follow[a] * depth + b for a in range(length) for b in range(depth)}
     return_ = {target: source for source, target in forth.items()}
-    onward = (forth, return_)
-    backward = (return_, forth)
+    onward = (return_, forth)
+    backward = (forth, return_)
     across = ({k: k ^ 1 for k in range(chips)},) * 2
 
     def send(parts, targets):
@@ -613,7 +618,7 @@
         out_specs=anywhere,
         scratch_shapes=[
             pltpu.VMEM(fine_shape, BF16),
-            pltpu.SemaphoreType.DMA((2,)),
+            pltpu.SemaphoreType.DMA((3,)),
         ],
         cost_estimate=up_cost,
         compiler_params=params(16),

time: 46.3 us -> 46.5 us (level)
  starting transfers between devices: 20.4 us -> 21.7 us
  waiting for transfers between devices: 9.35 us -> 8.26 us
    ppermute x1, starting transfers between devices: 1.04 us -> 3.23 us  [shards(): swap_rows = lax.ppermute(swap_rows, 'rows', swap)]
    ppermute x13, waiting for transfers between devices: 7.07 us -> 5.98 us  [send(): return [lax.ppermute(part, 'rows', pairs) for part in parts]]
    ppermute x13, starting transfers between devices: 14.7 us -> 13.8 us  [send(): return [lax.ppermute(part, 'rows', pairs) for part in parts]]
where the time goes in v4:
time: 46.5 us; the launch traced here: 46 us
  starting transfers between devices  21.7 us (47%)
  Pallas kernels  15.2 us (33%)
  waiting for transfers between devices  8.26 us (18%)
  between operations  0.78 us (2%)
    ppermute x13, starting transfers between devices, send(): return [lax.ppermute(part, 'rows', pairs) for part in parts]  13.8 us
    ppermute x13, waiting for transfers between devices, send(): return [lax.ppermute(part, 'rows', pairs) for part in parts]  5.98 us
    ppermute x1, starting transfers between devices, shards(): edge_rows = lax.ppermute(edge_rows, 'rows', neighbour)  4.54 us
    pallas_call x1, Pallas kernels, shards(): pl.pallas_call(prepare_kernel, out_shape=(jax.ShapeDtypeStruct((frames, o...  3.75 us
    ppermute x1, starting transfers between devices, shards(): swap_rows = lax.ppermute(swap_rows, 'rows', swap)  3.23 us
    pallas_call x1, Pallas kernels, shards(): pl.pallas_call(functools.partial(conv_kernel, width), out_shape=(block, h...  2.87 us
    pallas_call x1, Pallas kernels, shards(): pl.pallas_call(functools.partial(late_kernel, width, sources, counts, len...  2.7 us
    pallas_call x1, Pallas kernels, shards(): pl.pallas_call(functools.partial(up_kernel, width), out_shape=jax.ShapeDt...  1.69 us
  transfers between devices with their start and end apart: 17, of which 7 were waited for; matrix products, arithmetic and copies ran while one was open for 0% of the time, Pallas kernels for 15%

profile of v4, /device:TPU:1, one launch (start us, length us, event | category | flops | bytes accessed | tf_op | source)
XLA Modules:
  0.0 46.0 jit_solution(13819446600681010066)
XLA Ops:
  0.6 1.1 %shard_map.114 = (bf16[4,64,384]{2,1,0:T(8,128)(2,1)S(1)}, bf16[3,2,64,384]{3,2,1,0:T(8,128)(2,1)S(1)}) custom-call(bf16[2,2,64,384]{3,2,1,0:T(8,128)(2,1)} %latents_ref.1, bf16[2,2,64,384]{3,2,1,0:T(8,128)(2,1)} %cache_ref.1), custom_call_target="tpu_custom_call" | custom-call | bytes 491520 | tf_op jit(solution)/shard_map/pallas_call | solution.py:467
  1.8 4.5 %collective-permute-start = (bf16[4,64,384]{2,1,0:T(8,128)(2,1)S(1)}, bf16[4,64,384]{2,1,0:T(8,128)(2,1)S(1)}, u32[]{:S(2)}, u32[]{:S(2)}) collective-permute-start(bf16[4,64,384]{2,1,0:T(8,128)(2,1)S(1)} %get-tuple-element.32), channel_id=1, source_target_pairs={{1,2},{3,4},{5,6},{7,8},{9,10},{11,12},{13,14},{2,1},{4,3},{6,5},{... | collective-permute-start | bytes 589832 | tf_op jit(solution)/shard_map/ppermute | solution.py:479
  6.5 3.8 %shard_map.115 = (bf16[2,128,384]{2,1,0:T(8,128)(2,1)}, bf16[3,128,384]{2,1,0:T(8,128)(2,1)S(1)}, bf16[3,3,384,1152]{3,2,1,0:T(8,128)(2,1)S(1)}) custom-call(bf16[2,128,384]{2,1,0:T(8,128)(2,1)} %bitcast.9, bf16[2,128,384]{2,1,0:T(8,128)(2,1)} %bitcast.10, bf16[3,3,3,384,384]{4,3,2,1,0:T(8,128)(2,1)} %weight_ref.1, f32[384]{0:T(512)} %norm_gain_ref.1), custom_call_target="tpu_custom_call" | custom-call | flops 983040 | bytes 7962624 | tf_op jit(solution)/shard_map/pallas_call | solution.py:481
  10.2 0.8 %collective-permute-done.edge_ref = bf16[4,64,384]{2,1,0:T(8,128)(2,1)S(1)} collective-permute-done((bf16[4,64,384]{2,1,0:T(8,128)(2,1)S(1)}, bf16[4,64,384]{2,1,0:T(8,128)(2,1)S(1)}, u32[]{:S(2)}, u32[]{:S(2)}) %collective-permute-start) | collective-permute-done | bytes 196640 | tf_op jit(solution)/shard_map/ppermute | solution.py:479
  11.0 1.4 %collective-permute-done.2.far_ref = bf16[4,64,384]{2,1,0:T(8,128)(2,1)S(1)} collective-permute-done((bf16[4,64,384]{2,1,0:T(8,128)(2,1)S(1)}, bf16[4,64,384]{2,1,0:T(8,128)(2,1)S(1)}, u32[]{:S(2)}, u32[]{:S(2)}) %collective-permute-start.2) | collective-permute-done | bytes 196640 | tf_op jit(solution)/shard_map/ppermute | solution.py:507
  12.5 2.9 %shard_map.116 = (bf16[256,384]{1,0:T(8,128)(2,1)S(1)}, bf16[128,384]{1,0:T(8,128)(2,1)S(1)}, bf16[128,384]{1,0:T(8,128)(2,1)S(1)}, f32[256,384]{1,0:T(8,128)S(1)}) custom-call(bf16[3,128,384]{2,1,0:T(8,128)(2,1)S(1)} %get-tuple-element.34.own_ref, bf16[3,128,384]{2,1,0:T(8,128)(2,1)S(1)} %bitcast.8, bf16[4,64,384]{2,1,0:T(8,128)(2,1)S(1)} %collective-permute-done.edge_ref, ...), custom_call_target="tpu_custom_call" | custom-call | flops 2038431744 | bytes 7962624 | tf_op jit(solution)/shard_map/pallas_call | solution.py:510
  15.4 2.1 %collective-permute-start.3 = (bf16[128,384]{1,0:T(8,128)(2,1)S(1)}, bf16[128,384]{1,0:T(8,128)(2,1)S(1)}, u32[]{:S(2)}, u32[]{:S(2)}) collective-permute-start(bf16[128,384]{1,0:T(8,128)(2,1)S(1)} %get-tuple-element.39), channel_id=1, source_target_pairs={{0,8},{1,5},{2,10},{3,7},{4,0},{5,13},{6,2},{7,15},{8,12},{9,1},{1... | collective-permute-start | bytes 294920 | tf_op jit(solution)/shard_map/ppermute | solution.py:394
  17.4 2.3 %collective-permute-start.4 = (bf16[128,384]{1,0:T(8,128)(2,1)S(1)}, bf16[128,384]{1,0:T(8,128)(2,1)S(1)}, u32[]{:S(2)}, u32[]{:S(2)}) collective-permute-start(bf16[128,384]{1,0:T(8,128)(2,1)S(1)} %get-tuple-element.40), channel_id=1, source_target_pairs={{0,8},{1,5},{2,10},{3,7},{4,0},{5,13},{6,2},{7,15},{8,12},{9,1},{1... | collective-permute-start | bytes 294920 | tf_op jit(solution)/shard_map/ppermute | solution.py:394
  19.8 1.5 %collective-permute-start.10 = (bf16[128,384]{1,0:T(8,128)(2,1)S(1)}, bf16[128,384]{1,0:T(8,128)(2,1)S(1)}, u32[]{:S(2)}, u32[]{:S(2)}) collective-permute-start(bf16[128,384]{1,0:T(8,128)(2,1)S(1)} %get-tuple-element.40), channel_id=1, source_target_pairs={{0,2},{1,3},{2,0},{3,1},{4,6},{5,7},{6,4},{7,5},{8,10},{9,11},{10,... | collective-permute-start | bytes 294920 | tf_op jit(solution)/shard_map/ppermute | solution.py:394
  21.2 1.2 %collective-permute-start.6 = (bf16[128,384]{1,0:T(8,128)(2,1)S(1)}, bf16[128,384]{1,0:T(8,128)(2,1)S(1)}, u32[]{:S(2)}, u32[]{:S(2)}) collective-permute-start(bf16[128,384]{1,0:T(8,128)(2,1)S(1)} %collective-permute-done.3.refs_1_), channel_id=1, source_target_pairs={{0,8},{1,5},{2,10},{3,7},{4,0},{5,13},{6,2},{7,15},{8,12},{9,1},{1... | collective-permute-start | bytes 294920 | tf_op jit(solution)/shard_map/ppermute | solution.py:394
  23.5 1.8 %collective-permute-start.8 = (bf16[128,384]{1,0:T(8,128)(2,1)S(1)}, bf16[128,384]{1,0:T(8,128)(2,1)S(1)}, u32[]{:S(2)}, u32[]{:S(2)}) collective-permute-start(bf16[128,384]{1,0:T(8,128)(2,1)S(1)} %collective-permute-done.4.refs_2_), channel_id=1, source_target_pairs={{0,8},{1,5},{2,10},{3,7},{4,0},{5,13},{6,2},{7,15},{8,12},{9,1},{1... | collective-permute-start | bytes 294920 | tf_op jit(solution)/shard_map/ppermute | solution.py:394
  25.4 1.4 %collective-permute-start.9 = (bf16[128,384]{1,0:T(8,128)(2,1)S(1)}, bf16[128,384]{1,0:T(8,128)(2,1)S(1)}, u32[]{:S(2)}, u32[]{:S(2)}) collective-permute-start(bf16[128,384]{1,0:T(8,128)(2,1)S(1)} %collective-permute-done.4.refs_2_), channel_id=1, source_target_pairs={{0,2},{1,3},{2,0},{3,1},{4,6},{5,7},{6,4},{7,5},{8,10},{9,11},{10,... | collective-permute-start | bytes 294920 | tf_op jit(solution)/shard_map/ppermute | solution.py:394
  26.8 1.0 %collective-permute-start.15 = (bf16[128,384]{1,0:T(8,128)(2,1)S(1)}, bf16[128,384]{1,0:T(8,128)(2,1)S(1)}, u32[]{:S(2)}, u32[]{:S(2)}) collective-permute-start(bf16[128,384]{1,0:T(8,128)(2,1)S(1)} %collective-permute-done.10.refs_8_), channel_id=1, source_target_pairs={{0,4},{1,9},{2,6},{3,11},{4,12},{5,1},{6,14},{7,3},{8,0},{9,13},{1... | collective-permute-start | bytes 294920 | tf_op jit(solution)/shard_map/ppermute | solution.py:394
  27.8 0.7 %collective-permute-done.8.refs_6_ = bf16[128,384]{1,0:T(8,128)(2,1)S(1)} collective-permute-done((bf16[128,384]{1,0:T(8,128)(2,1)S(1)}, bf16[128,384]{1,0:T(8,128)(2,1)S(1)}, u32[]{:S(2)}, u32[]{:S(2)}) %collective-permute-start.8) | collective-permute-done | bytes 98336 | tf_op jit(solution)/shard_map/ppermute | solution.py:394
  28.5 1.6 %collective-permute-done.9.refs_4_ = bf16[128,384]{1,0:T(8,128)(2,1)S(1)} collective-permute-done((bf16[128,384]{1,0:T(8,128)(2,1)S(1)}, bf16[128,384]{1,0:T(8,128)(2,1)S(1)}, u32[]{:S(2)}, u32[]{:S(2)}) %collective-permute-start.9) | collective-permute-done | bytes 98336 | tf_op jit(solution)/shard_map/ppermute | solution.py:394
  30.7 0.8 %collective-permute-start.12 = (bf16[128,384]{1,0:T(8,128)(2,1)S(1)}, bf16[128,384]{1,0:T(8,128)(2,1)S(1)}, u32[]{:S(2)}, u32[]{:S(2)}) collective-permute-start(bf16[128,384]{1,0:T(8,128)(2,1)S(1)} %collective-permute-done.8.refs_6_), channel_id=1, source_target_pairs={{0,2},{1,3},{2,0},{3,1},{4,6},{5,7},{6,4},{7,5},{8,10},{9,11},{10,... | collective-permute-start | bytes 294920 | tf_op jit(solution)/shard_map/ppermute | solution.py:394
  31.4 0.7 %collective-permute-start.11 = (bf16[128,384]{1,0:T(8,128)(2,1)S(1)}, bf16[128,384]{1,0:T(8,128)(2,1)S(1)}, u32[]{:S(2)}, u32[]{:S(2)}) collective-permute-start(bf16[128,384]{1,0:T(8,128)(2,1)S(1)} %collective-permute-done.6.refs_5_), channel_id=1, source_target_pairs={{0,2},{1,3},{2,0},{3,1},{4,6},{5,7},{6,4},{7,5},{8,10},{9,11},{10,... | collective-permute-start | bytes 294920 | tf_op jit(solution)/shard_map/ppermute | solution.py:394
  32.7 1.5 %shard_map.117 = (bf16[256,384]{1,0:T(8,128)(2,1)S(1)}, f32[256,128]{1,0:T(8,128)S(1)}, f32[256,128]{1,0:T(8,128)S(1)}, f32[256,384]{1,0:T(8,128)S(1)}, bf16[5,256,384]{2,1,0:T(8,128)(2,1)S(1)}) custom-call(bf16[384,384]{1,0:T(8,128)(2,1)S(1)} %get-tuple-element.31.score_ref, f32[384]{0:T(512)S(1)} %copy-done.6, ...), custom_call_target="tpu_custom_call" | custom-call | flops 503316480 | bytes 983040 | tf_op jit(solution)/shard_map/pallas_call | solution.py:552
  34.2 1.0 %collective-permute-done.15.refs_13_ = bf16[128,384]{1,0:T(8,128)(2,1)S(1)} collective-permute-done((bf16[128,384]{1,0:T(8,128)(2,1)S(1)}, bf16[128,384]{1,0:T(8,128)(2,1)S(1)}, u32[]{:S(2)}, u32[]{:S(2)}) %collective-permute-start.15) | collective-permute-done | bytes 98336 | tf_op jit(solution)/shard_map/ppermute | solution.py:394
  35.2 2.1 %collective-permute-done.14.refs_12_ = bf16[128,384]{1,0:T(8,128)(2,1)S(1)} collective-permute-done((bf16[128,384]{1,0:T(8,128)(2,1)S(1)}, bf16[128,384]{1,0:T(8,128)(2,1)S(1)}, u32[]{:S(2)}, u32[]{:S(2)}) %collective-permute-start.14) | collective-permute-done | bytes 98336 | tf_op jit(solution)/shard_map/ppermute | solution.py:394
  37.3 2.7 %shard_map.118 = (bf16[256,384]{1,0:T(8,128)(2,1)S(1)}, bf16[256,384]{1,0:T(8,128)(2,1)S(1)}) custom-call(bf16[256,384]{1,0:T(8,128)(2,1)S(1)} %get-tuple-element.48.own_query_ref, f32[256,128]{1,0:T(8,128)S(1)} %get-tuple-element.49.peak_ref, f32[256,128]{1,0:T(8,128)S(1)} %get-tuple-element.50.sums_ref, f32[256,384]{1,0:T(8,128)S(1)} %get-tuple-element.51.added_ref, ...), custom_call_target="tpu_custom_call" | custom-call | flops 603979776 | bytes 1572864 | tf_op jit(solution)/shard_map/pallas_call | solution.py:572
  40.0 3.2 %collective-permute-start.16 = (bf16[256,384]{1,0:T(8,128)(2,1)S(1)}, bf16[256,384]{1,0:T(8,128)(2,1)S(1)}, u32[]{:S(2)}, u32[]{:S(2)}) collective-permute-start(bf16[256,384]{1,0:T(8,128)(2,1)S(1)} %get-tuple-element.57), channel_id=1, source_target_pairs={{0,1},{1,0},{2,3},{3,2},{4,5},{5,4},{6,7},{7,6},{8,9},{9,8},{10,11... | collective-permute-start | bytes 589832 | tf_op jit(solution)/shard_map/ppermute | solution.py:601
  43.2 1.0 %shard_map.119.own_ref = bf16[4,192,128]{2,1,0:T(8,128)(2,1)S(1)} custom-call(bf16[256,384]{1,0:T(8,128)(2,1)S(1)} %get-tuple-element.58.rows_ref, bf16[3,3,192,384]{3,2,1,0:T(8,128)(2,1)S(1)} %bitcast.6), custom_call_target="tpu_custom_call" | custom-call | flops 339738624 | bytes 1327104 | tf_op jit(solution)/shard_map/pallas_call | solution.py:606
  44.3 1.7 %shard_map.120 = bf16[2,4,192,128]{3,2,1,0:T(8,128)(2,1)} custom-call(bf16[256,384]{1,0:T(8,128)(2,1)S(1)} %collective-permute-done.16.rows_ref, bf16[3,3,192,384]{3,2,1,0:T(8,128)(2,1)S(1)} %bitcast.7, bf16[4,192,128]{2,1,0:T(8,128)(2,1)S(1)} %shard_map.119.own_ref), custom_call_target="tpu_custom_call" | custom-call | flops 339738624 | bytes 1327104 | tf_op jit(solution)/shard_map/pallas_call | solution.py:614
  (32 shorter events, 2.4 us)
Async XLA Ops:
  0.6 11.9 %copy-start.5 = (f32[384]{0:T(512)S(1)}, f32[384]{0:T(512)}, u32[]{:S(2)}) copy-start(f32[384]{0:T(512)} %norm_gain_ref.1) | copy-start | bytes 4612
  1.8 9.2 %collective-permute-start = (bf16[4,64,384]{2,1,0:T(8,128)(2,1)S(1)}, bf16[4,64,384]{2,1,0:T(8,128)(2,1)S(1)}, u32[]{:S(2)}, u32[]{:S(2)}) collective-permute-start(bf16[4,64,384]{2,1,0:T(8,128)(2,1)S(1)} %get-tuple-element.32), channel_id=1, source_target_pairs={{1,2},{3,4},{5,6},{7,8},{9,10},{11,12},{13,14},{2,1},{4,3},{6,5},{... | collective-permute-start | bytes 589832 | tf_op jit(solution)/shard_map/ppermute | solution.py:479
  6.3 4.7 %collective-permute-start.1 = (bf16[3,2,64,384]{3,2,1,0:T(8,128)(2,1)S(1)}, bf16[3,2,64,384]{3,2,1,0:T(8,128)(2,1)S(1)}, u32[]{:S(2)}, u32[]{:S(2)}) collective-permute-start(bf16[3,2,64,384]{3,2,1,0:T(8,128)(2,1)S(1)} %get-tuple-element.35), channel_id=1, source_target_pairs={{0,1},{1,0},{2,3},{3,2},{4,5},{5,4},{6,7},{7,6},{8,9},{9,8},{10,11... | collective-permute-start | bytes 884744 | tf_op jit(solution)/shard_map/ppermute | solution.py:480
  6.4 25.7 %copy-start.1 = (bf16[384,384]{1,0:T(8,128)(2,1)S(1)}, bf16[384,384]{1,0:T(8,128)(2,1)}, u32[]{:S(2)}) copy-start(bf16[384,384]{1,0:T(8,128)(2,1)} %query_ref.1) | copy-start | bytes 884740
  6.4 25.7 %copy-start.2 = (bf16[384,384]{1,0:T(8,128)(2,1)S(1)}, bf16[384,384]{1,0:T(8,128)(2,1)}, u32[]{:S(2)}) copy-start(bf16[384,384]{1,0:T(8,128)(2,1)} %key_ref.1) | copy-start | bytes 884740
  6.4 25.7 %copy-start.3 = (bf16[384,384]{1,0:T(8,128)(2,1)S(1)}, bf16[384,384]{1,0:T(8,128)(2,1)}, u32[]{:S(2)}) copy-start(bf16[384,384]{1,0:T(8,128)(2,1)} %value_ref.1) | copy-start | bytes 884740
  6.5 25.7 %copy-start.4 = (bf16[384,384]{1,0:T(8,128)(2,1)S(1)}, bf16[384,384]{1,0:T(8,128)(2,1)}, u32[]{:S(2)}) copy-start(bf16[384,384]{1,0:T(8,128)(2,1)} %out_ref.1) | copy-start | bytes 884740
  6.5 26.2 %copy-start.6 = (f32[384]{0:T(512)S(1)}, f32[384]{0:T(512)}, u32[]{:S(2)}) copy-start(f32[384]{0:T(512)} %gain_ref.5) | copy-start | bytes 4612
  11.0 1.4 %collective-permute-start.2 = (bf16[4,64,384]{2,1,0:T(8,128)(2,1)S(1)}, bf16[4,64,384]{2,1,0:T(8,128)(2,1)S(1)}, u32[]{:S(2)}, u32[]{:S(2)}) collective-permute-start(bf16[4,64,384]{2,1,0:T(8,128)(2,1)S(1)} %collective-permute-done.edge_ref), channel_id=1, source_target_pairs={{0,1},{1,0},{2,3},{3,2},{4,5},{5,4},{6,7},{7,6},{8,9},{9,8},{10,11... | collective-permute-start | bytes 589832 | tf_op jit(solution)/shard_map/ppermute | solution.py:507
  12.5 30.8 %copy-start = (bf16[3,3,384,192]{2,3,1,0:T(8,128)(2,1)S(1)}, bf16[3,3,384,192]{2,3,1,0:T(8,128)(2,1)}, u32[]{:S(2)}) copy-start(bf16[3,3,384,192]{2,3,1,0:T(8,128)(2,1)} %param.19) | copy-start | bytes 3981316
  15.4 5.9 %collective-permute-start.3 = (bf16[128,384]{1,0:T(8,128)(2,1)S(1)}, bf16[128,384]{1,0:T(8,128)(2,1)S(1)}, u32[]{:S(2)}, u32[]{:S(2)}) collective-permute-start(bf16[128,384]{1,0:T(8,128)(2,1)S(1)} %get-tuple-element.39), channel_id=1, source_target_pairs={{0,8},{1,5},{2,10},{3,7},{4,0},{5,13},{6,2},{7,15},{8,12},{9,1},{1... | collective-permute-start | bytes 294920 | tf_op jit(solution)/shard_map/ppermute | solution.py:394
  17.4 5.4 %collective-permute-start.4 = (bf16[128,384]{1,0:T(8,128)(2,1)S(1)}, bf16[128,384]{1,0:T(8,128)(2,1)S(1)}, u32[]{:S(2)}, u32[]{:S(2)}) collective-permute-start(bf16[128,384]{1,0:T(8,128)(2,1)S(1)} %get-tuple-element.40), channel_id=1, source_target_pairs={{0,8},{1,5},{2,10},{3,7},{4,0},{5,13},{6,2},{7,15},{8,12},{9,1},{1... | collective-permute-start | bytes 294920 | tf_op jit(solution)/shard_map/ppermute | solution.py:394
  19.8 3.8 %collective-permute-start.5 = (bf16[128,384]{1,0:T(8,128)(2,1)S(1)}, bf16[128,384]{1,0:T(8,128)(2,1)S(1)}, u32[]{:S(2)}, u32[]{:S(2)}) collective-permute-start(bf16[128,384]{1,0:T(8,128)(2,1)S(1)} %get-tuple-element.39), channel_id=1, source_target_pairs={{0,2},{1,3},{2,0},{3,1},{4,6},{5,7},{6,4},{7,5},{8,10},{9,11},{10,... | collective-permute-start | bytes 294920 | tf_op jit(solution)/shard_map/ppermute | solution.py:394
  19.8 7.0 %collective-permute-start.10 = (bf16[128,384]{1,0:T(8,128)(2,1)S(1)}, bf16[128,384]{1,0:T(8,128)(2,1)S(1)}, u32[]{:S(2)}, u32[]{:S(2)}) collective-permute-start(bf16[128,384]{1,0:T(8,128)(2,1)S(1)} %get-tuple-element.40), channel_id=1, source_target_pairs={{0,2},{1,3},{2,0},{3,1},{4,6},{5,7},{6,4},{7,5},{8,10},{9,11},{10,... | collective-permute-start | bytes 294920 | tf_op jit(solution)/shard_map/ppermute | solution.py:394
  21.2 5.5 %collective-permute-start.6 = (bf16[128,384]{1,0:T(8,128)(2,1)S(1)}, bf16[128,384]{1,0:T(8,128)(2,1)S(1)}, u32[]{:S(2)}, u32[]{:S(2)}) collective-permute-start(bf16[128,384]{1,0:T(8,128)(2,1)S(1)} %collective-permute-done.3.refs_1_), channel_id=1, source_target_pairs={{0,8},{1,5},{2,10},{3,7},{4,0},{5,13},{6,2},{7,15},{8,12},{9,1},{1... | collective-permute-start | bytes 294920 | tf_op jit(solution)/shard_map/ppermute | solution.py:394
  22.4 5.4 %collective-permute-start.7 = (bf16[128,384]{1,0:T(8,128)(2,1)S(1)}, bf16[128,384]{1,0:T(8,128)(2,1)S(1)}, u32[]{:S(2)}, u32[]{:S(2)}) collective-permute-start(bf16[128,384]{1,0:T(8,128)(2,1)S(1)} %collective-permute-done.3.refs_1_), channel_id=1, source_target_pairs={{0,2},{1,3},{2,0},{3,1},{4,6},{5,7},{6,4},{7,5},{8,10},{9,11},{10,... | collective-permute-start | bytes 294920 | tf_op jit(solution)/shard_map/ppermute | solution.py:394
  23.5 5.0 %collective-permute-start.8 = (bf16[128,384]{1,0:T(8,128)(2,1)S(1)}, bf16[128,384]{1,0:T(8,128)(2,1)S(1)}, u32[]{:S(2)}, u32[]{:S(2)}) collective-permute-start(bf16[128,384]{1,0:T(8,128)(2,1)S(1)} %collective-permute-done.4.refs_2_), channel_id=1, source_target_pairs={{0,8},{1,5},{2,10},{3,7},{4,0},{5,13},{6,2},{7,15},{8,12},{9,1},{1... | collective-permute-start | bytes 294920 | tf_op jit(solution)/shard_map/ppermute | solution.py:394
  25.4 4.7 %collective-permute-start.9 = (bf16[128,384]{1,0:T(8,128)(2,1)S(1)}, bf16[128,384]{1,0:T(8,128)(2,1)S(1)}, u32[]{:S(2)}, u32[]{:S(2)}) collective-permute-start(bf16[128,384]{1,0:T(8,128)(2,1)S(1)} %collective-permute-done.4.refs_2_), channel_id=1, source_target_pairs={{0,2},{1,3},{2,0},{3,1},{4,6},{5,7},{6,4},{7,5},{8,10},{9,11},{10,... | collective-permute-start | bytes 294920 | tf_op jit(solution)/shard_map/ppermute | solution.py:394
  26.8 10.5 %collective-permute-start.13 = (bf16[256,384]{1,0:T(8,128)(2,1)S(1)}, bf16[256,384]{1,0:T(8,128)(2,1)S(1)}, u32[]{:S(2)}, u32[]{:S(2)}) collective-permute-start(bf16[256,384]{1,0:T(8,128)(2,1)S(1)} %get-tuple-element.55.refs_0_), channel_id=1, source_target_pairs={{0,4},{1,9},{2,6},{3,11},{4,12},{5,1},{6,14},{7,3},{8,0},{9,13},{1... | collective-permute-start | bytes 589832 | tf_op jit(solution)/shard_map/ppermute | solution.py:394
  26.8 8.4 %collective-permute-start.15 = (bf16[128,384]{1,0:T(8,128)(2,1)S(1)}, bf16[128,384]{1,0:T(8,128)(2,1)S(1)}, u32[]{:S(2)}, u32[]{:S(2)}) collective-permute-start(bf16[128,384]{1,0:T(8,128)(2,1)S(1)} %collective-permute-done.10.refs_8_), channel_id=1, source_target_pairs={{0,4},{1,9},{2,6},{3,11},{4,12},{5,1},{6,14},{7,3},{8,0},{9,13},{1... | collective-permute-start | bytes 294920 | tf_op jit(solution)/shard_map/ppermute | solution.py:394
  30.1 7.2 %collective-permute-start.14 = (bf16[128,384]{1,0:T(8,128)(2,1)S(1)}, bf16[128,384]{1,0:T(8,128)(2,1)S(1)}, u32[]{:S(2)}, u32[]{:S(2)}) collective-permute-start(bf16[128,384]{1,0:T(8,128)(2,1)S(1)} %collective-permute-done.5.refs_7_), channel_id=1, source_target_pairs={{0,4},{1,9},{2,6},{3,11},{4,12},{5,1},{6,14},{7,3},{8,0},{9,13},{1... | collective-permute-start | bytes 294920 | tf_op jit(solution)/shard_map/ppermute | solution.py:394
  30.7 6.6 %collective-permute-start.12 = (bf16[128,384]{1,0:T(8,128)(2,1)S(1)}, bf16[128,384]{1,0:T(8,128)(2,1)S(1)}, u32[]{:S(2)}, u32[]{:S(2)}) collective-permute-start(bf16[128,384]{1,0:T(8,128)(2,1)S(1)} %collective-permute-done.8.refs_6_), channel_id=1, source_target_pairs={{0,2},{1,3},{2,0},{3,1},{4,6},{5,7},{6,4},{7,5},{8,10},{9,11},{10,... | collective-permute-start | bytes 294920 | tf_op jit(solution)/shard_map/ppermute | solution.py:394
  31.4 5.9 %collective-permute-start.11 = (bf16[128,384]{1,0:T(8,128)(2,1)S(1)}, bf16[128,384]{1,0:T(8,128)(2,1)S(1)}, u32[]{:S(2)}, u32[]{:S(2)}) collective-permute-start(bf16[128,384]{1,0:T(8,128)(2,1)S(1)} %collective-permute-done.6.refs_5_), channel_id=1, source_target_pairs={{0,2},{1,3},{2,0},{3,1},{4,6},{5,7},{6,4},{7,5},{8,10},{9,11},{10,... | collective-permute-start | bytes 294920 | tf_op jit(solution)/shard_map/ppermute | solution.py:394
  40.0 4.3 %collective-permute-start.16 = (bf16[256,384]{1,0:T(8,128)(2,1)S(1)}, bf16[256,384]{1,0:T(8,128)(2,1)S(1)}, u32[]{:S(2)}, u32[]{:S(2)}) collective-permute-start(bf16[256,384]{1,0:T(8,128)(2,1)S(1)} %get-tuple-element.57), channel_id=1, source_target_pairs={{0,1},{1,0},{2,3},{3,2},{4,5},{5,4},{6,7},{7,6},{8,9},{9,8},{10,11... | collective-permute-start | bytes 589832 | tf_op jit(solution)/shard_map/ppermute | solution.py:601

commit v5 on v4

--- a/solution.py
+++ b/solution.py
@@ -429,9 +429,6 @@
     if depth == 2:
         (early if length > 1 else late).append((crossed, moved(here, across)))
         if length > 1:
-            if steps > 0:
-                crossed = list(crossed)
-                tie((crossed, 0), (parts, 0))
             late.append((send(crossed, backward), moved(moved(here, across), backward)))
     return early, late
 

time: 46.5 us -> 46.5 us (level)
  starting transfers between devices: 21.7 us -> 25 us
  waiting for transfers between devices: 8.26 us -> 5.01 us
    ppermute x13, waiting for transfers between devices: 5.98 us -> 2.73 us  [send(): return [lax.ppermute(part, 'rows', pairs) for part in parts]]
    ppermute x13, starting transfers between devices: 13.8 us -> 15.8 us  [send(): return [lax.ppermute(part, 'rows', pairs) for part in parts]]
    ppermute x1, starting transfers between devices: 3.23 us -> 4.56 us  [shards(): swap_rows = lax.ppermute(swap_rows, 'rows', swap)]
  transfers between devices with their start and end apart: 17 -> 17, of which waited for: 7 -> 4; matrix products, arithmetic and copies ran while one was open for 0% -> 0% of each run, Pallas kernels for 15% -> 15%
where the time goes in v5:
time: 46.5 us; the launch traced here: 46 us
  starting transfers between devices  25 us (54%)
  Pallas kernels  15.2 us (33%)
  waiting for transfers between devices  5.01 us (11%)
  between operations  0.77 us (2%)
    ppermute x13, starting transfers between devices, send(): return [lax.ppermute(part, 'rows', pairs) for part in parts]  15.8 us
    ppermute x1, starting transfers between devices, shards(): swap_rows = lax.ppermute(swap_rows, 'rows', swap)  4.56 us
    ppermute x1, starting transfers between devices, shards(): edge_rows = lax.ppermute(edge_rows, 'rows', neighbour)  4.54 us
    pallas_call x1, Pallas kernels, shards(): pl.pallas_call(prepare_kernel, out_shape=(jax.ShapeDtypeStruct((frames, o...  3.75 us
    pallas_call x1, Pallas kernels, shards(): pl.pallas_call(functools.partial(conv_kernel, width), out_shape=(block, h...  2.87 us
    ppermute x13, waiting for transfers between devices, send(): return [lax.ppermute(part, 'rows', pairs) for part in parts]  2.73 us
    pallas_call x1, Pallas kernels, shards(): pl.pallas_call(functools.partial(late_kernel, width, sources, counts, len...  2.69 us
    pallas_call x1, Pallas kernels, shards(): pl.pallas_call(functools.partial(up_kernel, width), out_shape=jax.ShapeDt...  1.69 us
  transfers between devices with their start and end apart: 17, of which 4 were waited for; matrix products, arithmetic and copies ran while one was open for 0% of the time, Pallas kernels for 15%

profile of v5, /device:TPU:1, one launch (start us, length us, event | category | flops | bytes accessed | tf_op | source)
XLA Modules:
  0.0 46.0 jit_solution(14307502143500614444)
XLA Ops:
  0.6 1.1 %shard_map.114 = (bf16[4,64,384]{2,1,0:T(8,128)(2,1)S(1)}, bf16[3,2,64,384]{3,2,1,0:T(8,128)(2,1)S(1)}) custom-call(bf16[2,2,64,384]{3,2,1,0:T(8,128)(2,1)} %latents_ref.1, bf16[2,2,64,384]{3,2,1,0:T(8,128)(2,1)} %cache_ref.1), custom_call_target="tpu_custom_call" | custom-call | bytes 491520 | tf_op jit(solution)/shard_map/pallas_call | solution.py:464
  1.8 4.5 %collective-permute-start = (bf16[4,64,384]{2,1,0:T(8,128)(2,1)S(1)}, bf16[4,64,384]{2,1,0:T(8,128)(2,1)S(1)}, u32[]{:S(2)}, u32[]{:S(2)}) collective-permute-start(bf16[4,64,384]{2,1,0:T(8,128)(2,1)S(1)} %get-tuple-element.30), channel_id=1, source_target_pairs={{1,2},{3,4},{5,6},{7,8},{9,10},{11,12},{13,14},{2,1},{4,3},{6,5},{... | collective-permute-start | bytes 589832 | tf_op jit(solution)/shard_map/ppermute | solution.py:476
  6.5 3.8 %shard_map.115 = (bf16[2,128,384]{2,1,0:T(8,128)(2,1)}, bf16[3,128,384]{2,1,0:T(8,128)(2,1)S(1)}, bf16[3,3,384,1152]{3,2,1,0:T(8,128)(2,1)S(1)}) custom-call(bf16[2,128,384]{2,1,0:T(8,128)(2,1)} %bitcast.9, bf16[2,128,384]{2,1,0:T(8,128)(2,1)} %bitcast.10, bf16[3,3,3,384,384]{4,3,2,1,0:T(8,128)(2,1)} %weight_ref.1, f32[384]{0:T(512)} %norm_gain_ref.1), custom_call_target="tpu_custom_call" | custom-call | flops 983040 | bytes 7962624 | tf_op jit(solution)/shard_map/pallas_call | solution.py:478
  10.2 0.8 %collective-permute-done.edge_ref = bf16[4,64,384]{2,1,0:T(8,128)(2,1)S(1)} collective-permute-done((bf16[4,64,384]{2,1,0:T(8,128)(2,1)S(1)}, bf16[4,64,384]{2,1,0:T(8,128)(2,1)S(1)}, u32[]{:S(2)}, u32[]{:S(2)}) %collective-permute-start) | collective-permute-done | bytes 196640 | tf_op jit(solution)/shard_map/ppermute | solution.py:476
  11.0 1.4 %collective-permute-done.2.far_ref = bf16[4,64,384]{2,1,0:T(8,128)(2,1)S(1)} collective-permute-done((bf16[4,64,384]{2,1,0:T(8,128)(2,1)S(1)}, bf16[4,64,384]{2,1,0:T(8,128)(2,1)S(1)}, u32[]{:S(2)}, u32[]{:S(2)}) %collective-permute-start.2) | collective-permute-done | bytes 196640 | tf_op jit(solution)/shard_map/ppermute | solution.py:504
  12.5 2.9 %shard_map.116 = (bf16[256,384]{1,0:T(8,128)(2,1)S(1)}, bf16[128,384]{1,0:T(8,128)(2,1)S(1)}, bf16[128,384]{1,0:T(8,128)(2,1)S(1)}, f32[256,384]{1,0:T(8,128)S(1)}) custom-call(bf16[3,128,384]{2,1,0:T(8,128)(2,1)S(1)} %get-tuple-element.32.own_ref, bf16[3,128,384]{2,1,0:T(8,128)(2,1)S(1)} %bitcast.8, bf16[4,64,384]{2,1,0:T(8,128)(2,1)S(1)} %collective-permute-done.edge_ref, ...), custom_call_target="tpu_custom_call" | custom-call | flops 2038431744 | bytes 7962624 | tf_op jit(solution)/shard_map/pallas_call | solution.py:507
  15.4 2.1 %collective-permute-start.4 = (bf16[128,384]{1,0:T(8,128)(2,1)S(1)}, bf16[128,384]{1,0:T(8,128)(2,1)S(1)}, u32[]{:S(2)}, u32[]{:S(2)}) collective-permute-start(bf16[128,384]{1,0:T(8,128)(2,1)S(1)} %get-tuple-element.38), channel_id=1, source_target_pairs={{0,8},{1,5},{2,10},{3,7},{4,0},{5,13},{6,2},{7,15},{8,12},{9,1},{1... | collective-permute-start | bytes 294920 | tf_op jit(solution)/shard_map/ppermute | solution.py:394
  17.4 1.5 %collective-permute-start.5 = (bf16[128,384]{1,0:T(8,128)(2,1)S(1)}, bf16[128,384]{1,0:T(8,128)(2,1)S(1)}, u32[]{:S(2)}, u32[]{:S(2)}) collective-permute-start(bf16[128,384]{1,0:T(8,128)(2,1)S(1)} %get-tuple-element.37), channel_id=1, source_target_pairs={{0,2},{1,3},{2,0},{3,1},{4,6},{5,7},{6,4},{7,5},{8,10},{9,11},{10,... | collective-permute-start | bytes 294920 | tf_op jit(solution)/shard_map/ppermute | solution.py:394
  18.9 0.8 %collective-permute-start.3 = (bf16[128,384]{1,0:T(8,128)(2,1)S(1)}, bf16[128,384]{1,0:T(8,128)(2,1)S(1)}, u32[]{:S(2)}, u32[]{:S(2)}) collective-permute-start(bf16[128,384]{1,0:T(8,128)(2,1)S(1)} %get-tuple-element.37), channel_id=1, source_target_pairs={{0,8},{1,5},{2,10},{3,7},{4,0},{5,13},{6,2},{7,15},{8,12},{9,1},{1... | collective-permute-start | bytes 294920 | tf_op jit(solution)/shard_map/ppermute | solution.py:394
  19.8 1.5 %collective-permute-start.10 = (bf16[128,384]{1,0:T(8,128)(2,1)S(1)}, bf16[128,384]{1,0:T(8,128)(2,1)S(1)}, u32[]{:S(2)}, u32[]{:S(2)}) collective-permute-start(bf16[128,384]{1,0:T(8,128)(2,1)S(1)} %get-tuple-element.38), channel_id=1, source_target_pairs={{0,2},{1,3},{2,0},{3,1},{4,6},{5,7},{6,4},{7,5},{8,10},{9,11},{10,... | collective-permute-start | bytes 294920 | tf_op jit(solution)/shard_map/ppermute | solution.py:394
  21.2 2.3 %collective-permute-start.8 = (bf16[128,384]{1,0:T(8,128)(2,1)S(1)}, bf16[128,384]{1,0:T(8,128)(2,1)S(1)}, u32[]{:S(2)}, u32[]{:S(2)}) collective-permute-start(bf16[128,384]{1,0:T(8,128)(2,1)S(1)} %collective-permute-done.4.refs_2_), channel_id=1, source_target_pairs={{0,8},{1,5},{2,10},{3,7},{4,0},{5,13},{6,2},{7,15},{8,12},{9,1},{1... | collective-permute-start | bytes 294920 | tf_op jit(solution)/shard_map/ppermute | solution.py:394
  23.5 0.7 %collective-permute-start.9 = (bf16[128,384]{1,0:T(8,128)(2,1)S(1)}, bf16[128,384]{1,0:T(8,128)(2,1)S(1)}, u32[]{:S(2)}, u32[]{:S(2)}) collective-permute-start(bf16[128,384]{1,0:T(8,128)(2,1)S(1)} %collective-permute-done.4.refs_2_), channel_id=1, source_target_pairs={{0,2},{1,3},{2,0},{3,1},{4,6},{5,7},{6,4},{7,5},{8,10},{9,11},{10,... | collective-permute-start | bytes 294920 | tf_op jit(solution)/shard_map/ppermute | solution.py:394
  24.2 1.0 %collective-permute-start.6 = (bf16[128,384]{1,0:T(8,128)(2,1)S(1)}, bf16[128,384]{1,0:T(8,128)(2,1)S(1)}, u32[]{:S(2)}, u32[]{:S(2)}) collective-permute-start(bf16[128,384]{1,0:T(8,128)(2,1)S(1)} %collective-permute-done.3.refs_1_), channel_id=1, source_target_pairs={{0,8},{1,5},{2,10},{3,7},{4,0},{5,13},{6,2},{7,15},{8,12},{9,1},{1... | collective-permute-start | bytes 294920 | tf_op jit(solution)/shard_map/ppermute | solution.py:394
  25.2 1.4 %collective-permute-start.7 = (bf16[128,384]{1,0:T(8,128)(2,1)S(1)}, bf16[128,384]{1,0:T(8,128)(2,1)S(1)}, u32[]{:S(2)}, u32[]{:S(2)}) collective-permute-start(bf16[128,384]{1,0:T(8,128)(2,1)S(1)} %collective-permute-done.3.refs_1_), channel_id=1, source_target_pairs={{0,2},{1,3},{2,0},{3,1},{4,6},{5,7},{6,4},{7,5},{8,10},{9,11},{10,... | collective-permute-start | bytes 294920 | tf_op jit(solution)/shard_map/ppermute | solution.py:394
  26.7 0.7 %collective-permute-start.13 = (bf16[256,384]{1,0:T(8,128)(2,1)S(1)}, bf16[256,384]{1,0:T(8,128)(2,1)S(1)}, u32[]{:S(2)}, u32[]{:S(2)}) collective-permute-start(bf16[256,384]{1,0:T(8,128)(2,1)S(1)} %get-tuple-element.52.refs_0_), channel_id=1, source_target_pairs={{0,4},{1,9},{2,6},{3,11},{4,12},{5,1},{6,14},{7,3},{8,0},{9,13},{1... | collective-permute-start | bytes 589832 | tf_op jit(solution)/shard_map/ppermute | solution.py:394
  27.6 2.0 %collective-permute-start.15 = (bf16[128,384]{1,0:T(8,128)(2,1)S(1)}, bf16[128,384]{1,0:T(8,128)(2,1)S(1)}, u32[]{:S(2)}, u32[]{:S(2)}) collective-permute-start(bf16[128,384]{1,0:T(8,128)(2,1)S(1)} %collective-permute-done.10.refs_8_), channel_id=1, source_target_pairs={{0,4},{1,9},{2,6},{3,11},{4,12},{5,1},{6,14},{7,3},{8,0},{9,13},{1... | collective-permute-start | bytes 294920 | tf_op jit(solution)/shard_map/ppermute | solution.py:394
  29.7 1.5 %collective-permute-start.12 = (bf16[128,384]{1,0:T(8,128)(2,1)S(1)}, bf16[128,384]{1,0:T(8,128)(2,1)S(1)}, u32[]{:S(2)}, u32[]{:S(2)}) collective-permute-start(bf16[128,384]{1,0:T(8,128)(2,1)S(1)} %collective-permute-done.8.refs_6_), channel_id=1, source_target_pairs={{0,2},{1,3},{2,0},{3,1},{4,6},{5,7},{6,4},{7,5},{8,10},{9,11},{10,... | collective-permute-start | bytes 294920 | tf_op jit(solution)/shard_map/ppermute | solution.py:394
  31.8 1.5 %shard_map.117 = (bf16[256,384]{1,0:T(8,128)(2,1)S(1)}, f32[256,128]{1,0:T(8,128)S(1)}, f32[256,128]{1,0:T(8,128)S(1)}, f32[256,384]{1,0:T(8,128)S(1)}, bf16[5,256,384]{2,1,0:T(8,128)(2,1)S(1)}) custom-call(bf16[384,384]{1,0:T(8,128)(2,1)S(1)} %get-tuple-element.29.score_ref, f32[384]{0:T(512)S(1)} %copy-done.6, ...), custom_call_target="tpu_custom_call" | custom-call | flops 503316480 | bytes 983040 | tf_op jit(solution)/shard_map/pallas_call | solution.py:549
  33.3 0.8 %collective-permute-done.14.refs_12_ = bf16[128,384]{1,0:T(8,128)(2,1)S(1)} collective-permute-done((bf16[128,384]{1,0:T(8,128)(2,1)S(1)}, bf16[128,384]{1,0:T(8,128)(2,1)S(1)}, u32[]{:S(2)}, u32[]{:S(2)}) %collective-permute-start.14) | collective-permute-done | bytes 98336 | tf_op jit(solution)/shard_map/ppermute | solution.py:394
  34.1 1.9 %collective-permute-done.15.refs_13_ = bf16[128,384]{1,0:T(8,128)(2,1)S(1)} collective-permute-done((bf16[128,384]{1,0:T(8,128)(2,1)S(1)}, bf16[128,384]{1,0:T(8,128)(2,1)S(1)}, u32[]{:S(2)}, u32[]{:S(2)}) %collective-permute-start.15) | collective-permute-done | bytes 98336 | tf_op jit(solution)/shard_map/ppermute | solution.py:394
  36.0 2.7 %shard_map.118 = (bf16[256,384]{1,0:T(8,128)(2,1)S(1)}, bf16[256,384]{1,0:T(8,128)(2,1)S(1)}) custom-call(bf16[256,384]{1,0:T(8,128)(2,1)S(1)} %get-tuple-element.45.own_query_ref, f32[256,128]{1,0:T(8,128)S(1)} %get-tuple-element.46.peak_ref, f32[256,128]{1,0:T(8,128)S(1)} %get-tuple-element.47.sums_ref, f32[256,384]{1,0:T(8,128)S(1)} %get-tuple-element.48.added_ref, ...), custom_call_target="tpu_custom_call" | custom-call | flops 603979776 | bytes 1572864 | tf_op jit(solution)/shard_map/pallas_call | solution.py:569
  38.7 4.6 %collective-permute-start.16 = (bf16[256,384]{1,0:T(8,128)(2,1)S(1)}, bf16[256,384]{1,0:T(8,128)(2,1)S(1)}, u32[]{:S(2)}, u32[]{:S(2)}) collective-permute-start(bf16[256,384]{1,0:T(8,128)(2,1)S(1)} %get-tuple-element.53), channel_id=1, source_target_pairs={{0,1},{1,0},{2,3},{3,2},{4,5},{5,4},{6,7},{7,6},{8,9},{9,8},{10,11... | collective-permute-start | bytes 589832 | tf_op jit(solution)/shard_map/ppermute | solution.py:598
  43.3 1.0 %shard_map.119.own_ref = bf16[4,192,128]{2,1,0:T(8,128)(2,1)S(1)} custom-call(bf16[256,384]{1,0:T(8,128)(2,1)S(1)} %get-tuple-element.54.rows_ref, bf16[3,3,192,384]{3,2,1,0:T(8,128)(2,1)S(1)} %bitcast.6), custom_call_target="tpu_custom_call" | custom-call | flops 339738624 | bytes 1327104 | tf_op jit(solution)/shard_map/pallas_call | solution.py:603
  44.3 1.7 %shard_map.120 = bf16[2,4,192,128]{3,2,1,0:T(8,128)(2,1)} custom-call(bf16[256,384]{1,0:T(8,128)(2,1)S(1)} %collective-permute-done.16.rows_ref, bf16[3,3,192,384]{3,2,1,0:T(8,128)(2,1)S(1)} %bitcast.7, bf16[4,192,128]{2,1,0:T(8,128)(2,1)S(1)} %shard_map.119.own_ref), custom_call_target="tpu_custom_call" | custom-call | flops 339738624 | bytes 1327104 | tf_op jit(solution)/shard_map/pallas_call | solution.py:611
  (32 shorter events, 1.1 us)
Async XLA Ops:
  0.6 11.9 %copy-start.5 = (f32[384]{0:T(512)S(1)}, f32[384]{0:T(512)}, u32[]{:S(2)}) copy-start(f32[384]{0:T(512)} %norm_gain_ref.1) | copy-start | bytes 4612
  1.8 9.2 %collective-permute-start = (bf16[4,64,384]{2,1,0:T(8,128)(2,1)S(1)}, bf16[4,64,384]{2,1,0:T(8,128)(2,1)S(1)}, u32[]{:S(2)}, u32[]{:S(2)}) collective-permute-start(bf16[4,64,384]{2,1,0:T(8,128)(2,1)S(1)} %get-tuple-element.30), channel_id=1, source_target_pairs={{1,2},{3,4},{5,6},{7,8},{9,10},{11,12},{13,14},{2,1},{4,3},{6,5},{... | collective-permute-start | bytes 589832 | tf_op jit(solution)/shard_map/ppermute | solution.py:476
  6.3 4.7 %collective-permute-start.1 = (bf16[3,2,64,384]{3,2,1,0:T(8,128)(2,1)S(1)}, bf16[3,2,64,384]{3,2,1,0:T(8,128)(2,1)S(1)}, u32[]{:S(2)}, u32[]{:S(2)}) collective-permute-start(bf16[3,2,64,384]{3,2,1,0:T(8,128)(2,1)S(1)} %get-tuple-element.33), channel_id=1, source_target_pairs={{0,1},{1,0},{2,3},{3,2},{4,5},{5,4},{6,7},{7,6},{8,9},{9,8},{10,11... | collective-permute-start | bytes 884744 | tf_op jit(solution)/shard_map/ppermute | solution.py:477
  6.4 24.8 %copy-start.1 = (bf16[384,384]{1,0:T(8,128)(2,1)S(1)}, bf16[384,384]{1,0:T(8,128)(2,1)}, u32[]{:S(2)}) copy-start(bf16[384,384]{1,0:T(8,128)(2,1)} %query_ref.1) | copy-start | bytes 884740
  6.4 24.8 %copy-start.2 = (bf16[384,384]{1,0:T(8,128)(2,1)S(1)}, bf16[384,384]{1,0:T(8,128)(2,1)}, u32[]{:S(2)}) copy-start(bf16[384,384]{1,0:T(8,128)(2,1)} %key_ref.1) | copy-start | bytes 884740
  6.4 24.8 %copy-start.3 = (bf16[384,384]{1,0:T(8,128)(2,1)S(1)}, bf16[384,384]{1,0:T(8,128)(2,1)}, u32[]{:S(2)}) copy-start(bf16[384,384]{1,0:T(8,128)(2,1)} %value_ref.1) | copy-start | bytes 884740
  6.5 24.8 %copy-start.4 = (bf16[384,384]{1,0:T(8,128)(2,1)S(1)}, bf16[384,384]{1,0:T(8,128)(2,1)}, u32[]{:S(2)}) copy-start(bf16[384,384]{1,0:T(8,128)(2,1)} %out_ref.1) | copy-start | bytes 884740
  6.5 25.3 %copy-start.6 = (f32[384]{0:T(512)S(1)}, f32[384]{0:T(512)}, u32[]{:S(2)}) copy-start(f32[384]{0:T(512)} %gain_ref.5) | copy-start | bytes 4612
  11.0 1.4 %collective-permute-start.2 = (bf16[4,64,384]{2,1,0:T(8,128)(2,1)S(1)}, bf16[4,64,384]{2,1,0:T(8,128)(2,1)S(1)}, u32[]{:S(2)}, u32[]{:S(2)}) collective-permute-start(bf16[4,64,384]{2,1,0:T(8,128)(2,1)S(1)} %collective-permute-done.edge_ref), channel_id=1, source_target_pairs={{0,1},{1,0},{2,3},{3,2},{4,5},{5,4},{6,7},{7,6},{8,9},{9,8},{10,11... | collective-permute-start | bytes 589832 | tf_op jit(solution)/shard_map/ppermute | solution.py:504
  12.5 30.8 %copy-start = (bf16[3,3,384,192]{2,3,1,0:T(8,128)(2,1)S(1)}, bf16[3,3,384,192]{2,3,1,0:T(8,128)(2,1)}, u32[]{:S(2)}) copy-start(bf16[3,3,384,192]{2,3,1,0:T(8,128)(2,1)} %param.19) | copy-start | bytes 3981316
  15.4 5.9 %collective-permute-start.4 = (bf16[128,384]{1,0:T(8,128)(2,1)S(1)}, bf16[128,384]{1,0:T(8,128)(2,1)S(1)}, u32[]{:S(2)}, u32[]{:S(2)}) collective-permute-start(bf16[128,384]{1,0:T(8,128)(2,1)S(1)} %get-tuple-element.38), channel_id=1, source_target_pairs={{0,8},{1,5},{2,10},{3,7},{4,0},{5,13},{6,2},{7,15},{8,12},{9,1},{1... | collective-permute-start | bytes 294920 | tf_op jit(solution)/shard_map/ppermute | solution.py:394
  17.4 3.8 %collective-permute-start.5 = (bf16[128,384]{1,0:T(8,128)(2,1)S(1)}, bf16[128,384]{1,0:T(8,128)(2,1)S(1)}, u32[]{:S(2)}, u32[]{:S(2)}) collective-permute-start(bf16[128,384]{1,0:T(8,128)(2,1)S(1)} %get-tuple-element.37), channel_id=1, source_target_pairs={{0,2},{1,3},{2,0},{3,1},{4,6},{5,7},{6,4},{7,5},{8,10},{9,11},{10,... | collective-permute-start | bytes 294920 | tf_op jit(solution)/shard_map/ppermute | solution.py:394
  18.9 5.3 %collective-permute-start.3 = (bf16[128,384]{1,0:T(8,128)(2,1)S(1)}, bf16[128,384]{1,0:T(8,128)(2,1)S(1)}, u32[]{:S(2)}, u32[]{:S(2)}) collective-permute-start(bf16[128,384]{1,0:T(8,128)(2,1)S(1)} %get-tuple-element.37), channel_id=1, source_target_pairs={{0,8},{1,5},{2,10},{3,7},{4,0},{5,13},{6,2},{7,15},{8,12},{9,1},{1... | collective-permute-start | bytes 294920 | tf_op jit(solution)/shard_map/ppermute | solution.py:394
  19.8 6.9 %collective-permute-start.10 = (bf16[128,384]{1,0:T(8,128)(2,1)S(1)}, bf16[128,384]{1,0:T(8,128)(2,1)S(1)}, u32[]{:S(2)}, u32[]{:S(2)}) collective-permute-start(bf16[128,384]{1,0:T(8,128)(2,1)S(1)} %get-tuple-element.38), channel_id=1, source_target_pairs={{0,2},{1,3},{2,0},{3,1},{4,6},{5,7},{6,4},{7,5},{8,10},{9,11},{10,... | collective-permute-start | bytes 294920 | tf_op jit(solution)/shard_map/ppermute | solution.py:394
  21.2 6.1 %collective-permute-start.8 = (bf16[128,384]{1,0:T(8,128)(2,1)S(1)}, bf16[128,384]{1,0:T(8,128)(2,1)S(1)}, u32[]{:S(2)}, u32[]{:S(2)}) collective-permute-start(bf16[128,384]{1,0:T(8,128)(2,1)S(1)} %collective-permute-done.4.refs_2_), channel_id=1, source_target_pairs={{0,8},{1,5},{2,10},{3,7},{4,0},{5,13},{6,2},{7,15},{8,12},{9,1},{1... | collective-permute-start | bytes 294920 | tf_op jit(solution)/shard_map/ppermute | solution.py:394
  23.5 4.1 %collective-permute-start.9 = (bf16[128,384]{1,0:T(8,128)(2,1)S(1)}, bf16[128,384]{1,0:T(8,128)(2,1)S(1)}, u32[]{:S(2)}, u32[]{:S(2)}) collective-permute-start(bf16[128,384]{1,0:T(8,128)(2,1)S(1)} %collective-permute-done.4.refs_2_), channel_id=1, source_target_pairs={{0,2},{1,3},{2,0},{3,1},{4,6},{5,7},{6,4},{7,5},{8,10},{9,11},{10,... | collective-permute-start | bytes 294920 | tf_op jit(solution)/shard_map/ppermute | solution.py:394
  24.2 5.5 %collective-permute-start.6 = (bf16[128,384]{1,0:T(8,128)(2,1)S(1)}, bf16[128,384]{1,0:T(8,128)(2,1)S(1)}, u32[]{:S(2)}, u32[]{:S(2)}) collective-permute-start(bf16[128,384]{1,0:T(8,128)(2,1)S(1)} %collective-permute-done.3.refs_1_), channel_id=1, source_target_pairs={{0,8},{1,5},{2,10},{3,7},{4,0},{5,13},{6,2},{7,15},{8,12},{9,1},{1... | collective-permute-start | bytes 294920 | tf_op jit(solution)/shard_map/ppermute | solution.py:394
  25.2 4.5 %collective-permute-start.7 = (bf16[128,384]{1,0:T(8,128)(2,1)S(1)}, bf16[128,384]{1,0:T(8,128)(2,1)S(1)}, u32[]{:S(2)}, u32[]{:S(2)}) collective-permute-start(bf16[128,384]{1,0:T(8,128)(2,1)S(1)} %collective-permute-done.3.refs_1_), channel_id=1, source_target_pairs={{0,2},{1,3},{2,0},{3,1},{4,6},{5,7},{6,4},{7,5},{8,10},{9,11},{10,... | collective-permute-start | bytes 294920 | tf_op jit(solution)/shard_map/ppermute | solution.py:394
  26.7 9.3 %collective-permute-start.13 = (bf16[256,384]{1,0:T(8,128)(2,1)S(1)}, bf16[256,384]{1,0:T(8,128)(2,1)S(1)}, u32[]{:S(2)}, u32[]{:S(2)}) collective-permute-start(bf16[256,384]{1,0:T(8,128)(2,1)S(1)} %get-tuple-element.52.refs_0_), channel_id=1, source_target_pairs={{0,4},{1,9},{2,6},{3,11},{4,12},{5,1},{6,14},{7,3},{8,0},{9,13},{1... | collective-permute-start | bytes 589832 | tf_op jit(solution)/shard_map/ppermute | solution.py:394
  27.4 6.7 %collective-permute-start.14 = (bf16[128,384]{1,0:T(8,128)(2,1)S(1)}, bf16[128,384]{1,0:T(8,128)(2,1)S(1)}, u32[]{:S(2)}, u32[]{:S(2)}) collective-permute-start(bf16[128,384]{1,0:T(8,128)(2,1)S(1)} %collective-permute-done.5.refs_7_), channel_id=1, source_target_pairs={{0,4},{1,9},{2,6},{3,11},{4,12},{5,1},{6,14},{7,3},{8,0},{9,13},{1... | collective-permute-start | bytes 294920 | tf_op jit(solution)/shard_map/ppermute | solution.py:394
  27.6 8.4 %collective-permute-start.15 = (bf16[128,384]{1,0:T(8,128)(2,1)S(1)}, bf16[128,384]{1,0:T(8,128)(2,1)S(1)}, u32[]{:S(2)}, u32[]{:S(2)}) collective-permute-start(bf16[128,384]{1,0:T(8,128)(2,1)S(1)} %collective-permute-done.10.refs_8_), channel_id=1, source_target_pairs={{0,4},{1,9},{2,6},{3,11},{4,12},{5,1},{6,14},{7,3},{8,0},{9,13},{1... | collective-permute-start | bytes 294920 | tf_op jit(solution)/shard_map/ppermute | solution.py:394
  29.7 6.3 %collective-permute-start.12 = (bf16[128,384]{1,0:T(8,128)(2,1)S(1)}, bf16[128,384]{1,0:T(8,128)(2,1)S(1)}, u32[]{:S(2)}, u32[]{:S(2)}) collective-permute-start(bf16[128,384]{1,0:T(8,128)(2,1)S(1)} %collective-permute-done.8.refs_6_), channel_id=1, source_target_pairs={{0,2},{1,3},{2,0},{3,1},{4,6},{5,7},{6,4},{7,5},{8,10},{9,11},{10,... | collective-permute-start | bytes 294920 | tf_op jit(solution)/shard_map/ppermute | solution.py:394
  31.1 4.9 %collective-permute-start.11 = (bf16[128,384]{1,0:T(8,128)(2,1)S(1)}, bf16[128,384]{1,0:T(8,128)(2,1)S(1)}, u32[]{:S(2)}, u32[]{:S(2)}) collective-permute-start(bf16[128,384]{1,0:T(8,128)(2,1)S(1)} %collective-permute-done.6.refs_5_), channel_id=1, source_target_pairs={{0,2},{1,3},{2,0},{3,1},{4,6},{5,7},{6,4},{7,5},{8,10},{9,11},{10,... | collective-permute-start | bytes 294920 | tf_op jit(solution)/shard_map/ppermute | solution.py:394
  38.7 5.6 %collective-permute-start.16 = (bf16[256,384]{1,0:T(8,128)(2,1)S(1)}, bf16[256,384]{1,0:T(8,128)(2,1)S(1)}, u32[]{:S(2)}, u32[]{:S(2)}) collective-permute-start(bf16[256,384]{1,0:T(8,128)(2,1)S(1)} %get-tuple-element.53), channel_id=1, source_target_pairs={{0,1},{1,0},{2,3},{3,2},{4,5},{5,4},{6,7},{7,6},{8,9},{9,8},{10,11... | collective-permute-start | bytes 589832 | tf_op jit(solution)/shard_map/ppermute | solution.py:598

commit v6 on v3

--- a/solution.py
+++ b/solution.py
@@ -34,30 +34,14 @@
     return pl.CostEstimate(flops=flops, bytes_accessed=size, transcendentals=exps)
 
 
-def edges_kernel(latents_ref, cache_ref, edge_ref, both_ref, sems):
-    core = lax.axis_index("rows") % 2
-    row = core * (latents_ref.shape[1] - 1)
+def edges_kernel(latents_ref, cache_ref, edge_ref, sems):
+    row = lax.axis_index("rows") % 2 * (latents_ref.shape[1] - 1)
     copies = [
         pltpu.make_async_copy(cache_ref.at[:, row], edge_ref.at[pl.ds(0, 2)], sems.at[0]),
         pltpu.make_async_copy(latents_ref.at[:, row], edge_ref.at[pl.ds(2, 2)], sems.at[1]),
-        pltpu.make_async_copy(cache_ref.at[1], both_ref.at[core], sems.at[2]),
-        pltpu.make_async_copy(latents_ref.at[0], both_ref.at[1 + core], sems.at[3]),
     ]
     for copy in copies:
         copy.start()
-
-    @pl.when(core == 0)
-    def _():
-        last = pltpu.make_async_copy(latents_ref.at[1], both_ref.at[2], sems.at[4])
-        last.start()
-        last.wait()
-
-    @pl.when(core == 1)
-    def _():
-        last = pltpu.make_async_copy(cache_ref.at[0], both_ref.at[0], sems.at[4])
-        last.start()
-        last.wait()
-
     for copy in copies:
         copy.wait()
 
@@ -84,6 +68,7 @@
     gain_ref,
     act_ref,
     own_ref,
+    both_ref,
     staged_ref,
     latents,
     cache,
@@ -112,6 +97,9 @@
     own_ref[0] = cache[core]
     own_ref[1] = jnp.where(core == 0, cache[1], latents[0])
     own_ref[2] = latents[core]
+    both_ref[0] = cache[1 - core]
+    both_ref[1] = jnp.where(core == 0, latents[0], cache[1])
+    both_ref[2] = latents[1 - core]
     wait_all(store + stages)
 
 
@@ -459,29 +447,26 @@
 
     latents_in = pltpu.with_memory_space_constraint(latents, pltpu.HBM)
     cache_in = pltpu.with_memory_space_constraint(conv_cache, pltpu.HBM)
-    edge_rows, both = pl.pallas_call(
+    edge_rows = pl.pallas_call(
         edges_kernel,
-        out_shape=(
-            jax.ShapeDtypeStruct((2 * frames, width, channels), BF16),
-            jax.ShapeDtypeStruct((3, rows_here, width, channels), BF16),
-        ),
+        out_shape=jax.ShapeDtypeStruct((2 * frames, width, channels), BF16),
         in_specs=[hbm] * 2,
-        out_specs=(anywhere,) * 2,
-        scratch_shapes=[pltpu.SemaphoreType.DMA((5,))],
-        cost_estimate=cost(0, 20 * width * channels),
+        out_specs=anywhere,
+        scratch_shapes=[pltpu.SemaphoreType.DMA((2,))],
+        cost_estimate=cost(0, 8 * width * channels),
         compiler_params=params(4),
     )(latents_in, cache_in)
     edge_rows = lax.ppermute(edge_rows, "rows", neighbour)
-    both = lax.ppermute(both, "rows", swap)
-    act, own_rows, staged = pl.pallas_call(
+    act, own_rows, both, staged = pl.pallas_call(
         prepare_kernel,
         out_shape=(
             jax.ShapeDtypeStruct((frames, own, channels), BF16),
             jax.ShapeDtypeStruct((3, own, channels), BF16),
+            jax.ShapeDtypeStruct((3, own, channels), BF16),
             jax.ShapeDtypeStruct((3, 3, channels, 3 * channels), BF16),
         ),
         in_specs=[hbm] * 4,
-        out_specs=(anywhere, vmem(), anywhere),
+        out_specs=(anywhere, vmem(), vmem(), anywhere),
         scratch_shapes=[
             pltpu.VMEM((frames, own, channels), BF16),
             pltpu.VMEM((frames, own, channels), BF16),
@@ -498,6 +483,7 @@
         pltpu.with_memory_space_constraint(norm_gain, pltpu.HBM),
     )
 
+    both = lax.ppermute(both, "rows", swap)
     edge_rows, own_rows = lax.optimization_barrier((edge_rows, own_rows))
     far_rows = lax.ppermute(edge_rows, "rows", swap)
     block = jax.ShapeDtypeStruct((span, channels), BF16)
@@ -517,7 +503,7 @@
         compiler_params=params(20),
     )(
         own_rows,
-        both.reshape(3, own, channels),
+        both,
         edge_rows,
         far_rows,
         norm_gain,

time: 46.3 us -> 46.1 us (level)
    ppermute x1, waiting for transfers between devices: 0.01 us -> 0.77 us  [shards(): both = lax.ppermute(both, 'rows', swap)]
    ppermute x1, waiting for transfers between devices: 1.44 us -> 0.67 us  [shards(): far_rows = lax.ppermute(edge_rows, 'rows', swap)]
  transfers between devices with their start and end apart: 17 -> 17, of which waited for: 7 -> 8; matrix products, arithmetic and copies ran while one was open for 0% -> 0% of each run, Pallas kernels for 15% -> 15%
where the time goes in v6:
time: 46.1 us; the launch traced here: 45.6 us
  starting transfers between devices  20.4 us (44%)
  Pallas kernels  15.1 us (33%)
  waiting for transfers between devices  9.34 us (20%)
  between operations  0.78 us (2%)
    ppermute x13, starting transfers between devices, send(): return [lax.ppermute(part, 'rows', pairs) for part in parts]  14.8 us
    ppermute x13, waiting for transfers between devices, send(): return [lax.ppermute(part, 'rows', pairs) for part in parts]  7.06 us
    ppermute x1, starting transfers between devices, shards(): edge_rows = lax.ppermute(edge_rows, 'rows', neighbour)  4.54 us
    pallas_call x1, Pallas kernels, shards(): pl.pallas_call(prepare_kernel, out_shape=(jax.ShapeDtypeStruct((frames, o...  3.75 us
    pallas_call x1, Pallas kernels, shards(): pl.pallas_call(functools.partial(conv_kernel, width), out_shape=(block, h...  2.86 us
    pallas_call x1, Pallas kernels, shards(): pl.pallas_call(functools.partial(late_kernel, width, sources, counts, len...  2.7 us
    pallas_call x1, Pallas kernels, shards(): pl.pallas_call(functools.partial(up_kernel, width), out_shape=jax.ShapeDt...  1.72 us
    pallas_call x1, Pallas kernels, shards(): pl.pallas_call(functools.partial(early_kernel, counts[:len(early)]), out_...  1.52 us
  transfers between devices with their start and end apart: 17, of which 8 were waited for; matrix products, arithmetic and copies ran while one was open for 0% of the time, Pallas kernels for 15%

profile of v6, /device:TPU:1, one launch (start us, length us, event | category | flops | bytes accessed | tf_op | source)
XLA Modules:
  0.0 45.6 jit_solution(12189400375252331322)
XLA Ops:
  0.6 1.0 %shard_map.114 = bf16[4,64,384]{2,1,0:T(8,128)(2,1)S(1)} custom-call(bf16[2,2,64,384]{3,2,1,0:T(8,128)(2,1)} %latents_ref.1, bf16[2,2,64,384]{3,2,1,0:T(8,128)(2,1)} %cache_ref.1), custom_call_target="tpu_custom_call" | custom-call | bytes 196608 | tf_op jit(solution)/shard_map/pallas_call | solution.py:450
  1.6 4.5 %collective-permute-start = (bf16[4,64,384]{2,1,0:T(8,128)(2,1)S(1)}, bf16[4,64,384]{2,1,0:T(8,128)(2,1)S(1)}, u32[]{:S(2)}, u32[]{:S(2)}) collective-permute-start(bf16[4,64,384]{2,1,0:T(8,128)(2,1)S(1)} %shard_map.114), channel_id=1, source_target_pairs={{1,2},{3,4},{5,6},{7,8},{9,10},{11,12},{13,14},{2,1},{4,3},{6,5},{... | collective-permute-start | bytes 589832 | tf_op jit(solution)/shard_map/ppermute | solution.py:459
  6.2 3.8 %shard_map.115 = (bf16[2,128,384]{2,1,0:T(8,128)(2,1)}, bf16[3,128,384]{2,1,0:T(8,128)(2,1)S(1)}, bf16[3,128,384]{2,1,0:T(8,128)(2,1)S(1)}, bf16[3,3,384,1152]{3,2,1,0:T(8,128)(2,1)S(1)}) custom-call(bf16[2,128,384]{2,1,0:T(8,128)(2,1)} %bitcast.7, bf16[2,128,384]{2,1,0:T(8,128)(2,1)} %bitcast.8, bf16[3,3,3,384,384]{4,3,2,1,0:T(8,128)(2,1)} %weight_ref.1, ...), custom_call_target="tpu_custom_call" | custom-call | flops 983040 | bytes 7962624 | tf_op jit(solution)/shard_map/pallas_call | solution.py:460
  10.1 0.8 %collective-permute-done.edge_ref = bf16[4,64,384]{2,1,0:T(8,128)(2,1)S(1)} collective-permute-done((bf16[4,64,384]{2,1,0:T(8,128)(2,1)S(1)}, bf16[4,64,384]{2,1,0:T(8,128)(2,1)S(1)}, u32[]{:S(2)}, u32[]{:S(2)}) %collective-permute-start) | collective-permute-done | bytes 196640 | tf_op jit(solution)/shard_map/ppermute | solution.py:459
  10.9 0.8 %collective-permute-done.1.swap_ref = bf16[3,128,384]{2,1,0:T(8,128)(2,1)S(1)} collective-permute-done((bf16[3,128,384]{2,1,0:T(8,128)(2,1)S(1)}, bf16[3,128,384]{2,1,0:T(8,128)(2,1)S(1)}, u32[]{:S(2)}, u32[]{:S(2)}) %collective-permute-start.1) | collective-permute-done | bytes 294944 | tf_op jit(solution)/shard_map/ppermute | solution.py:486
  11.6 0.7 %collective-permute-done.2.far_ref = bf16[4,64,384]{2,1,0:T(8,128)(2,1)S(1)} collective-permute-done((bf16[4,64,384]{2,1,0:T(8,128)(2,1)S(1)}, bf16[4,64,384]{2,1,0:T(8,128)(2,1)S(1)}, u32[]{:S(2)}, u32[]{:S(2)}) %collective-permute-start.2) | collective-permute-done | bytes 196640 | tf_op jit(solution)/shard_map/ppermute | solution.py:488
  12.3 2.9 %shard_map.116 = (bf16[256,384]{1,0:T(8,128)(2,1)S(1)}, bf16[128,384]{1,0:T(8,128)(2,1)S(1)}, bf16[128,384]{1,0:T(8,128)(2,1)S(1)}, f32[256,384]{1,0:T(8,128)S(1)}) custom-call(bf16[3,128,384]{2,1,0:T(8,128)(2,1)S(1)} %get-tuple-element.32.own_ref, bf16[3,128,384]{2,1,0:T(8,128)(2,1)S(1)} %collective-permute-done.1.swap_ref, ...), custom_call_target="tpu_custom_call" | custom-call | flops 2038431744 | bytes 7962624 | tf_op jit(solution)/shard_map/pallas_call | solution.py:491
  15.2 3.1 %collective-permute-start.3 = (bf16[128,384]{1,0:T(8,128)(2,1)S(1)}, bf16[128,384]{1,0:T(8,128)(2,1)S(1)}, u32[]{:S(2)}, u32[]{:S(2)}) collective-permute-start(bf16[128,384]{1,0:T(8,128)(2,1)S(1)} %get-tuple-element.37), channel_id=1, source_target_pairs={{0,4},{1,9},{2,6},{3,11},{4,12},{5,1},{6,14},{7,3},{8,0},{9,13},{1... | collective-permute-start | bytes 294920 | tf_op jit(solution)/shard_map/ppermute | solution.py:377
  18.3 1.3 %collective-permute-start.4 = (bf16[128,384]{1,0:T(8,128)(2,1)S(1)}, bf16[128,384]{1,0:T(8,128)(2,1)S(1)}, u32[]{:S(2)}, u32[]{:S(2)}) collective-permute-start(bf16[128,384]{1,0:T(8,128)(2,1)S(1)} %get-tuple-element.38), channel_id=1, source_target_pairs={{0,4},{1,9},{2,6},{3,11},{4,12},{5,1},{6,14},{7,3},{8,0},{9,13},{1... | collective-permute-start | bytes 294920 | tf_op jit(solution)/shard_map/ppermute | solution.py:377
  19.8 1.2 %collective-permute-start.10 = (bf16[128,384]{1,0:T(8,128)(2,1)S(1)}, bf16[128,384]{1,0:T(8,128)(2,1)S(1)}, u32[]{:S(2)}, u32[]{:S(2)}) collective-permute-start(bf16[128,384]{1,0:T(8,128)(2,1)S(1)} %get-tuple-element.38), channel_id=1, source_target_pairs={{0,2},{1,3},{2,0},{3,1},{4,6},{5,7},{6,4},{7,5},{8,10},{9,11},{10,... | collective-permute-start | bytes 294920 | tf_op jit(solution)/shard_map/ppermute | solution.py:377
  21.1 2.3 %collective-permute-start.6 = (bf16[128,384]{1,0:T(8,128)(2,1)S(1)}, bf16[128,384]{1,0:T(8,128)(2,1)S(1)}, u32[]{:S(2)}, u32[]{:S(2)}) collective-permute-start(bf16[128,384]{1,0:T(8,128)(2,1)S(1)} %collective-permute-done.3.refs_1_), channel_id=1, source_target_pairs={{0,4},{1,9},{2,6},{3,11},{4,12},{5,1},{6,14},{7,3},{8,0},{9,13},{1... | collective-permute-start | bytes 294920 | tf_op jit(solution)/shard_map/ppermute | solution.py:377
  23.4 1.8 %collective-permute-start.7 = (bf16[128,384]{1,0:T(8,128)(2,1)S(1)}, bf16[128,384]{1,0:T(8,128)(2,1)S(1)}, u32[]{:S(2)}, u32[]{:S(2)}) collective-permute-start(bf16[128,384]{1,0:T(8,128)(2,1)S(1)} %collective-permute-done.3.refs_1_), channel_id=1, source_target_pairs={{0,2},{1,3},{2,0},{3,1},{4,6},{5,7},{6,4},{7,5},{8,10},{9,11},{10,... | collective-permute-start | bytes 294920 | tf_op jit(solution)/shard_map/ppermute | solution.py:377
  25.2 1.9 %collective-permute-start.9 = (bf16[128,384]{1,0:T(8,128)(2,1)S(1)}, bf16[128,384]{1,0:T(8,128)(2,1)S(1)}, u32[]{:S(2)}, u32[]{:S(2)}) collective-permute-start(bf16[128,384]{1,0:T(8,128)(2,1)S(1)} %collective-permute-done.4.refs_2_), channel_id=1, source_target_pairs={{0,2},{1,3},{2,0},{3,1},{4,6},{5,7},{6,4},{7,5},{8,10},{9,11},{10,... | collective-permute-start | bytes 294920 | tf_op jit(solution)/shard_map/ppermute | solution.py:377
  27.1 0.6 %collective-permute-start.15 = (bf16[128,384]{1,0:T(8,128)(2,1)S(1)}, bf16[128,384]{1,0:T(8,128)(2,1)S(1)}, u32[]{:S(2)}, u32[]{:S(2)}) collective-permute-start(bf16[128,384]{1,0:T(8,128)(2,1)S(1)} %collective-permute-done.10.refs_8_), channel_id=1, source_target_pairs={{0,8},{1,5},{2,10},{3,7},{4,0},{5,13},{6,2},{7,15},{8,12},{9,1},{1... | collective-permute-start | bytes 294920 | tf_op jit(solution)/shard_map/ppermute | solution.py:377
  27.8 1.0 %collective-permute-done.8.refs_6_ = bf16[128,384]{1,0:T(8,128)(2,1)S(1)} collective-permute-done((bf16[128,384]{1,0:T(8,128)(2,1)S(1)}, bf16[128,384]{1,0:T(8,128)(2,1)S(1)}, u32[]{:S(2)}, u32[]{:S(2)}) %collective-permute-start.8) | collective-permute-done | bytes 98336 | tf_op jit(solution)/shard_map/ppermute | solution.py:377
  29.4 0.8 %collective-permute-start.14 = (bf16[128,384]{1,0:T(8,128)(2,1)S(1)}, bf16[128,384]{1,0:T(8,128)(2,1)S(1)}, u32[]{:S(2)}, u32[]{:S(2)}) collective-permute-start(bf16[128,384]{1,0:T(8,128)(2,1)S(1)} %collective-permute-done.5.refs_7_), channel_id=1, source_target_pairs={{0,8},{1,5},{2,10},{3,7},{4,0},{5,13},{6,2},{7,15},{8,12},{9,1},{1... | collective-permute-start | bytes 294920 | tf_op jit(solution)/shard_map/ppermute | solution.py:377
  30.1 0.9 %collective-permute-start.12 = (bf16[128,384]{1,0:T(8,128)(2,1)S(1)}, bf16[128,384]{1,0:T(8,128)(2,1)S(1)}, u32[]{:S(2)}, u32[]{:S(2)}) collective-permute-start(bf16[128,384]{1,0:T(8,128)(2,1)S(1)} %collective-permute-done.8.refs_6_), channel_id=1, source_target_pairs={{0,2},{1,3},{2,0},{3,1},{4,6},{5,7},{6,4},{7,5},{8,10},{9,11},{10,... | collective-permute-start | bytes 294920 | tf_op jit(solution)/shard_map/ppermute | solution.py:377
  32.2 1.5 %shard_map.117 = (bf16[256,384]{1,0:T(8,128)(2,1)S(1)}, f32[256,128]{1,0:T(8,128)S(1)}, f32[256,128]{1,0:T(8,128)S(1)}, f32[256,384]{1,0:T(8,128)S(1)}, bf16[5,256,384]{2,1,0:T(8,128)(2,1)S(1)}) custom-call(bf16[384,384]{1,0:T(8,128)(2,1)S(1)} %get-tuple-element.30.score_ref, f32[384]{0:T(512)S(1)} %copy-done.6, ...), custom_call_target="tpu_custom_call" | custom-call | flops 503316480 | bytes 983040 | tf_op jit(solution)/shard_map/pallas_call | solution.py:533
  33.7 1.0 %collective-permute-done.15.refs_13_ = bf16[128,384]{1,0:T(8,128)(2,1)S(1)} collective-permute-done((bf16[128,384]{1,0:T(8,128)(2,1)S(1)}, bf16[128,384]{1,0:T(8,128)(2,1)S(1)}, u32[]{:S(2)}, u32[]{:S(2)}) %collective-permute-start.15) | collective-permute-done | bytes 98336 | tf_op jit(solution)/shard_map/ppermute | solution.py:377
  34.7 4.4 %collective-permute-done.14.refs_12_ = bf16[128,384]{1,0:T(8,128)(2,1)S(1)} collective-permute-done((bf16[128,384]{1,0:T(8,128)(2,1)S(1)}, bf16[128,384]{1,0:T(8,128)(2,1)S(1)}, u32[]{:S(2)}, u32[]{:S(2)}) %collective-permute-start.14) | collective-permute-done | bytes 98336 | tf_op jit(solution)/shard_map/ppermute | solution.py:377
  39.1 2.7 %shard_map.118 = (bf16[256,384]{1,0:T(8,128)(2,1)S(1)}, bf16[256,384]{1,0:T(8,128)(2,1)S(1)}) custom-call(bf16[256,384]{1,0:T(8,128)(2,1)S(1)} %get-tuple-element.46.own_query_ref, f32[256,128]{1,0:T(8,128)S(1)} %get-tuple-element.47.peak_ref, f32[256,128]{1,0:T(8,128)S(1)} %get-tuple-element.48.sums_ref, f32[256,384]{1,0:T(8,128)S(1)} %get-tuple-element.49.added_ref, ...), custom_call_target="tpu_custom_call" | custom-call | flops 603979776 | bytes 1572864 | tf_op jit(solution)/shard_map/pallas_call | solution.py:553
  41.8 1.0 %collective-permute-start.16 = (bf16[256,384]{1,0:T(8,128)(2,1)S(1)}, bf16[256,384]{1,0:T(8,128)(2,1)S(1)}, u32[]{:S(2)}, u32[]{:S(2)}) collective-permute-start(bf16[256,384]{1,0:T(8,128)(2,1)S(1)} %get-tuple-element.55), channel_id=1, source_target_pairs={{0,1},{1,0},{2,3},{3,2},{4,5},{5,4},{6,7},{7,6},{8,9},{9,8},{10,11... | collective-permute-start | bytes 589832 | tf_op jit(solution)/shard_map/ppermute | solution.py:582
  42.9 1.0 %shard_map.119.own_ref = bf16[4,192,128]{2,1,0:T(8,128)(2,1)S(1)} custom-call(bf16[256,384]{1,0:T(8,128)(2,1)S(1)} %get-tuple-element.56.rows_ref, bf16[3,3,192,384]{3,2,1,0:T(8,128)(2,1)S(1)} %bitcast.5), custom_call_target="tpu_custom_call" | custom-call | flops 339738624 | bytes 1327104 | tf_op jit(solution)/shard_map/pallas_call | solution.py:587
  43.9 1.7 %shard_map.120 = bf16[2,4,192,128]{3,2,1,0:T(8,128)(2,1)} custom-call(bf16[256,384]{1,0:T(8,128)(2,1)S(1)} %collective-permute-done.16.rows_ref, bf16[3,3,192,384]{3,2,1,0:T(8,128)(2,1)S(1)} %bitcast.6, bf16[4,192,128]{2,1,0:T(8,128)(2,1)S(1)} %shard_map.119.own_ref), custom_call_target="tpu_custom_call" | custom-call | flops 339738624 | bytes 1327104 | tf_op jit(solution)/shard_map/pallas_call | solution.py:595
  (32 shorter events, 2.1 us)
Async XLA Ops:
  0.6 11.7 %copy-start.5 = (f32[384]{0:T(512)S(1)}, f32[384]{0:T(512)}, u32[]{:S(2)}) copy-start(f32[384]{0:T(512)} %norm_gain_ref.1) | copy-start | bytes 4612
  1.6 9.2 %collective-permute-start = (bf16[4,64,384]{2,1,0:T(8,128)(2,1)S(1)}, bf16[4,64,384]{2,1,0:T(8,128)(2,1)S(1)}, u32[]{:S(2)}, u32[]{:S(2)}) collective-permute-start(bf16[4,64,384]{2,1,0:T(8,128)(2,1)S(1)} %shard_map.114), channel_id=1, source_target_pairs={{1,2},{3,4},{5,6},{7,8},{9,10},{11,12},{13,14},{2,1},{4,3},{6,5},{... | collective-permute-start | bytes 589832 | tf_op jit(solution)/shard_map/ppermute | solution.py:459
  6.2 25.4 %copy-start.1 = (bf16[384,384]{1,0:T(8,128)(2,1)S(1)}, bf16[384,384]{1,0:T(8,128)(2,1)}, u32[]{:S(2)}) copy-start(bf16[384,384]{1,0:T(8,128)(2,1)} %query_ref.1) | copy-start | bytes 884740
  6.2 25.4 %copy-start.2 = (bf16[384,384]{1,0:T(8,128)(2,1)S(1)}, bf16[384,384]{1,0:T(8,128)(2,1)}, u32[]{:S(2)}) copy-start(bf16[384,384]{1,0:T(8,128)(2,1)} %key_ref.1) | copy-start | bytes 884740
  6.2 25.4 %copy-start.3 = (bf16[384,384]{1,0:T(8,128)(2,1)S(1)}, bf16[384,384]{1,0:T(8,128)(2,1)}, u32[]{:S(2)}) copy-start(bf16[384,384]{1,0:T(8,128)(2,1)} %value_ref.1) | copy-start | bytes 884740
  6.2 25.4 %copy-start.4 = (bf16[384,384]{1,0:T(8,128)(2,1)S(1)}, bf16[384,384]{1,0:T(8,128)(2,1)}, u32[]{:S(2)}) copy-start(bf16[384,384]{1,0:T(8,128)(2,1)} %out_ref.1) | copy-start | bytes 884740
  6.2 25.9 %copy-start.6 = (f32[384]{0:T(512)S(1)}, f32[384]{0:T(512)}, u32[]{:S(2)}) copy-start(f32[384]{0:T(512)} %gain_ref.5) | copy-start | bytes 4612
  10.0 1.6 %collective-permute-start.1 = (bf16[3,128,384]{2,1,0:T(8,128)(2,1)S(1)}, bf16[3,128,384]{2,1,0:T(8,128)(2,1)S(1)}, u32[]{:S(2)}, u32[]{:S(2)}) collective-permute-start(bf16[3,128,384]{2,1,0:T(8,128)(2,1)S(1)} %get-tuple-element.33), channel_id=1, source_target_pairs={{0,1},{1,0},{2,3},{3,2},{4,5},{5,4},{6,7},{7,6},{8,9},{9,8},{10,11... | collective-permute-start | bytes 884744 | tf_op jit(solution)/shard_map/ppermute | solution.py:486
  10.9 1.4 %collective-permute-start.2 = (bf16[4,64,384]{2,1,0:T(8,128)(2,1)S(1)}, bf16[4,64,384]{2,1,0:T(8,128)(2,1)S(1)}, u32[]{:S(2)}, u32[]{:S(2)}) collective-permute-start(bf16[4,64,384]{2,1,0:T(8,128)(2,1)S(1)} %collective-permute-done.edge_ref), channel_id=1, source_target_pairs={{0,1},{1,0},{2,3},{3,2},{4,5},{5,4},{6,7},{7,6},{8,9},{9,8},{10,11... | collective-permute-start | bytes 589832 | tf_op jit(solution)/shard_map/ppermute | solution.py:488
  12.3 30.5 %copy-start = (bf16[3,3,384,192]{2,3,1,0:T(8,128)(2,1)S(1)}, bf16[3,3,384,192]{2,3,1,0:T(8,128)(2,1)}, u32[]{:S(2)}) copy-start(bf16[3,3,384,192]{2,3,1,0:T(8,128)(2,1)} %param.19) | copy-start | bytes 3981316
  15.2 5.9 %collective-permute-start.3 = (bf16[128,384]{1,0:T(8,128)(2,1)S(1)}, bf16[128,384]{1,0:T(8,128)(2,1)S(1)}, u32[]{:S(2)}, u32[]{:S(2)}) collective-permute-start(bf16[128,384]{1,0:T(8,128)(2,1)S(1)} %get-tuple-element.37), channel_id=1, source_target_pairs={{0,4},{1,9},{2,6},{3,11},{4,12},{5,1},{6,14},{7,3},{8,0},{9,13},{1... | collective-permute-start | bytes 294920 | tf_op jit(solution)/shard_map/ppermute | solution.py:377
  18.3 6.9 %collective-permute-start.4 = (bf16[128,384]{1,0:T(8,128)(2,1)S(1)}, bf16[128,384]{1,0:T(8,128)(2,1)S(1)}, u32[]{:S(2)}, u32[]{:S(2)}) collective-permute-start(bf16[128,384]{1,0:T(8,128)(2,1)S(1)} %get-tuple-element.38), channel_id=1, source_target_pairs={{0,4},{1,9},{2,6},{3,11},{4,12},{5,1},{6,14},{7,3},{8,0},{9,13},{1... | collective-permute-start | bytes 294920 | tf_op jit(solution)/shard_map/ppermute | solution.py:377
  19.6 5.6 %collective-permute-start.5 = (bf16[128,384]{1,0:T(8,128)(2,1)S(1)}, bf16[128,384]{1,0:T(8,128)(2,1)S(1)}, u32[]{:S(2)}, u32[]{:S(2)}) collective-permute-start(bf16[128,384]{1,0:T(8,128)(2,1)S(1)} %get-tuple-element.37), channel_id=1, source_target_pairs={{0,2},{1,3},{2,0},{3,1},{4,6},{5,7},{6,4},{7,5},{8,10},{9,11},{10,... | collective-permute-start | bytes 294920 | tf_op jit(solution)/shard_map/ppermute | solution.py:377
  19.8 7.3 %collective-permute-start.10 = (bf16[128,384]{1,0:T(8,128)(2,1)S(1)}, bf16[128,384]{1,0:T(8,128)(2,1)S(1)}, u32[]{:S(2)}, u32[]{:S(2)}) collective-permute-start(bf16[128,384]{1,0:T(8,128)(2,1)S(1)} %get-tuple-element.38), channel_id=1, source_target_pairs={{0,2},{1,3},{2,0},{3,1},{4,6},{5,7},{6,4},{7,5},{8,10},{9,11},{10,... | collective-permute-start | bytes 294920 | tf_op jit(solution)/shard_map/ppermute | solution.py:377
  21.1 6.1 %collective-permute-start.6 = (bf16[128,384]{1,0:T(8,128)(2,1)S(1)}, bf16[128,384]{1,0:T(8,128)(2,1)S(1)}, u32[]{:S(2)}, u32[]{:S(2)}) collective-permute-start(bf16[128,384]{1,0:T(8,128)(2,1)S(1)} %collective-permute-done.3.refs_1_), channel_id=1, source_target_pairs={{0,4},{1,9},{2,6},{3,11},{4,12},{5,1},{6,14},{7,3},{8,0},{9,13},{1... | collective-permute-start | bytes 294920 | tf_op jit(solution)/shard_map/ppermute | solution.py:377
  23.4 4.4 %collective-permute-start.7 = (bf16[128,384]{1,0:T(8,128)(2,1)S(1)}, bf16[128,384]{1,0:T(8,128)(2,1)S(1)}, u32[]{:S(2)}, u32[]{:S(2)}) collective-permute-start(bf16[128,384]{1,0:T(8,128)(2,1)S(1)} %collective-permute-done.3.refs_1_), channel_id=1, source_target_pairs={{0,2},{1,3},{2,0},{3,1},{4,6},{5,7},{6,4},{7,5},{8,10},{9,11},{10,... | collective-permute-start | bytes 294920 | tf_op jit(solution)/shard_map/ppermute | solution.py:377
  25.2 3.6 %collective-permute-start.8 = (bf16[128,384]{1,0:T(8,128)(2,1)S(1)}, bf16[128,384]{1,0:T(8,128)(2,1)S(1)}, u32[]{:S(2)}, u32[]{:S(2)}) collective-permute-start(bf16[128,384]{1,0:T(8,128)(2,1)S(1)} %collective-permute-done.4.refs_2_), channel_id=1, source_target_pairs={{0,4},{1,9},{2,6},{3,11},{4,12},{5,1},{6,14},{7,3},{8,0},{9,13},{1... | collective-permute-start | bytes 294920 | tf_op jit(solution)/shard_map/ppermute | solution.py:377
  25.2 4.2 %collective-permute-start.9 = (bf16[128,384]{1,0:T(8,128)(2,1)S(1)}, bf16[128,384]{1,0:T(8,128)(2,1)S(1)}, u32[]{:S(2)}, u32[]{:S(2)}) collective-permute-start(bf16[128,384]{1,0:T(8,128)(2,1)S(1)} %collective-permute-done.4.refs_2_), channel_id=1, source_target_pairs={{0,2},{1,3},{2,0},{3,1},{4,6},{5,7},{6,4},{7,5},{8,10},{9,11},{10,... | collective-permute-start | bytes 294920 | tf_op jit(solution)/shard_map/ppermute | solution.py:377
  27.1 12.0 %collective-permute-start.13 = (bf16[256,384]{1,0:T(8,128)(2,1)S(1)}, bf16[256,384]{1,0:T(8,128)(2,1)S(1)}, u32[]{:S(2)}, u32[]{:S(2)}) collective-permute-start(bf16[256,384]{1,0:T(8,128)(2,1)S(1)} %get-tuple-element.53.refs_0_), channel_id=1, source_target_pairs={{0,8},{1,5},{2,10},{3,7},{4,0},{5,13},{6,2},{7,15},{8,12},{9,1},{1... | collective-permute-start | bytes 589832 | tf_op jit(solution)/shard_map/ppermute | solution.py:377
  27.1 7.5 %collective-permute-start.15 = (bf16[128,384]{1,0:T(8,128)(2,1)S(1)}, bf16[128,384]{1,0:T(8,128)(2,1)S(1)}, u32[]{:S(2)}, u32[]{:S(2)}) collective-permute-start(bf16[128,384]{1,0:T(8,128)(2,1)S(1)} %collective-permute-done.10.refs_8_), channel_id=1, source_target_pairs={{0,8},{1,5},{2,10},{3,7},{4,0},{5,13},{6,2},{7,15},{8,12},{9,1},{1... | collective-permute-start | bytes 294920 | tf_op jit(solution)/shard_map/ppermute | solution.py:377
  29.4 9.7 %collective-permute-start.14 = (bf16[128,384]{1,0:T(8,128)(2,1)S(1)}, bf16[128,384]{1,0:T(8,128)(2,1)S(1)}, u32[]{:S(2)}, u32[]{:S(2)}) collective-permute-start(bf16[128,384]{1,0:T(8,128)(2,1)S(1)} %collective-permute-done.5.refs_7_), channel_id=1, source_target_pairs={{0,8},{1,5},{2,10},{3,7},{4,0},{5,13},{6,2},{7,15},{8,12},{9,1},{1... | collective-permute-start | bytes 294920 | tf_op jit(solution)/shard_map/ppermute | solution.py:377
  30.1 9.0 %collective-permute-start.12 = (bf16[128,384]{1,0:T(8,128)(2,1)S(1)}, bf16[128,384]{1,0:T(8,128)(2,1)S(1)}, u32[]{:S(2)}, u32[]{:S(2)}) collective-permute-start(bf16[128,384]{1,0:T(8,128)(2,1)S(1)} %collective-permute-done.8.refs_6_), channel_id=1, source_target_pairs={{0,2},{1,3},{2,0},{3,1},{4,6},{5,7},{6,4},{7,5},{8,10},{9,11},{10,... | collective-permute-start | bytes 294920 | tf_op jit(solution)/shard_map/ppermute | solution.py:377
  31.1 8.0 %collective-permute-start.11 = (bf16[128,384]{1,0:T(8,128)(2,1)S(1)}, bf16[128,384]{1,0:T(8,128)(2,1)S(1)}, u32[]{:S(2)}, u32[]{:S(2)}) collective-permute-start(bf16[128,384]{1,0:T(8,128)(2,1)S(1)} %collective-permute-done.6.refs_5_), channel_id=1, source_target_pairs={{0,2},{1,3},{2,0},{3,1},{4,6},{5,7},{6,4},{7,5},{8,10},{9,11},{10,... | collective-permute-start | bytes 294920 | tf_op jit(solution)/shard_map/ppermute | solution.py:377
  41.8 2.1 %collective-permute-start.16 = (bf16[256,384]{1,0:T(8,128)(2,1)S(1)}, bf16[256,384]{1,0:T(8,128)(2,1)S(1)}, u32[]{:S(2)}, u32[]{:S(2)}) collective-permute-start(bf16[256,384]{1,0:T(8,128)(2,1)S(1)} %get-tuple-element.55), channel_id=1, source_target_pairs={{0,1},{1,0},{2,3},{3,2},{4,5},{5,4},{6,7},{7,6},{8,9},{9,8},{10,11... | collective-permute-start | bytes 589832 | tf_op jit(solution)/shard_map/ppermute | solution.py:582

commit v7 on v6

--- a/solution.py
+++ b/solution.py
@@ -314,7 +314,7 @@
     swap_ref[...] = mid[pl.ds(pl.multiple_of(2 * (1 - core) * width, width), 4 * width), :]
 
 
-def up_rows(width, ref, weight_ref, out):
+def up_rows(width, ref, weight_ref, out, done=lambda pair: None):
     channels = ref.shape[1]
     outputs = weight_ref.shape[2]
     span = 4 * width
@@ -345,6 +345,7 @@
         woven = jnp.dot(mixed, weave, preferred_element_type=F32).astype(BF16)
         for i in range(2):
             out[2 * pair + i] = woven[:, i * wide : (i + 1) * wide]
+        done(pair)
 
 
 def up_own_kernel(width, rows_ref, weight_ref, out_ref):
@@ -354,8 +355,12 @@
 def up_kernel(width, rows_ref, weight_ref, own_ref, out_ref, result, sems):
     core = lax.axis_index("rows") % 2
     stores = start_all([(own_ref, out_ref.at[core])], sems)
-    up_rows(width, rows_ref, weight_ref, result)
-    stores = stores + start_all([(result, out_ref.at[1 - core])], sems, 1)
+
+    def store(pair):
+        rows = pl.ds(2 * pair, 2)
+        stores.extend(start_all([(result.at[rows], out_ref.at[1 - core, rows])], sems, 1 + pair))
+
+    up_rows(width, rows_ref, weight_ref, result, store)
     wait_all(stores)
 
 
@@ -599,7 +604,7 @@
         out_specs=anywhere,
         scratch_shapes=[
             pltpu.VMEM(fine_shape, BF16),
-            pltpu.SemaphoreType.DMA((2,)),
+            pltpu.SemaphoreType.DMA((3,)),
         ],
         cost_estimate=up_cost,
         compiler_params=params(16),

time: 46.1 us -> 46.1 us (level)
  no operation moved by 1% of the time
where the time goes in v7:
time: 46.1 us; the launch traced here: 45.6 us
  starting transfers between devices  20.4 us (44%)
  Pallas kernels  15.1 us (33%)
  waiting for transfers between devices  9.34 us (20%)
  between operations  0.78 us (2%)
    ppermute x13, starting transfers between devices, send(): return [lax.ppermute(part, 'rows', pairs) for part in parts]  14.8 us
    ppermute x13, waiting for transfers between devices, send(): return [lax.ppermute(part, 'rows', pairs) for part in parts]  7.06 us
    ppermute x1, starting transfers between devices, shards(): edge_rows = lax.ppermute(edge_rows, 'rows', neighbour)  4.54 us
    pallas_call x1, Pallas kernels, shards(): pl.pallas_call(prepare_kernel, out_shape=(jax.ShapeDtypeStruct((frames, o...  3.75 us
    pallas_call x1, Pallas kernels, shards(): pl.pallas_call(functools.partial(conv_kernel, width), out_shape=(block, h...  2.86 us
    pallas_call x1, Pallas kernels, shards(): pl.pallas_call(functools.partial(late_kernel, width, sources, counts, len...  2.7 us
    pallas_call x1, Pallas kernels, shards(): pl.pallas_call(functools.partial(up_kernel, width), out_shape=jax.ShapeDt...  1.69 us
    pallas_call x1, Pallas kernels, shards(): pl.pallas_call(functools.partial(early_kernel, counts[:len(early)]), out_...  1.52 us
  transfers between devices with their start and end apart: 17, of which 8 were waited for; matrix products, arithmetic and copies ran while one was open for 0% of the time, Pallas kernels for 15%

profile of v7, /device:TPU:1, one launch (start us, length us, event | category | flops | bytes accessed | tf_op | source)
XLA Modules:
  0.0 45.6 jit_solution(13056986117683718420)
XLA Ops:
  0.6 1.0 %shard_map.114 = bf16[4,64,384]{2,1,0:T(8,128)(2,1)S(1)} custom-call(bf16[2,2,64,384]{3,2,1,0:T(8,128)(2,1)} %latents_ref.1, bf16[2,2,64,384]{3,2,1,0:T(8,128)(2,1)} %cache_ref.1), custom_call_target="tpu_custom_call" | custom-call | bytes 196608 | tf_op jit(solution)/shard_map/pallas_call | solution.py:455
  1.6 4.5 %collective-permute-start = (bf16[4,64,384]{2,1,0:T(8,128)(2,1)S(1)}, bf16[4,64,384]{2,1,0:T(8,128)(2,1)S(1)}, u32[]{:S(2)}, u32[]{:S(2)}) collective-permute-start(bf16[4,64,384]{2,1,0:T(8,128)(2,1)S(1)} %shard_map.114), channel_id=1, source_target_pairs={{1,2},{3,4},{5,6},{7,8},{9,10},{11,12},{13,14},{2,1},{4,3},{6,5},{... | collective-permute-start | bytes 589832 | tf_op jit(solution)/shard_map/ppermute | solution.py:464
  6.2 3.8 %shard_map.115 = (bf16[2,128,384]{2,1,0:T(8,128)(2,1)}, bf16[3,128,384]{2,1,0:T(8,128)(2,1)S(1)}, bf16[3,128,384]{2,1,0:T(8,128)(2,1)S(1)}, bf16[3,3,384,1152]{3,2,1,0:T(8,128)(2,1)S(1)}) custom-call(bf16[2,128,384]{2,1,0:T(8,128)(2,1)} %bitcast.7, bf16[2,128,384]{2,1,0:T(8,128)(2,1)} %bitcast.8, bf16[3,3,3,384,384]{4,3,2,1,0:T(8,128)(2,1)} %weight_ref.1, ...), custom_call_target="tpu_custom_call" | custom-call | flops 983040 | bytes 7962624 | tf_op jit(solution)/shard_map/pallas_call | solution.py:465
  10.1 0.8 %collective-permute-done.edge_ref = bf16[4,64,384]{2,1,0:T(8,128)(2,1)S(1)} collective-permute-done((bf16[4,64,384]{2,1,0:T(8,128)(2,1)S(1)}, bf16[4,64,384]{2,1,0:T(8,128)(2,1)S(1)}, u32[]{:S(2)}, u32[]{:S(2)}) %collective-permute-start) | collective-permute-done | bytes 196640 | tf_op jit(solution)/shard_map/ppermute | solution.py:464
  10.9 0.8 %collective-permute-done.1.swap_ref = bf16[3,128,384]{2,1,0:T(8,128)(2,1)S(1)} collective-permute-done((bf16[3,128,384]{2,1,0:T(8,128)(2,1)S(1)}, bf16[3,128,384]{2,1,0:T(8,128)(2,1)S(1)}, u32[]{:S(2)}, u32[]{:S(2)}) %collective-permute-start.1) | collective-permute-done | bytes 294944 | tf_op jit(solution)/shard_map/ppermute | solution.py:491
  11.6 0.7 %collective-permute-done.2.far_ref = bf16[4,64,384]{2,1,0:T(8,128)(2,1)S(1)} collective-permute-done((bf16[4,64,384]{2,1,0:T(8,128)(2,1)S(1)}, bf16[4,64,384]{2,1,0:T(8,128)(2,1)S(1)}, u32[]{:S(2)}, u32[]{:S(2)}) %collective-permute-start.2) | collective-permute-done | bytes 196640 | tf_op jit(solution)/shard_map/ppermute | solution.py:493
  12.3 2.9 %shard_map.116 = (bf16[256,384]{1,0:T(8,128)(2,1)S(1)}, bf16[128,384]{1,0:T(8,128)(2,1)S(1)}, bf16[128,384]{1,0:T(8,128)(2,1)S(1)}, f32[256,384]{1,0:T(8,128)S(1)}) custom-call(bf16[3,128,384]{2,1,0:T(8,128)(2,1)S(1)} %get-tuple-element.32.own_ref, bf16[3,128,384]{2,1,0:T(8,128)(2,1)S(1)} %collective-permute-done.1.swap_ref, ...), custom_call_target="tpu_custom_call" | custom-call | flops 2038431744 | bytes 7962624 | tf_op jit(solution)/shard_map/pallas_call | solution.py:496
  15.2 3.1 %collective-permute-start.3 = (bf16[128,384]{1,0:T(8,128)(2,1)S(1)}, bf16[128,384]{1,0:T(8,128)(2,1)S(1)}, u32[]{:S(2)}, u32[]{:S(2)}) collective-permute-start(bf16[128,384]{1,0:T(8,128)(2,1)S(1)} %get-tuple-element.37), channel_id=1, source_target_pairs={{0,4},{1,9},{2,6},{3,11},{4,12},{5,1},{6,14},{7,3},{8,0},{9,13},{1... | collective-permute-start | bytes 294920 | tf_op jit(solution)/shard_map/ppermute | solution.py:382
  18.3 1.3 %collective-permute-start.4 = (bf16[128,384]{1,0:T(8,128)(2,1)S(1)}, bf16[128,384]{1,0:T(8,128)(2,1)S(1)}, u32[]{:S(2)}, u32[]{:S(2)}) collective-permute-start(bf16[128,384]{1,0:T(8,128)(2,1)S(1)} %get-tuple-element.38), channel_id=1, source_target_pairs={{0,4},{1,9},{2,6},{3,11},{4,12},{5,1},{6,14},{7,3},{8,0},{9,13},{1... | collective-permute-start | bytes 294920 | tf_op jit(solution)/shard_map/ppermute | solution.py:382
  19.8 1.2 %collective-permute-start.10 = (bf16[128,384]{1,0:T(8,128)(2,1)S(1)}, bf16[128,384]{1,0:T(8,128)(2,1)S(1)}, u32[]{:S(2)}, u32[]{:S(2)}) collective-permute-start(bf16[128,384]{1,0:T(8,128)(2,1)S(1)} %get-tuple-element.38), channel_id=1, source_target_pairs={{0,2},{1,3},{2,0},{3,1},{4,6},{5,7},{6,4},{7,5},{8,10},{9,11},{10,... | collective-permute-start | bytes 294920 | tf_op jit(solution)/shard_map/ppermute | solution.py:382
  21.1 2.3 %collective-permute-start.6 = (bf16[128,384]{1,0:T(8,128)(2,1)S(1)}, bf16[128,384]{1,0:T(8,128)(2,1)S(1)}, u32[]{:S(2)}, u32[]{:S(2)}) collective-permute-start(bf16[128,384]{1,0:T(8,128)(2,1)S(1)} %collective-permute-done.3.refs_1_), channel_id=1, source_target_pairs={{0,4},{1,9},{2,6},{3,11},{4,12},{5,1},{6,14},{7,3},{8,0},{9,13},{1... | collective-permute-start | bytes 294920 | tf_op jit(solution)/shard_map/ppermute | solution.py:382
  23.4 1.8 %collective-permute-start.7 = (bf16[128,384]{1,0:T(8,128)(2,1)S(1)}, bf16[128,384]{1,0:T(8,128)(2,1)S(1)}, u32[]{:S(2)}, u32[]{:S(2)}) collective-permute-start(bf16[128,384]{1,0:T(8,128)(2,1)S(1)} %collective-permute-done.3.refs_1_), channel_id=1, source_target_pairs={{0,2},{1,3},{2,0},{3,1},{4,6},{5,7},{6,4},{7,5},{8,10},{9,11},{10,... | collective-permute-start | bytes 294920 | tf_op jit(solution)/shard_map/ppermute | solution.py:382
  25.2 1.9 %collective-permute-start.9 = (bf16[128,384]{1,0:T(8,128)(2,1)S(1)}, bf16[128,384]{1,0:T(8,128)(2,1)S(1)}, u32[]{:S(2)}, u32[]{:S(2)}) collective-permute-start(bf16[128,384]{1,0:T(8,128)(2,1)S(1)} %collective-permute-done.4.refs_2_), channel_id=1, source_target_pairs={{0,2},{1,3},{2,0},{3,1},{4,6},{5,7},{6,4},{7,5},{8,10},{9,11},{10,... | collective-permute-start | bytes 294920 | tf_op jit(solution)/shard_map/ppermute | solution.py:382
  27.1 0.6 %collective-permute-start.15 = (bf16[128,384]{1,0:T(8,128)(2,1)S(1)}, bf16[128,384]{1,0:T(8,128)(2,1)S(1)}, u32[]{:S(2)}, u32[]{:S(2)}) collective-permute-start(bf16[128,384]{1,0:T(8,128)(2,1)S(1)} %collective-permute-done.10.refs_8_), channel_id=1, source_target_pairs={{0,8},{1,5},{2,10},{3,7},{4,0},{5,13},{6,2},{7,15},{8,12},{9,1},{1... | collective-permute-start | bytes 294920 | tf_op jit(solution)/shard_map/ppermute | solution.py:382
  27.8 1.0 %collective-permute-done.8.refs_6_ = bf16[128,384]{1,0:T(8,128)(2,1)S(1)} collective-permute-done((bf16[128,384]{1,0:T(8,128)(2,1)S(1)}, bf16[128,384]{1,0:T(8,128)(2,1)S(1)}, u32[]{:S(2)}, u32[]{:S(2)}) %collective-permute-start.8) | collective-permute-done | bytes 98336 | tf_op jit(solution)/shard_map/ppermute | solution.py:382
  29.4 0.8 %collective-permute-start.14 = (bf16[128,384]{1,0:T(8,128)(2,1)S(1)}, bf16[128,384]{1,0:T(8,128)(2,1)S(1)}, u32[]{:S(2)}, u32[]{:S(2)}) collective-permute-start(bf16[128,384]{1,0:T(8,128)(2,1)S(1)} %collective-permute-done.5.refs_7_), channel_id=1, source_target_pairs={{0,8},{1,5},{2,10},{3,7},{4,0},{5,13},{6,2},{7,15},{8,12},{9,1},{1... | collective-permute-start | bytes 294920 | tf_op jit(solution)/shard_map/ppermute | solution.py:382
  30.1 0.9 %collective-permute-start.12 = (bf16[128,384]{1,0:T(8,128)(2,1)S(1)}, bf16[128,384]{1,0:T(8,128)(2,1)S(1)}, u32[]{:S(2)}, u32[]{:S(2)}) collective-permute-start(bf16[128,384]{1,0:T(8,128)(2,1)S(1)} %collective-permute-done.8.refs_6_), channel_id=1, source_target_pairs={{0,2},{1,3},{2,0},{3,1},{4,6},{5,7},{6,4},{7,5},{8,10},{9,11},{10,... | collective-permute-start | bytes 294920 | tf_op jit(solution)/shard_map/ppermute | solution.py:382
  32.2 1.5 %shard_map.117 = (bf16[256,384]{1,0:T(8,128)(2,1)S(1)}, f32[256,128]{1,0:T(8,128)S(1)}, f32[256,128]{1,0:T(8,128)S(1)}, f32[256,384]{1,0:T(8,128)S(1)}, bf16[5,256,384]{2,1,0:T(8,128)(2,1)S(1)}) custom-call(bf16[384,384]{1,0:T(8,128)(2,1)S(1)} %get-tuple-element.30.score_ref, f32[384]{0:T(512)S(1)} %copy-done.6, ...), custom_call_target="tpu_custom_call" | custom-call | flops 503316480 | bytes 983040 | tf_op jit(solution)/shard_map/pallas_call | solution.py:538
  33.7 1.0 %collective-permute-done.15.refs_13_ = bf16[128,384]{1,0:T(8,128)(2,1)S(1)} collective-permute-done((bf16[128,384]{1,0:T(8,128)(2,1)S(1)}, bf16[128,384]{1,0:T(8,128)(2,1)S(1)}, u32[]{:S(2)}, u32[]{:S(2)}) %collective-permute-start.15) | collective-permute-done | bytes 98336 | tf_op jit(solution)/shard_map/ppermute | solution.py:382
  34.7 4.4 %collective-permute-done.14.refs_12_ = bf16[128,384]{1,0:T(8,128)(2,1)S(1)} collective-permute-done((bf16[128,384]{1,0:T(8,128)(2,1)S(1)}, bf16[128,384]{1,0:T(8,128)(2,1)S(1)}, u32[]{:S(2)}, u32[]{:S(2)}) %collective-permute-start.14) | collective-permute-done | bytes 98336 | tf_op jit(solution)/shard_map/ppermute | solution.py:382
  39.1 2.7 %shard_map.118 = (bf16[256,384]{1,0:T(8,128)(2,1)S(1)}, bf16[256,384]{1,0:T(8,128)(2,1)S(1)}) custom-call(bf16[256,384]{1,0:T(8,128)(2,1)S(1)} %get-tuple-element.46.own_query_ref, f32[256,128]{1,0:T(8,128)S(1)} %get-tuple-element.47.peak_ref, f32[256,128]{1,0:T(8,128)S(1)} %get-tuple-element.48.sums_ref, f32[256,384]{1,0:T(8,128)S(1)} %get-tuple-element.49.added_ref, ...), custom_call_target="tpu_custom_call" | custom-call | flops 603979776 | bytes 1572864 | tf_op jit(solution)/shard_map/pallas_call | solution.py:558
  41.8 1.0 %collective-permute-start.16 = (bf16[256,384]{1,0:T(8,128)(2,1)S(1)}, bf16[256,384]{1,0:T(8,128)(2,1)S(1)}, u32[]{:S(2)}, u32[]{:S(2)}) collective-permute-start(bf16[256,384]{1,0:T(8,128)(2,1)S(1)} %get-tuple-element.55), channel_id=1, source_target_pairs={{0,1},{1,0},{2,3},{3,2},{4,5},{5,4},{6,7},{7,6},{8,9},{9,8},{10,11... | collective-permute-start | bytes 589832 | tf_op jit(solution)/shard_map/ppermute | solution.py:587
  42.9 1.0 %shard_map.119.own_ref = bf16[4,192,128]{2,1,0:T(8,128)(2,1)S(1)} custom-call(bf16[256,384]{1,0:T(8,128)(2,1)S(1)} %get-tuple-element.56.rows_ref, bf16[3,3,192,384]{3,2,1,0:T(8,128)(2,1)S(1)} %bitcast.5), custom_call_target="tpu_custom_call" | custom-call | flops 339738624 | bytes 1327104 | tf_op jit(solution)/shard_map/pallas_call | solution.py:592
  43.9 1.7 %shard_map.120 = bf16[2,4,192,128]{3,2,1,0:T(8,128)(2,1)} custom-call(bf16[256,384]{1,0:T(8,128)(2,1)S(1)} %collective-permute-done.16.rows_ref, bf16[3,3,192,384]{3,2,1,0:T(8,128)(2,1)S(1)} %bitcast.6, bf16[4,192,128]{2,1,0:T(8,128)(2,1)S(1)} %shard_map.119.own_ref), custom_call_target="tpu_custom_call" | custom-call | flops 339738624 | bytes 1327104 | tf_op jit(solution)/shard_map/pallas_call | solution.py:600
  (32 shorter events, 2.1 us)
Async XLA Ops:
  0.6 11.7 %copy-start.5 = (f32[384]{0:T(512)S(1)}, f32[384]{0:T(512)}, u32[]{:S(2)}) copy-start(f32[384]{0:T(512)} %norm_gain_ref.1) | copy-start | bytes 4612
  1.6 9.2 %collective-permute-start = (bf16[4,64,384]{2,1,0:T(8,128)(2,1)S(1)}, bf16[4,64,384]{2,1,0:T(8,128)(2,1)S(1)}, u32[]{:S(2)}, u32[]{:S(2)}) collective-permute-start(bf16[4,64,384]{2,1,0:T(8,128)(2,1)S(1)} %shard_map.114), channel_id=1, source_target_pairs={{1,2},{3,4},{5,6},{7,8},{9,10},{11,12},{13,14},{2,1},{4,3},{6,5},{... | collective-permute-start | bytes 589832 | tf_op jit(solution)/shard_map/ppermute | solution.py:464
  6.2 25.4 %copy-start.1 = (bf16[384,384]{1,0:T(8,128)(2,1)S(1)}, bf16[384,384]{1,0:T(8,128)(2,1)}, u32[]{:S(2)}) copy-start(bf16[384,384]{1,0:T(8,128)(2,1)} %query_ref.1) | copy-start | bytes 884740
  6.2 25.4 %copy-start.2 = (bf16[384,384]{1,0:T(8,128)(2,1)S(1)}, bf16[384,384]{1,0:T(8,128)(2,1)}, u32[]{:S(2)}) copy-start(bf16[384,384]{1,0:T(8,128)(2,1)} %key_ref.1) | copy-start | bytes 884740
  6.2 25.4 %copy-start.3 = (bf16[384,384]{1,0:T(8,128)(2,1)S(1)}, bf16[384,384]{1,0:T(8,128)(2,1)}, u32[]{:S(2)}) copy-start(bf16[384,384]{1,0:T(8,128)(2,1)} %value_ref.1) | copy-start | bytes 884740
  6.2 25.4 %copy-start.4 = (bf16[384,384]{1,0:T(8,128)(2,1)S(1)}, bf16[384,384]{1,0:T(8,128)(2,1)}, u32[]{:S(2)}) copy-start(bf16[384,384]{1,0:T(8,128)(2,1)} %out_ref.1) | copy-start | bytes 884740
  6.2 25.9 %copy-start.6 = (f32[384]{0:T(512)S(1)}, f32[384]{0:T(512)}, u32[]{:S(2)}) copy-start(f32[384]{0:T(512)} %gain_ref.5) | copy-start | bytes 4612
  10.0 1.6 %collective-permute-start.1 = (bf16[3,128,384]{2,1,0:T(8,128)(2,1)S(1)}, bf16[3,128,384]{2,1,0:T(8,128)(2,1)S(1)}, u32[]{:S(2)}, u32[]{:S(2)}) collective-permute-start(bf16[3,128,384]{2,1,0:T(8,128)(2,1)S(1)} %get-tuple-element.33), channel_id=1, source_target_pairs={{0,1},{1,0},{2,3},{3,2},{4,5},{5,4},{6,7},{7,6},{8,9},{9,8},{10,11... | collective-permute-start | bytes 884744 | tf_op jit(solution)/shard_map/ppermute | solution.py:491
  10.9 1.4 %collective-permute-start.2 = (bf16[4,64,384]{2,1,0:T(8,128)(2,1)S(1)}, bf16[4,64,384]{2,1,0:T(8,128)(2,1)S(1)}, u32[]{:S(2)}, u32[]{:S(2)}) collective-permute-start(bf16[4,64,384]{2,1,0:T(8,128)(2,1)S(1)} %collective-permute-done.edge_ref), channel_id=1, source_target_pairs={{0,1},{1,0},{2,3},{3,2},{4,5},{5,4},{6,7},{7,6},{8,9},{9,8},{10,11... | collective-permute-start | bytes 589832 | tf_op jit(solution)/shard_map/ppermute | solution.py:493
  12.3 30.5 %copy-start = (bf16[3,3,384,192]{2,3,1,0:T(8,128)(2,1)S(1)}, bf16[3,3,384,192]{2,3,1,0:T(8,128)(2,1)}, u32[]{:S(2)}) copy-start(bf16[3,3,384,192]{2,3,1,0:T(8,128)(2,1)} %param.19) | copy-start | bytes 3981316
  15.2 5.9 %collective-permute-start.3 = (bf16[128,384]{1,0:T(8,128)(2,1)S(1)}, bf16[128,384]{1,0:T(8,128)(2,1)S(1)}, u32[]{:S(2)}, u32[]{:S(2)}) collective-permute-start(bf16[128,384]{1,0:T(8,128)(2,1)S(1)} %get-tuple-element.37), channel_id=1, source_target_pairs={{0,4},{1,9},{2,6},{3,11},{4,12},{5,1},{6,14},{7,3},{8,0},{9,13},{1... | collective-permute-start | bytes 294920 | tf_op jit(solution)/shard_map/ppermute | solution.py:382
  18.3 6.9 %collective-permute-start.4 = (bf16[128,384]{1,0:T(8,128)(2,1)S(1)}, bf16[128,384]{1,0:T(8,128)(2,1)S(1)}, u32[]{:S(2)}, u32[]{:S(2)}) collective-permute-start(bf16[128,384]{1,0:T(8,128)(2,1)S(1)} %get-tuple-element.38), channel_id=1, source_target_pairs={{0,4},{1,9},{2,6},{3,11},{4,12},{5,1},{6,14},{7,3},{8,0},{9,13},{1... | collective-permute-start | bytes 294920 | tf_op jit(solution)/shard_map/ppermute | solution.py:382
  19.6 5.6 %collective-permute-start.5 = (bf16[128,384]{1,0:T(8,128)(2,1)S(1)}, bf16[128,384]{1,0:T(8,128)(2,1)S(1)}, u32[]{:S(2)}, u32[]{:S(2)}) collective-permute-start(bf16[128,384]{1,0:T(8,128)(2,1)S(1)} %get-tuple-element.37), channel_id=1, source_target_pairs={{0,2},{1,3},{2,0},{3,1},{4,6},{5,7},{6,4},{7,5},{8,10},{9,11},{10,... | collective-permute-start | bytes 294920 | tf_op jit(solution)/shard_map/ppermute | solution.py:382
  19.8 7.3 %collective-permute-start.10 = (bf16[128,384]{1,0:T(8,128)(2,1)S(1)}, bf16[128,384]{1,0:T(8,128)(2,1)S(1)}, u32[]{:S(2)}, u32[]{:S(2)}) collective-permute-start(bf16[128,384]{1,0:T(8,128)(2,1)S(1)} %get-tuple-element.38), channel_id=1, source_target_pairs={{0,2},{1,3},{2,0},{3,1},{4,6},{5,7},{6,4},{7,5},{8,10},{9,11},{10,... | collective-permute-start | bytes 294920 | tf_op jit(solution)/shard_map/ppermute | solution.py:382
  21.1 6.1 %collective-permute-start.6 = (bf16[128,384]{1,0:T(8,128)(2,1)S(1)}, bf16[128,384]{1,0:T(8,128)(2,1)S(1)}, u32[]{:S(2)}, u32[]{:S(2)}) collective-permute-start(bf16[128,384]{1,0:T(8,128)(2,1)S(1)} %collective-permute-done.3.refs_1_), channel_id=1, source_target_pairs={{0,4},{1,9},{2,6},{3,11},{4,12},{5,1},{6,14},{7,3},{8,0},{9,13},{1... | collective-permute-start | bytes 294920 | tf_op jit(solution)/shard_map/ppermute | solution.py:382
  23.4 4.4 %collective-permute-start.7 = (bf16[128,384]{1,0:T(8,128)(2,1)S(1)}, bf16[128,384]{1,0:T(8,128)(2,1)S(1)}, u32[]{:S(2)}, u32[]{:S(2)}) collective-permute-start(bf16[128,384]{1,0:T(8,128)(2,1)S(1)} %collective-permute-done.3.refs_1_), channel_id=1, source_target_pairs={{0,2},{1,3},{2,0},{3,1},{4,6},{5,7},{6,4},{7,5},{8,10},{9,11},{10,... | collective-permute-start | bytes 294920 | tf_op jit(solution)/shard_map/ppermute | solution.py:382
  25.2 3.6 %collective-permute-start.8 = (bf16[128,384]{1,0:T(8,128)(2,1)S(1)}, bf16[128,384]{1,0:T(8,128)(2,1)S(1)}, u32[]{:S(2)}, u32[]{:S(2)}) collective-permute-start(bf16[128,384]{1,0:T(8,128)(2,1)S(1)} %collective-permute-done.4.refs_2_), channel_id=1, source_target_pairs={{0,4},{1,9},{2,6},{3,11},{4,12},{5,1},{6,14},{7,3},{8,0},{9,13},{1... | collective-permute-start | bytes 294920 | tf_op jit(solution)/shard_map/ppermute | solution.py:382
  25.2 4.2 %collective-permute-start.9 = (bf16[128,384]{1,0:T(8,128)(2,1)S(1)}, bf16[128,384]{1,0:T(8,128)(2,1)S(1)}, u32[]{:S(2)}, u32[]{:S(2)}) collective-permute-start(bf16[128,384]{1,0:T(8,128)(2,1)S(1)} %collective-permute-done.4.refs_2_), channel_id=1, source_target_pairs={{0,2},{1,3},{2,0},{3,1},{4,6},{5,7},{6,4},{7,5},{8,10},{9,11},{10,... | collective-permute-start | bytes 294920 | tf_op jit(solution)/shard_map/ppermute | solution.py:382
  27.1 12.0 %collective-permute-start.13 = (bf16[256,384]{1,0:T(8,128)(2,1)S(1)}, bf16[256,384]{1,0:T(8,128)(2,1)S(1)}, u32[]{:S(2)}, u32[]{:S(2)}) collective-permute-start(bf16[256,384]{1,0:T(8,128)(2,1)S(1)} %get-tuple-element.53.refs_0_), channel_id=1, source_target_pairs={{0,8},{1,5},{2,10},{3,7},{4,0},{5,13},{6,2},{7,15},{8,12},{9,1},{1... | collective-permute-start | bytes 589832 | tf_op jit(solution)/shard_map/ppermute | solution.py:382
  27.1 7.5 %collective-permute-start.15 = (bf16[128,384]{1,0:T(8,128)(2,1)S(1)}, bf16[128,384]{1,0:T(8,128)(2,1)S(1)}, u32[]{:S(2)}, u32[]{:S(2)}) collective-permute-start(bf16[128,384]{1,0:T(8,128)(2,1)S(1)} %collective-permute-done.10.refs_8_), channel_id=1, source_target_pairs={{0,8},{1,5},{2,10},{3,7},{4,0},{5,13},{6,2},{7,15},{8,12},{9,1},{1... | collective-permute-start | bytes 294920 | tf_op jit(solution)/shard_map/ppermute | solution.py:382
  29.4 9.7 %collective-permute-start.14 = (bf16[128,384]{1,0:T(8,128)(2,1)S(1)}, bf16[128,384]{1,0:T(8,128)(2,1)S(1)}, u32[]{:S(2)}, u32[]{:S(2)}) collective-permute-start(bf16[128,384]{1,0:T(8,128)(2,1)S(1)} %collective-permute-done.5.refs_7_), channel_id=1, source_target_pairs={{0,8},{1,5},{2,10},{3,7},{4,0},{5,13},{6,2},{7,15},{8,12},{9,1},{1... | collective-permute-start | bytes 294920 | tf_op jit(solution)/shard_map/ppermute | solution.py:382
  30.1 9.0 %collective-permute-start.12 = (bf16[128,384]{1,0:T(8,128)(2,1)S(1)}, bf16[128,384]{1,0:T(8,128)(2,1)S(1)}, u32[]{:S(2)}, u32[]{:S(2)}) collective-permute-start(bf16[128,384]{1,0:T(8,128)(2,1)S(1)} %collective-permute-done.8.refs_6_), channel_id=1, source_target_pairs={{0,2},{1,3},{2,0},{3,1},{4,6},{5,7},{6,4},{7,5},{8,10},{9,11},{10,... | collective-permute-start | bytes 294920 | tf_op jit(solution)/shard_map/ppermute | solution.py:382
  31.1 8.0 %collective-permute-start.11 = (bf16[128,384]{1,0:T(8,128)(2,1)S(1)}, bf16[128,384]{1,0:T(8,128)(2,1)S(1)}, u32[]{:S(2)}, u32[]{:S(2)}) collective-permute-start(bf16[128,384]{1,0:T(8,128)(2,1)S(1)} %collective-permute-done.6.refs_5_), channel_id=1, source_target_pairs={{0,2},{1,3},{2,0},{3,1},{4,6},{5,7},{6,4},{7,5},{8,10},{9,11},{10,... | collective-permute-start | bytes 294920 | tf_op jit(solution)/shard_map/ppermute | solution.py:382
  41.8 2.1 %collective-permute-start.16 = (bf16[256,384]{1,0:T(8,128)(2,1)S(1)}, bf16[256,384]{1,0:T(8,128)(2,1)S(1)}, u32[]{:S(2)}, u32[]{:S(2)}) collective-permute-start(bf16[256,384]{1,0:T(8,128)(2,1)S(1)} %get-tuple-element.55), channel_id=1, source_target_pairs={{0,1},{1,0},{2,3},{3,2},{4,5},{5,4},{6,7},{7,6},{8,9},{9,8},{10,11... | collective-permute-start | bytes 589832 | tf_op jit(solution)/shard_map/ppermute | solution.py:587
